TPU v7x, 32 devices: a whole 2x2x4 slice. The times are simulated.
32 devices in a mesh: grp: 2 (over x), gx: 16 (over z, y, core).
Axes of the slice: x: 2, y: 2, z: 4, core: 2. Of those that a mesh axis runs over, the one named last changes fastest.
Arguments:
- cell_offsets: float32 [3, 81920], P(None, ('grp', 'gx')), parts along dimension 1, may hold values from 0 to 1
- electronegativity: float32 [81920], P(('grp', 'gx')), parts along dimension 0, may hold values from -44 to 80
- hardness: float32 [81920], P(('grp', 'gx')), parts along dimension 0, may hold values from 5 to 12
- charge_widths: float32 [81920], P(('grp', 'gx')), parts along dimension 0, may hold values from 0.9 to 1.4
- cell_counts: int32 [1024], P(('grp', 'gx')), parts along dimension 0, may hold values from 72 to 88, as said below
- cell_atoms: int32 [1024, 128], P(('grp', 'gx')), parts along dimension 0, may hold values from -1 to 2559, as said below
Outputs:
- charges: float32 [81920], P(('grp', 'gx')), parts along dimension 0
There are 2 independent parts, one for each index of `grp`. A program takes and returns all parts, laid end to end along the dimension named above; each array names one. Nothing has to cross between parts.
Inputs may be any that keep to these rules, and one draw needn't show every extreme that they name: `cell_counts`: within each device's 32 cells the counts add up to 2560; on every device some cell holds 88 atoms and some cell 5 * 16 - 128 / 16. `cell_atoms`: row c lists the indices of cell c's atoms in its first cell_counts[c] slots and -1 in the others; each of a device's 2560 atoms appears exactly once in that device's rows.
All inputs are finite; a program needn't handle non-finite values.
Results may differ from a plain program's by a relative error of at most 0.0003.
Values sent between devices are 32-bit elements; how exact they have to be, the bound alone decides.
No kernel may reach another device: no remote copies, remote signals or barrier semaphores. Data moves between devices by JAX's collectives and lax.ppermute only.
A program may use at most 192 MiB of HBM per device.

v0:
```python
import functools
import math

import jax
import jax.numpy as jnp
from jax import lax
from jax.experimental import pallas as pl
from jax.experimental.pallas import tpu as pltpu
from jax.sharding import PartitionSpec as P

CX = 2
CY = 2
CZ = 8
EZ = CZ + 2
CELLS = CX * CY * CZ
QUADS = CX * CY
LANES = 128
BLOCKS = 11
GROUPS = ((0, 1, 2, 3), (4, 5, 6, 7), (8, 9, 10))

COULOMB = 14.399645
ROOT_PI = math.sqrt(math.pi)
SCREEN = 1.0 / (math.sqrt(2.0) * 3.0)
EWALD_SELF = math.sqrt(2.0 / math.pi) / 3.0
SIDE = 12.0 * SCREEN
CUT_SQUARED = (12.0 * SCREEN) ** 2
CLOSEST_SQUARED = (0.5 * SCREEN) ** 2
PAIR_SCALE = COULOMB * SCREEN

VMEM = pltpu.VMEM
SMEM = pltpu.SMEM


def params(mib):
    return pltpu.CompilerParams(vmem_limit_bytes=mib * 2**20)


def lane_index(shape):
    return lax.broadcasted_iota(jnp.int32, shape, len(shape) - 1)


def row_index(shape):
    return lax.broadcasted_iota(jnp.int32, shape, len(shape) - 2)


def edge_place(slot):
    return slot // 2, (CZ - 1) * (1 - slot % 2)


def inner_place(slot):
    return slot // (CZ - 2), 1 + slot % (CZ - 2)


EDGES = 2 * QUADS
INNER = CELLS - EDGES
PLACES = {EDGES: edge_place, INNER: inner_place}
LAYERS = {EDGES: (0, CZ - 1), INNER: range(1, CZ - 1)}


def gather_cells(counted, atoms, table, others, out):
    place = PLACES[out.shape[0]]
    row = row_index((8, LANES))
    lane = lane_index((1, LANES))

    def pick(source, pointers):
        share = 8 // len(pointers)
        pointer = spread(pointers[-1])
        for k in range(len(pointers) - 2, -1, -1):
            pointer = jnp.where(row < share * (k + 1), pointers[k], pointer)
        high = pointer >> 7
        low = pointer & 127
        picked = jnp.zeros((8, LANES), jnp.float32)
        for chunk in range(source.shape[0]):
            part = jnp.take_along_axis(source[chunk], low, axis=1)
            picked = jnp.where(high == chunk, part, picked)
        return picked

    def four_cells(step, _):
        slots = [4 * step + k for k in range(4)]
        places = [place(slot) for slot in slots]
        counts = [counted[pl.ds(q * CZ + z, 1), :] for q, z in places]
        occupied = [lane < count for count in counts]
        pointers = [
            jnp.where(live, atoms[pl.ds(q * CZ + z, 1), :], 0)
            for (q, z), live in zip(places, occupied)
        ]
        pairs = [pick(table, pointers[:2]), pick(table, pointers[2:])]
        both = pick(others, pointers)
        for k, (slot, live) in enumerate(zip(slots, occupied)):
            q = places[k][0]
            at = 4 * (k % 2)
            picked = pairs[k // 2][at : at + 4]
            width = jnp.where(live, picked[3:4], 1.0)
            hard = both[2 * k + 1 : 2 * k + 2]
            diag = jnp.where(live, hard + COULOMB * (1.0 / (width * ROOT_PI) - EWALD_SELF), 1.0)
            negative = jnp.where(live, both[2 * k : 2 * k + 1], 0.0)
            out[slot, 0:1, :] = (picked[0:1] + (q // CY).astype(jnp.float32)) * SIDE
            out[slot, 1:2, :] = (picked[1:2] + (q % CY).astype(jnp.float32)) * SIDE
            out[slot, 2:3, :] = picked[2:3] * SIDE
            out[slot, 3:4, :] = (2.0 * SCREEN * SCREEN) * width * width
            out[slot, 4:5, :] = -negative / diag
            out[slot, 5:6, :] = jnp.where(live, 1.0 / diag, 0.0)
            out[slot, 6:7, :] = diag
            out[slot, 7:8, :] = counts[k].astype(jnp.float32)
        return 0

    lax.fori_loop(0, out.shape[0] // 4, four_cells, 0, unroll=2)


def prepare_kernel(
    counts_hbm, offsets, negativity, hardness, widths, atoms_hbm, edge, counted, atoms, table, others,
    counts, raw_offsets, raw_negativity, raw_hardness, raw_widths, sems,
):
    copies = [
        pltpu.make_async_copy(source, target, sems.at[index])
        for index, (source, target) in enumerate(
            [
                (counts_hbm, counts),
                (offsets, raw_offsets),
                (negativity, raw_negativity),
                (hardness, raw_hardness),
                (widths, raw_widths),
                (atoms_hbm, atoms),
            ]
        )
    ]
    for copy in copies:
        copy.start()
    for copy in copies:
        copy.wait()
    for chunk in range(table.shape[0]):
        here = slice(chunk * LANES, (chunk + 1) * LANES)
        for first in (0, 4):
            table[chunk, first : first + 3, :] = raw_offsets[:, here]
            table[chunk, first + 3 : first + 4, :] = raw_widths[chunk : chunk + 1, :]
        for first in (0, 2, 4, 6):
            others[chunk, first : first + 1, :] = raw_negativity[chunk : chunk + 1, :]
            others[chunk, first + 1 : first + 2, :] = raw_hardness[chunk : chunk + 1, :]
    for cell in range(CELLS):
        counted[cell : cell + 1, :] = jnp.full((1, LANES), counts[cell])
    gather_cells(counted, atoms, table, others, edge)


def prepare_rest_kernel(counted, atoms, table, others, inner):
    gather_cells(counted, atoms, table, others, inner)


def prepare(counts, offsets, negativity, hardness, widths, atoms):
    chunks = offsets.shape[1] // LANES
    plane = (chunks, LANES)
    tables = jax.ShapeDtypeStruct((chunks, 8, LANES), jnp.float32)
    lists = jax.ShapeDtypeStruct(atoms.shape, jnp.int32)
    edge, *rest = pl.pallas_call(
        prepare_kernel,
        out_shape=(
            jax.ShapeDtypeStruct((EDGES, 8, LANES), jnp.float32),
            lists,
            lists,
            tables,
            tables,
        ),
        in_specs=[pl.BlockSpec(memory_space=pltpu.HBM)] * 6,
        out_specs=(pl.BlockSpec(memory_space=VMEM),) * 5,
        scratch_shapes=[
            SMEM(counts.shape, jnp.int32),
            VMEM(offsets.shape, jnp.float32),
            VMEM(plane, jnp.float32),
            VMEM(plane, jnp.float32),
            VMEM(plane, jnp.float32),
            pltpu.SemaphoreType.DMA((6,)),
        ],
        compiler_params=params(8),
    )(
        *[
            pltpu.with_memory_space_constraint(array, pltpu.HBM)
            for array in (
                counts,
                offsets,
                negativity.reshape(plane),
                hardness.reshape(plane),
                widths.reshape(plane),
                atoms,
            )
        ]
    )
    inner = pl.pallas_call(
        prepare_rest_kernel,
        out_shape=jax.ShapeDtypeStruct((INNER, 8, LANES), jnp.float32),
        in_specs=[pl.BlockSpec(memory_space=VMEM)] * 4,
        out_specs=pl.BlockSpec(memory_space=VMEM),
        compiler_params=params(8),
        cost_estimate=pl.CostEstimate(flops=2**20, bytes_accessed=2**22, transcendentals=0),
    )(*rest)
    return edge, inner


def pack_column(
    info, cells, source, packed, spills, target, at, shift, layers=range(CZ), info_source=None
):
    lane = lane_index((8, LANES))
    row = row_index((8, LANES))
    for z in layers:
        base = source * EZ + z
        known = base if info_source is None else info_source * EZ + z
        low, mid, top = [spread(info[known + k, 7:8, :]).astype(jnp.int32) for k in range(3)]
        end = low + mid - LANES
        tiles = [cells[base + k] for k in range(3)]
        if shift is not None:
            for k in range(3):
                offset = jnp.where(row == 2, (k - 1) * SIDE, 0.0)
                for axis in range(2):
                    offset = jnp.where(row == axis, shift[axis] * SIDE, offset)
                tiles[k] = tiles[k] + offset
        second = jnp.take_along_axis(tiles[1], (lane - low) & 127, axis=1)
        third = jnp.take_along_axis(tiles[2], (lane - end) & 127, axis=1)
        packed[target * CZ + z, 0] = jnp.where(lane < low, tiles[0], second)
        packed[target * CZ + z, 1] = jnp.where(lane < end, second, third)
        spill = jnp.where(lane < end + top - LANES, third, 0.0)
        spills[target * CZ + z] = pltpu.roll(spill, at, 1) if at else spill


def pack_core(info, cells, packed, spills, build):
    for q in range(QUADS):
        pack_column(info, cells, q, packed, spills, q, 8 * q, (0, 0) if build else None)


def pack_faces(infos, pieces, packed, spills, build):
    for side in range(2):
        sign = 2 * side - 1
        for y in range(CY):
            shift = (sign * CX, 0) if build else None
            at = 32 + 8 * y
            pack_column(infos[side], pieces[side], y, packed, spills, 2 * side + y, at, shift)
        for x in range(CX):
            shift = (0, sign * CY) if build else None
            source = 2 * x + 1 - side
            target = 4 + 2 * x + side
            at = 48 + 8 * x
            pack_column(infos[2], pieces[2], source, packed, spills, target, at, shift)


def pack_corners(info, cells, packed, spills, build, layers):
    for side_x in range(2):
        for side_y in range(2):
            shift = ((2 * side_x - 1) * CX, (2 * side_y - 1) * CY) if build else None
            source = 2 * side_x + 1 - side_y
            target = 2 * side_x + side_y
            pack_column(info, cells, source, packed, spills, target, 64, shift, layers)


def pack_upper_faces(infos, pieces, packed, spills):
    for y in range(CY):
        pack_column(infos[0], pieces[0], y, packed, spills, 2 + y, 32 + 8 * y, None)
    for x in range(CX):
        pack_column(infos[1], pieces[1], 2 * x, packed, spills, 5 + 2 * x, 48 + 8 * x, None)


def pack_upper_corners(info, cells, packed, spills):
    for side_y in range(2):
        source = 1 - side_y
        pack_column(info, cells, source, packed, spills, 2 + side_y, 64, None, info_source=2 + source)


def upper_columns(q):
    columns = face_columns(q)
    return [columns[2 * k : 2 * k + 2] for k in range(2) if (q >> (1 - k)) & 1], 4 * (q == 1)


def core_columns(q):
    return [q ^ k for k in range(4)]


def face_columns(q):
    x, y = q >> 1, q & 1
    return [2 * x, 2 * x + 1, 4 + y, 6 + y]


def overflow_of(spills, columns, z):
    return sum(spills[column * CZ + z] for column in columns)


def spread(row):
    return jnp.broadcast_to(row, (8, LANES))


def couple(x_i, y_i, z_i, w_i, x_j, y_j, z_j, w_j):
    delta_x = x_j - x_i
    delta_y = y_j - y_i
    delta_z = z_j - z_i
    squared = delta_x * delta_x + delta_y * delta_y + delta_z * delta_z
    held = jnp.maximum(squared, CLOSEST_SQUARED)
    inverse = lax.rsqrt(held)
    distance = held * inverse
    scaled = distance * lax.rsqrt(w_i + w_j)
    value = (lax.erf(scaled) - lax.erf(distance)) * inverse
    return jnp.where(squared < CUT_SQUARED, value, 0.0)


def to_rows(sums, block):
    here = lane_index((8, LANES)) - row_index((8, LANES)) == 8 * block
    return jnp.where(here, jnp.sum(sums, axis=1, keepdims=True), 0.0)


def add_rows(cell, sums, rows):
    for index in range(2):
        total = jnp.zeros((8, LANES), jnp.float32)
        for block in range(BLOCKS):
            total = total + to_rows(sums[cell, block, index], block)
        rows.append(jnp.sum(total, axis=0, keepdims=True))


def finish_cell(slot, place, target, info, sums, out):
    q, z = place(slot)
    rows = []
    add_rows(slot, sums, rows)
    own = info.at[q * EZ + z + 1]
    scale = PAIR_SCALE / own[6:7, :]
    live = lane_index((1, LANES)) < own[7:8, :].astype(jnp.int32)
    out[target, 0:1, :] = jnp.where(live, rows[0] * scale, 0.0)
    out[target, 1:2, :] = jnp.where(live, rows[1] * scale, 0.0)


def build_cell(cell, slot, lines, turned, kernels, before, sums, below):
    own = None
    if below is not None:
        own = lane_index((8, LANES)) - row_index((8, LANES)) - below
    for group in GROUPS:
        sums_s, sums_t = start_sums(cell, before, group)
        mine = [[turned[cell, block, k] for k in range(4)] for block in group]
        for index, line in enumerate(lines):
            beside = [line(k) for k in range(6)]
            for at, block in enumerate(group):
                value = couple(*mine[at], *beside[:4])
                if own is not None and index < 2:
                    value = jnp.where(own == 8 * block - LANES * index, 0.0, value)
                kernels[slot, block, index] = value
                sums_s[at] = sums_s[at] + value * beside[4]
                sums_t[at] = sums_t[at] + value * beside[5]
        for at, block in enumerate(group):
            sums[slot, block, 0] = sums_s[at]
            sums[slot, block, 1] = sums_t[at]


def start_sums(cell, before, blocks):
    if before is None:
        zeros = [jnp.zeros((8, LANES), jnp.float32) for _ in blocks]
        return zeros, list(zeros)
    sums_s = [before[cell, block, 0] for block in blocks]
    return sums_s, [before[cell, block, 1] for block in blocks]


def lines_of(packed, columns, z):
    def line(column, half):
        return lambda k: spread(packed[column * CZ + z, half, k : k + 1, :])

    return [line(column, half) for column in columns for half in range(2)]


def rest_line(rest, cell):
    return lambda k: spread(rest[cell, k : k + 1, :])


def parts_of(value):
    high = value.astype(jnp.bfloat16).astype(jnp.float32)
    rest = value - high
    middle = rest.astype(jnp.bfloat16).astype(jnp.float32)
    return high, middle, rest - middle


def turn_cells(core, turned):
    chosen = row_index((24, 4 * LANES)) & 7
    ones = jnp.where(chosen == lane_index((24, 4 * LANES)) >> 7, 1.0, 0.0).astype(jnp.bfloat16)
    for cell in range(CELLS):
        here = core[(cell // CZ) * EZ + cell % CZ + 1]
        left = jnp.concatenate(parts_of(here), axis=0).T[: 8 * BLOCKS + 8].astype(jnp.bfloat16)
        wide = lax.dot_general(
            left, ones, (((1,), (0,)), ((), ())), preferred_element_type=jnp.float32
        )
        for block in range(BLOCKS):
            for k in range(4):
                turned[cell, block, k] = wide[8 * block : 8 * block + 8, k * LANES : (k + 1) * LANES]


def core_spills(spills, spill):
    for z in range(CZ):
        spill[z] = overflow_of(spills, range(QUADS), z)


def face_spills(spills, before, spill):
    for cell in range(CELLS):
        q, z = cell // CZ, cell % CZ
        spill[cell] = before[z] + overflow_of(spills, face_columns(q), z)


def corner_loop(start, stop, work, finish, sums):
    def one_cell(slot, _):
        finish(jnp.maximum(slot - 1, start))
        work(slot)
        return 0

    sums[start] = jnp.zeros(sums.shape[1:], jnp.float32)
    lax.fori_loop(start, stop, one_cell, 0, unroll=4)
    finish(stop - 1)


def corner_spills(spills, before, rest, place):
    for slot in range(rest.shape[0]):
        q, z = place(slot)
        rest[slot] = before[q * CZ + z] + spills[q * CZ + z]


def core_kernel(core, kernels, sums, spill, turned, packed, spills):
    turn_cells(core, turned)
    pack_core(core, core, packed, spills, True)
    core_spills(spills, spill)

    def one_cell(cell, _):
        q, z = cell // CZ, cell % CZ
        below = spread(core[q * EZ + z, 7:8, :]).astype(jnp.int32)
        lines = lines_of(packed, core_columns(q), z)
        build_cell(cell, cell, lines, turned, kernels, None, sums, below)
        return 0

    lax.fori_loop(0, CELLS, one_cell, 0, unroll=2)


def face_kernel(
    x_low, x_high, beyond, turned, before, spill_before, kernels, sums, spill, packed, spills
):
    pieces = [x_low, x_high, beyond]
    pack_faces(pieces, pieces, packed, spills, True)
    face_spills(spills, spill_before, spill)

    def one_cell(cell, _):
        lines = lines_of(packed, face_columns(cell // CZ), cell % CZ)
        build_cell(cell, cell, lines, turned, kernels, before, sums, None)
        return 0

    lax.fori_loop(0, CELLS, one_cell, 0, unroll=2)


def corner_kernel(
    corners, turned, before, spill_before, core, kernels, out, packed, spills, rest, sums
):
    slots = kernels.shape[0]
    place = PLACES[slots]
    pack_corners(corners, corners, packed, spills, True, LAYERS[slots])
    corner_spills(spills, spill_before, rest, place)

    def work(slot):
        q, z = place(slot)
        lines = lines_of(packed, [q], z) + [rest_line(rest, slot)]
        build_cell(q * CZ + z, slot, lines, turned, kernels, before, sums, None)

    def finish(slot):
        finish_cell(slot, place, slot, core, sums, out)

    corner_loop(0, slots, work, finish, sums)


IN_VMEM = pl.BlockSpec(memory_space=VMEM)
IN_SMEM = pl.BlockSpec(memory_space=SMEM)
PAIR = jax.ShapeDtypeStruct((CELLS, 2, LANES), jnp.float32)
SPILL = jax.ShapeDtypeStruct((CELLS, 8, LANES), jnp.float32)
SUMS = jax.ShapeDtypeStruct((CELLS, BLOCKS, 2, 8, LANES), jnp.float32)
TURNED = jax.ShapeDtypeStruct((CELLS, BLOCKS, 4, 8, LANES), jnp.float32)
CORE_SPILL = jax.ShapeDtypeStruct((CZ, 8, LANES), jnp.float32)
CORE_TILES, FACE_TILES, CORNER_TILES = 8, 8, 3


def held(tiles, cells=CELLS):
    return VMEM((cells, BLOCKS, tiles, 8, LANES), jnp.float32)


def pairs(cells):
    return jax.ShapeDtypeStruct((cells, 2, LANES), jnp.float32)


def call(kernel, outs, scratch, tiles, *arrays):
    work = CELLS * BLOCKS * tiles * 8 * LANES
    return pl.pallas_call(
        kernel,
        out_shape=outs,
        in_specs=[IN_SMEM if array.ndim == 1 else IN_VMEM for array in arrays],
        out_specs=jax.tree.map(lambda _: IN_VMEM, outs),
        scratch_shapes=scratch,
        compiler_params=params(8),
        cost_estimate=pl.CostEstimate(
            flops=30 * work, bytes_accessed=8 * work, transcendentals=4 * work
        ),
    )(*arrays)


def packs(columns):
    return [
        VMEM((columns * CZ, 2, 8, LANES), jnp.float32),
        VMEM((columns * CZ, 8, LANES), jnp.float32),
    ]


def build_core(core):
    outs = (held(CORE_TILES), SUMS, CORE_SPILL, TURNED)
    return call(core_kernel, outs, packs(4), CORE_TILES, core)


def build_faces(pieces, turned, before, spill):
    outs = (held(FACE_TILES), SUMS, SPILL)
    return call(face_kernel, outs, packs(8), FACE_TILES, *pieces, turned, before, spill)


def corner_scratch(cells):
    rest = VMEM((cells, 8, LANES), jnp.float32)
    return packs(4) + [rest, VMEM((cells, BLOCKS, 2, 8, LANES), jnp.float32)]


def build_corners(cells, corners, turned, before, spill, core):
    outs = (held(CORNER_TILES, cells), pairs(cells))
    arrays = [corners, turned, before, spill, core]
    return call(corner_kernel, outs, corner_scratch(cells), CORNER_TILES, *arrays)


def cell_sums(cell, slot, lines, stored, before, first=0):
    sums_s, sums_t = start_sums(cell, before, range(BLOCKS))
    for index, line in enumerate(lines):
        line_s, line_t = line(0), line(1)
        for block in range(BLOCKS):
            value = stored[slot, block, first + index]
            sums_s[block] = sums_s[block] + value * line_s
            sums_t[block] = sums_t[block] + value * line_t
    return sums_s, sums_t


def apply_cell(cell, slot, lines, stored, before, sums, first=0):
    sums_s, sums_t = cell_sums(cell, slot, lines, stored, before, first)
    for block in range(BLOCKS):
        sums[slot, block, 0] = sums_s[block]
        sums[slot, block, 1] = sums_t[block]


def widen(pieces, wides, scale=None):
    for piece, wide in zip(pieces, wides):
        wide[:, 0:2, :] = piece[...] if scale is None else scale * piece[...]


def apply_core_kernel(info, core, stored, sums, spill, wide, packed, spills):
    widen([core], [wide])
    pack_core(info, wide, packed, spills, False)
    core_spills(spills, spill)

    def one_cell(cell, _):
        lines = lines_of(packed, core_columns(cell // CZ), cell % CZ)
        apply_cell(cell, cell, lines, stored, None, sums)
        return 0

    lax.fori_loop(0, CELLS, one_cell, 0, unroll=4)


def apply_face_kernel(*refs):
    infos, pieces, (stored, before, spill_before, sums, spill), wides, (packed, spills) = split(
        refs, 3, 3, 5, 3, 2
    )
    widen(pieces, wides)
    pack_faces(infos, wides, packed, spills, False)
    face_spills(spills, spill_before, spill)

    def one_cell(cell, _):
        lines = lines_of(packed, face_columns(cell // CZ), cell % CZ)
        apply_cell(cell, cell, lines, stored, before, sums)
        return 0

    lax.fori_loop(0, CELLS, one_cell, 0, unroll=4)


def apply_corner_cells(stored, before, spill_before, core, out, packed, spills, rest, sums):
    slots = stored.shape[0]
    place = PLACES[slots]
    corner_spills(spills, spill_before, rest, place)

    def work(slot):
        q, z = place(slot)
        lines = lines_of(packed, [q], z) + [rest_line(rest, slot)]
        apply_cell(q * CZ + z, slot, lines, stored, before, sums)

    def finish(slot):
        finish_cell(slot, place, slot, core, sums, out)

    corner_loop(0, slots, work, finish, sums)


def upper_corner_cells(stored, before, spill_before, turned, packed, spills, rest, total):
    slots = stored.shape[0]
    place = PLACES[slots]
    for slot in range(slots):
        q, z = place(slot)
        tile = spill_before[q * CZ + z]
        rest[slot] = tile + spills[q * CZ + z] if q >= CY else tile

    def weigh(cell, sums, total):
        total_s, total_t = total
        for block in range(BLOCKS):
            total_s = total_s + sums[0][block] * turned[cell, block, 0]
            total_t = total_t + sums[1][block] * turned[cell, block, 1]
        return total_s, total_t

    def low(slot, total):
        q, z = place(slot)
        cell = q * CZ + z
        return weigh(cell, cell_sums(cell, slot, [rest_line(rest, slot)], stored, before, 2), total)

    def high(slot, total):
        q, z = place(slot)
        cell = q * CZ + z
        lines = lines_of(packed, [q], z) + [rest_line(rest, slot)]
        return weigh(cell, cell_sums(cell, slot, lines, stored, before), total)

    total = lax.fori_loop(0, slots // 2, low, total, unroll=4)
    return lax.fori_loop(slots // 2, slots, high, total, unroll=4)


def upper_face_kernel(
    info_high, info_beyond, high, beyond, stored, before, spill_before, sums, spill,
    wide_high, wide_beyond, packed, spills,
):
    wides = [wide_high, wide_beyond]
    widen([high, beyond], wides, 2.0)
    pack_upper_faces([info_high, info_beyond], wides, packed, spills)
    for cell in range(CELLS):
        q, z = cell // CZ, cell % CZ
        groups, _ = upper_columns(q)
        spill[cell] = sum([spills[c * CZ + z] for group in groups for c in group], spill_before[z])
    sums[0:CZ] = before[0:CZ]
    for q in range(1, QUADS):
        groups, first = upper_columns(q)
        columns = [column for group in groups for column in group]

        def one_cell(z, _, q=q, columns=columns, first=first):
            cell = q * CZ + z
            apply_cell(cell, cell, lines_of(packed, columns, z), stored, before, sums, first)
            return 0

        lax.fori_loop(0, CZ, one_cell, 0, unroll=4)


def apply_corner_kernel(
    info, corners, stored, before, spill_before, core, out, wide, packed, spills, rest, sums
):
    widen([corners], [wide])
    pack_corners(info, wide, packed, spills, False, LAYERS[stored.shape[0]])
    apply_corner_cells(
        stored, before, spill_before, core, out, packed, spills, rest, sums
    )


def split(refs, *sizes):
    parts = []
    for size in sizes:
        parts.append(refs[:size])
        refs = refs[size:]
    return parts


def turn_pairs(core, turned):
    row = row_index((8, 2 * LANES))
    chosen = ((row & 1) == lane_index((8, 2 * LANES)) >> 7) & (row < 6)
    ones = jnp.where(chosen, 1.0, 0.0).astype(jnp.bfloat16)
    for cell in range(CELLS):
        pair = core[(cell // CZ) * EZ + cell % CZ + 1]
        parts = jnp.concatenate(parts_of(pair) + (jnp.zeros_like(pair),), axis=0)
        left = parts.T[: 8 * BLOCKS + 8].astype(jnp.bfloat16)
        wide = lax.dot_general(
            left, ones, (((1,), (0,)), ((), ())), preferred_element_type=jnp.float32
        )
        for block in range(BLOCKS):
            for k in range(2):
                turned[cell, block, k] = wide[8 * block : 8 * block + 8, k * LANES : (k + 1) * LANES]


def pair_place(index):
    return lane_index((2, LANES)) - row_index((2, LANES)) == 2 * index


def last_core_kernel(
    info, core, stored, slots, first, second, sums, spill, turned, line, wide, packed, spills
):
    turn_pairs(core, turned)
    apply_core_kernel(info, core, stored, sums, spill, wide, packed, spills)
    d = slots[:, 1 : 1 + CZ, 6:7, :].reshape(CELLS, 1, LANES)
    v_0 = slots[:, 1 : 1 + CZ, 4:6, :].reshape(CELLS, 2, LANES)
    v_1 = first[:, 1 : 1 + CZ].reshape(v_0.shape)
    v_2 = second[:, 1 : 1 + CZ].reshape(v_0.shape)
    d_0 = d * v_0
    d_2 = d * v_2
    parts = [d_0 * v_0, d_0 * v_1, d * v_1 * v_1, d_2 * v_1, d_2 * v_2, None, v_0, v_1, v_2]
    found = jnp.zeros((2, LANES), jnp.float32)
    for index, part in enumerate(parts):
        if part is not None:
            total = jnp.sum(jnp.sum(part, axis=0), axis=1, keepdims=True)
            found = jnp.where(pair_place(index), total, found)
    line[...] = found


def apply_last_kernel(
    info, corners, edge, inner, before, spill_before, turned, line, moments,
    wide, packed, spills, edge_rest, inner_rest,
):
    widen([corners], [wide], 2.0)
    pack_upper_corners(info, wide, packed, spills)
    total = (jnp.zeros((8, LANES), jnp.float32), jnp.zeros((8, LANES), jnp.float32))
    for stored, rest in ((edge, edge_rest), (inner, inner_rest)):
        total = upper_corner_cells(
            stored, before, spill_before, turned, packed, spills, rest, total
        )
    last = [jnp.sum(part, axis=0, keepdims=True) for part in total]
    last = PAIR_SCALE * jnp.sum(jnp.concatenate(last, axis=0), axis=1, keepdims=True)
    found = jnp.where(pair_place(5), last, line[...])
    moments[...] = jnp.sum(found, axis=0, keepdims=True)


def wide(piece):
    return VMEM((piece.shape[0], 8, LANES), jnp.float32)


def apply_core(info, core, stored):
    stored = pltpu.with_memory_space_constraint(stored, VMEM)
    scratch = [wide(core)] + packs(4)
    return call(apply_core_kernel, (SUMS, CORE_SPILL), scratch, 2, info, core, stored)


def apply_faces(infos, pieces, stored, before, spill):
    stored = pltpu.with_memory_space_constraint(stored, VMEM)
    scratch = [wide(piece) for piece in pieces] + packs(8)
    return call(
        apply_face_kernel, (SUMS, SPILL), scratch, 2, *infos, *pieces, stored, before, spill
    )


def apply_upper_faces(infos, pieces, stored, before, spill):
    stored = pltpu.with_memory_space_constraint(stored, VMEM)
    scratch = [wide(piece) for piece in pieces] + packs(8)
    return call(
        upper_face_kernel, (SUMS, SPILL), scratch, 2, *infos, *pieces, stored, before, spill
    )


def apply_corners(info, corners, stored, before, spill, core):
    stored = pltpu.with_memory_space_constraint(stored, VMEM)
    cells = stored.shape[0]
    arrays = [info, corners, stored, before, spill, core]
    scratch = [wide(corners)] + corner_scratch(cells)
    return call(apply_corner_kernel, pairs(cells), scratch, 2, *arrays)


def apply_last_core(info, core, stored, slots, first, second):
    stored = pltpu.with_memory_space_constraint(stored, VMEM)
    outs = (SUMS, CORE_SPILL, SUMS, jax.ShapeDtypeStruct((2, LANES), jnp.float32))
    scratch = [wide(core)] + packs(4)
    return call(last_core_kernel, outs, scratch, 2, info, core, stored, slots, first, second)


def apply_last(info, corners, edge, inner, before, spill, turned, line):
    edge = pltpu.with_memory_space_constraint(edge, VMEM)
    inner = pltpu.with_memory_space_constraint(inner, VMEM)
    arrays = [info, corners, edge, inner, before, spill, turned, line]
    scratch = [wide(corners)] + packs(4)
    scratch += [VMEM((cells, 8, LANES), jnp.float32) for cells in (EDGES, INNER)]
    out = jax.ShapeDtypeStruct((1, LANES), jnp.float32)
    return call(apply_last_kernel, out, scratch, 2, *arrays)


def solve(g):
    tiny = 1e-6
    h = [g[k] + g[k + 1] for k in range(5)]
    ratio_1 = h[1] / h[0]
    ratio_2 = h[2] / h[0]
    pivot_1 = h[2] - ratio_1 * h[1]
    mixed = h[3] - ratio_1 * h[2]
    rest_1 = g[1] - ratio_1 * g[0]
    live_1 = pivot_1 > tiny * h[2]
    safe_1 = jnp.where(live_1, pivot_1, 1.0)
    ratio_3 = jnp.where(live_1, mixed / safe_1, 0.0)
    pivot_2 = h[4] - ratio_2 * h[2] - ratio_3 * mixed
    rest_2 = g[2] - ratio_2 * g[0] - ratio_3 * rest_1
    live_2 = live_1 & (pivot_2 > tiny * h[4])
    c_2 = jnp.where(live_2, rest_2 / jnp.where(live_2, pivot_2, 1.0), 0.0)
    c_1 = jnp.where(live_1, (rest_1 - mixed * c_2) / safe_1, 0.0)
    c_0 = (g[0] - h[1] * c_1 - h[2] * c_2) / h[0]
    return c_0, c_1, c_2


def invert(counts, atoms, places):
    rows = places.shape[1]
    row_low = row_index((LANES, LANES))
    row_high = row_index((rows, LANES))
    lane = lane_index((rows, LANES))

    def one_cell(cell, total):
        live = lane_index((1, LANES)) < counts[cell]
        pointer = jnp.where(live, atoms[pl.ds(cell, 1), :], -1)
        here = (pointer >> 7) == row_high
        cells = jnp.where(here, cell, 0).astype(jnp.float32)
        slots = jnp.where(here, lane, 0).astype(jnp.float32)
        parts = jnp.concatenate([cells, slots], axis=0).astype(jnp.bfloat16)
        lows = jnp.where((pointer & 127) == row_low, 1.0, 0.0).astype(jnp.bfloat16)
        return total + lax.dot_general(
            parts, lows, (((1,), (1,)), ((), ())), preferred_element_type=jnp.float32
        )

    total = jnp.zeros((2 * rows, LANES), jnp.float32)
    total = lax.fori_loop(0, CELLS, one_cell, total, unroll=8).astype(jnp.int32)
    places[0] = total[:rows]
    places[1] = total[rows:]


def inverted(counts, atoms, atoms_local):
    rows = (atoms_local // LANES + 15) // 16 * 16
    return call(invert, jax.ShapeDtypeStruct((2, rows, LANES), jnp.int32), [], 2, counts, atoms)


def finish_kernel(moments, slots, first, second, places, out, charges):
    summed = moments[...]
    lane = lane_index((2, LANES))
    row = row_index((2, LANES))

    def pair(index):
        picked = jnp.where(lane - row == 2 * index, summed, 0.0)
        return jnp.broadcast_to(jnp.sum(picked, axis=1, keepdims=True), (2, LANES))

    rows = [pair(index) for index in range(9)]
    c_0, c_1, c_2 = solve(rows[:6])
    totals = c_0 * rows[6] + c_1 * rows[7] + c_2 * rows[8]
    balance = totals[0:1] / totals[1:2]
    sign = jnp.concatenate([jnp.ones((1, LANES), jnp.float32), -balance], axis=0)
    c_0, c_1, c_2 = c_0 * sign, c_1 * sign, c_2 * sign
    for cell in range(CELLS):
        q, z = cell // CZ, cell % CZ + 1
        mixed = c_0 * slots[q, z, 4:6, :] + c_1 * first[q, z] + c_2 * second[q, z]
        charges[cell : cell + 1, :] = jnp.sum(mixed, axis=0, keepdims=True)
    tiles = [jnp.zeros((8, LANES), jnp.float32) for _ in range(places.shape[1] // 8)]
    for cell in range(CELLS):
        line = spread(charges[cell : cell + 1, :])
        for at in range(len(tiles)):
            here = slice(8 * at, 8 * at + 8)
            moved = jnp.take_along_axis(line, places[1, here, :], axis=1)
            tiles[at] = jnp.where(places[0, here, :] == cell, moved, tiles[at])
    out[...] = jnp.concatenate(tiles, axis=0)[: out.shape[0]]


def finish(moments, slots, first, second, places, atoms_local):
    return pl.pallas_call(
        finish_kernel,
        out_shape=jax.ShapeDtypeStruct((atoms_local // LANES, LANES), jnp.float32),
        in_specs=[IN_VMEM] * 5,
        out_specs=IN_VMEM,
        scratch_shapes=[VMEM((CELLS, LANES), jnp.float32)],
        compiler_params=params(8),
    )(moments, slots, first, second, places)


def partner(block, axis, mask):
    count = lax.axis_size(axis)
    return lax.ppermute(block, axis, [(low, low ^ mask) for low in range(count)])


def shifted(block, along_x, across_y=0):
    count = lax.axis_size("gx")
    route = [(i, ((i + 4 * along_x) % count) ^ (2 * across_y)) for i in range(count)]
    return lax.ppermute(block, "gx", route)


def with_z_faces(edge, inner):
    other = partner(edge, "gx", 1)
    parts = [other[:, 0:1], edge[:, 1:2], inner, edge[:, 0:1], other[:, 1:2]]
    return jnp.concatenate(parts, axis=1)


def flat(columns):
    return columns.reshape((-1,) + columns.shape[-2:])


def x_faces(core):
    count = lax.axis_size("gx")
    rows = count // 4
    odd = (lax.axis_index("gx") // 4) % 2 == 1
    if rows % 2:
        return shifted(core[2:], 1), shifted(core[:2], -1)
    route = [(i, (i + (4 if (i // 4) % 2 else -4)) % count) for i in range(count)]
    second = lax.ppermute(jnp.where(odd, core[2:], core[:2]), "gx", route)
    first = lax.ppermute(jnp.where(odd, core[:2], core[2:]), "gx", [(i, i ^ 4) for i in range(count)])
    return first, second


def sorted_faces(first, second):
    odd = (lax.axis_index("gx") // 4) % 2 == 1
    if (lax.axis_size("gx") // 4) % 2:
        return first, second
    return jnp.where(odd, first, second), jnp.where(odd, second, first)


def exchange(edge, inner, on_core, on_faces, on_corners, faces_last=False):
    core = with_z_faces(edge, inner)
    first, second = x_faces(core)
    beyond = partner(core, "gx", 2)
    sums, spill, *more = on_core(flat(core))
    if faces_last:
        second, first, beyond, sums = lax.optimization_barrier((second, first, beyond, sums))
    else:
        second, first, sums = lax.optimization_barrier((second, first, sums))
    low, high = sorted_faces(first, second)
    corners = partner(jnp.concatenate([low, high], axis=0), "gx", 2)
    pieces = [flat(part) for part in (low, high, beyond)]
    sums, spill, *more = on_faces(pieces, sums, spill, *more)
    corners = flat(corners)
    return core, pieces, corners, on_corners(corners, sums, spill, core, *more)


def global_sum(values):
    count = lax.axis_size("gx")
    if count & (count - 1):
        return lax.psum(values, "gx")
    step = 1
    while step < count:
        if step >= 2 and 4 * step <= count:
            others = [partner(values, "gx", k * step) for k in (3, 2, 1)]
            values = (values + others[0]) + (others[1] + others[2])
            step *= 4
        else:
            values = values + partner(values, "gx", step)
            step *= 2
    return values


def local(cell_offsets, electronegativity, hardness, charge_widths, cell_counts, cell_atoms):
    edge, inner = prepare(
        cell_counts, cell_offsets, electronegativity, hardness, charge_widths, cell_atoms
    )
    stored = []

    def keep(tiles, *others):
        stored.append(tiles)
        return others

    def build_ends(corners, sums, spill, core, *own):
        (edge,) = keep(*build_corners(EDGES, corners, *own, sums, spill, flat(core)))
        (inner,) = keep(*build_corners(INNER, corners, *own, sums, spill, flat(core)))
        return by_column(edge), by_column(inner)

    def by_column(cells):
        return cells.reshape((QUADS, -1) + cells.shape[1:])

    slots, pieces, corners, ends = exchange(
        by_column(edge),
        by_column(inner),
        lambda core: keep(*build_core(core)),
        lambda faces, sums, spill, *own: keep(*build_faces(faces, *own, sums, spill)) + own,
        build_ends,
        faces_last=True,
    )
    info = flat(slots)

    def apply(edge, inner, on_corners):
        return exchange(
            edge,
            inner,
            lambda own: apply_core(info, own, stored[0]),
            lambda faces, sums, spill: apply_faces(pieces, faces, stored[1], sums, spill),
            on_corners,
        )

    def apply_ends(others, sums, spill, _):
        edge = apply_corners(corners, others, stored[2], sums, spill, info)
        inner = apply_corners(corners, others, stored[3], sums, spill, info)
        return by_column(edge), by_column(inner)

    first, _, _, ends = apply(*ends, apply_ends)
    second = with_z_faces(*ends)
    high = shifted(second[:2], -1)
    beyond = partner(second, "gx", 2)
    corner = shifted(second[:2], -1, 1)
    sums, spill, turned, line = apply_last_core(
        info, flat(second), stored[0], slots, first, second
    )
    high, beyond, sums = lax.optimization_barrier((high, beyond, sums))
    upper = [flat(high), flat(beyond)]
    sums, spill = apply_upper_faces(pieces[1:], upper, stored[1], sums, spill)
    corner, sums = lax.optimization_barrier((corner, sums))
    moments = apply_last(
        corners, flat(corner), stored[2], stored[3], sums, spill, turned, line
    )
    moments, cell_counts, cell_atoms = lax.optimization_barrier((moments, cell_counts, cell_atoms))
    atoms_local = cell_offsets.shape[1]
    places = inverted(cell_counts, cell_atoms, atoms_local)
    charges = finish(global_sum(moments), slots, first, second, places, atoms_local)
    return charges.reshape(-1)


def solution(mesh):
    placed = (
        P(None, ("grp", "gx")),
        P(("grp", "gx")),
        P(("grp", "gx")),
        P(("grp", "gx")),
        P(("grp", "gx")),
        P(("grp", "gx"), None),
    )
    return jax.shard_map(
        local, mesh=mesh, in_specs=placed, out_specs=P(("grp", "gx")), check_vma=False
    )
```

profile of v0, /device:TPU:0, one launch (start us, length us, event | category | flops | bytes accessed | tf_op | source)
XLA Modules:
  0.0 69.7 jit_solution(1986083861134282483)
XLA Ops:
  0.0 1.1 %shard_map.64 = (f32[8,8,128]{2,1,0:T(8,128)S(1)}, s32[32,128]{1,0:T(8,128)S(1)}, s32[32,128]{1,0:T(8,128)S(1)}, f32[20,8,128]{2,1,0:T(8,128)S(1)}, f32[20,8,128]{2,1,0:T(8,128)S(1)}) custom-call(s32[32]{0:T(128)} %counts, f32[3,2560]{1,0:T(4,128)} %offsets.1, f32[20,128]{1,0:T(8,128)} %bitcast.66, f32[20,128]{1,0:T(8,128)} %bitcast.67, f32[20,128]{1,0:T(8,128)} %bitcast.68, ...), custom_call_target="tpu_custom_call" | custom-call | tf_op jit(solution)/shard_map/pallas_call | solution.py:153
  1.1 0.5 collective-permute-start
  1.6 0.7 %shard_map.65 = f32[24,8,128]{2,1,0:T(8,128)S(1)} custom-call(s32[32,128]{1,0:T(8,128)S(1)} %get-tuple-element.47.counted, s32[32,128]{1,0:T(8,128)S(1)} %get-tuple-element.48.atoms, f32[20,8,128]{2,1,0:T(8,128)S(1)} %get-tuple-element.49.table, f32[20,8,128]{2,1,0:T(8,128)S(1)} %get-tuple-element.50.others), custom_call_target="tpu_custom_call" | custom-call | flops 1048576 | bytes 4194304 | tf_op jit(solution)/shard_map/pallas_call | solution.py:186
  2.4 0.1 collective-permute-done
  2.5 2.9 %collective-permute-start.3 = (f32[4,10,8,128]{3,2,1,0:T(8,128)S(1)}, f32[4,10,8,128]{3,2,1,0:T(8,128)S(1)}, u32[]{:S(2)}, u32[]{:S(2)}) collective-permute-start(f32[4,10,8,128]{3,2,1,0:T(8,128)S(1)} %constant_dynamic-update-slice_fusion.slots), channel_id=1, source_target_pairs={{0,2},{1,3},{2,0},{3,1},{4,6},{5,7},{6,4},{7,5},{8,10},{9,11},{10,... | collective-permute-start | bytes 491528 | tf_op jit(solution)/shard_map/ppermute | solution.py:861
  5.5 1.6 %collective-permute-start.2 = (f32[2,10,8,128]{3,2,1,0:T(8,128)S(1)}, f32[2,10,8,128]{3,2,1,0:T(8,128)S(1)}, u32[]{:S(2)}, u32[]{:S(2)}) collective-permute-start(f32[2,10,8,128]{3,2,1,0:T(8,128)S(1)} %get-tuple-element.89), channel_id=1, source_target_pairs={{0,4},{1,5},{2,6},{3,7},{4,0},{5,1},{6,2},{7,3},{8,12},{9,13},{10,... | collective-permute-start | bytes 245768 | tf_op jit(solution)/shard_map/ppermute | solution.py:888
  7.1 2.5 %collective-permute-start.1 = (f32[2,10,8,128]{3,2,1,0:T(8,128)S(1)}, f32[2,10,8,128]{3,2,1,0:T(8,128)S(1)}, u32[]{:S(2)}, u32[]{:S(2)}) collective-permute-start(f32[2,10,8,128]{3,2,1,0:T(8,128)S(1)} %get-tuple-element.90), channel_id=1, source_target_pairs={{0,12},{1,13},{2,14},{3,15},{4,8},{5,9},{6,10},{7,11},{8,4},{9,5},... | collective-permute-start | bytes 245768 | tf_op jit(solution)/shard_map/ppermute | solution.py:887
  9.6 10.5 %shard_map.66 = (f32[32,11,8,8,128]{4,3,2,1,0:T(8,128)S(1)}, f32[32,11,2,8,128]{4,3,2,1,0:T(8,128)S(1)}, f32[8,8,128]{2,1,0:T(8,128)S(1)}, f32[32,11,4,8,128]{4,3,2,1,0:T(8,128)S(1)}) custom-call(f32[40,8,128]{2,1,0:T(8,128)S(1)} %bitcast.24), custom_call_target="tpu_custom_call" | custom-call | flops 86507520 | bytes 23068672 | tf_op jit(solution)/shard_map/pallas_call | solution.py:481
  20.1 0.0 collective-permute-done.2
  20.1 0.0 collective-permute-done.1
  20.1 0.0 collective-permute-done.3
  20.1 0.6 collective-permute-start.4
  20.7 9.8 %shard_map.67 = (f32[32,11,8,8,128]{4,3,2,1,0:T(8,128)S(1)}, f32[32,11,2,8,128]{4,3,2,1,0:T(8,128)S(1)}, f32[32,8,128]{2,1,0:T(8,128)S(1)}) custom-call(f32[20,8,128]{2,1,0:T(8,128)S(1)} %bitcast.39, f32[20,8,128]{2,1,0:T(8,128)S(1)} %bitcast.36, f32[40,8,128]{2,1,0:T(8,128)S(1)} %bitcast.42, f32[32,11,4,8,128]{4,3,2,1,0:T(8,128)S(1)} %get-tuple-element.54.turned, ...), custom_call_target="tpu_custom_call" | custom-call | flops 86507520 | bytes 23068672 | tf_op jit(solution)/shard_map/pallas_call | solution.py:481
  30.5 0.0 collective-permute-done.4
  30.5 1.2 %shard_map.68 = (f32[8,11,3,8,128]{4,3,2,1,0:T(8,128)S(1)}, f32[8,2,128]{2,1,0:T(2,128)S(1)}) custom-call(f32[40,8,128]{2,1,0:T(8,128)S(1)} %bitcast.31, f32[32,11,4,8,128]{4,3,2,1,0:T(8,128)S(1)} %get-tuple-element.54.turned, f32[32,11,2,8,128]{4,3,2,1,0:T(8,128)S(1)} %get-tuple-element.58.before, f32[32,8,128]{2,1,0:T(8,128)S(1)} %get-tuple-element.59.spill_before, ...), custom_call_target="tpu_custom_call" | custom-call | flops 32440320 | bytes 8650752 | tf_op jit(solution)/shard_map/pallas_call | solution.py:481
  31.7 0.1 collective-permute-start.5
  31.8 3.2 %shard_map.69 = (f32[24,11,3,8,128]{4,3,2,1,0:T(8,128)S(1)}, f32[24,2,128]{2,1,0:T(2,128)S(1)}) custom-call(f32[40,8,128]{2,1,0:T(8,128)S(1)} %bitcast.32, f32[32,11,4,8,128]{4,3,2,1,0:T(8,128)S(1)} %get-tuple-element.54.turned, f32[32,11,2,8,128]{4,3,2,1,0:T(8,128)S(1)} %get-tuple-element.58.before, f32[32,8,128]{2,1,0:T(8,128)S(1)} %get-tuple-element.59.spill_before, ...), custom_call_target="tpu_custom_call" | custom-call | flops 32440320 | bytes 8650752 | tf_op jit(solution)/shard_map/pallas_call | solution.py:481
  35.0 0.0 collective-permute-done.5
  35.1 0.7 %collective-permute-start.7 = (f32[2,10,2,128]{3,2,1,0:T(2,128)S(1)}, f32[2,10,2,128]{3,2,1,0:T(2,128)S(1)}, u32[]{:S(2)}, u32[]{:S(2)}) collective-permute-start(f32[2,10,2,128]{3,2,1,0:T(2,128)S(1)} %get-tuple-element.93), channel_id=1, source_target_pairs={{0,4},{1,5},{2,6},{3,7},{4,0},{5,1},{6,2},{7,3},{8,12},{9,13},{10,... | collective-permute-start | bytes 61448 | tf_op jit(solution)/shard_map/ppermute | solution.py:888
  35.9 0.9 %collective-permute-start.6 = (f32[2,10,2,128]{3,2,1,0:T(2,128)S(1)}, f32[2,10,2,128]{3,2,1,0:T(2,128)S(1)}, u32[]{:S(2)}, u32[]{:S(2)}) collective-permute-start(f32[2,10,2,128]{3,2,1,0:T(2,128)S(1)} %get-tuple-element.94), channel_id=1, source_target_pairs={{0,12},{1,13},{2,14},{3,15},{4,8},{5,9},{6,10},{7,11},{8,4},{9,5},... | collective-permute-start | bytes 61448 | tf_op jit(solution)/shard_map/ppermute | solution.py:887
  36.8 1.5 %collective-permute-start.9 = (f32[4,10,2,128]{3,2,1,0:T(2,128)S(1)}, f32[4,10,2,128]{3,2,1,0:T(2,128)S(1)}, u32[]{:S(2)}, u32[]{:S(2)}) collective-permute-start(f32[4,10,2,128]{3,2,1,0:T(2,128)S(1)} %constant_dynamic-update-slice_fusion.5.first), channel_id=1, source_target_pairs={{0,2},{1,3},{2,0},{3,1},{4,6},{5,7},{6,4},{7,5},{8,10},{9,11},{10,... | collective-permute-start | bytes 122888 | tf_op jit(solution)/shard_map/ppermute | solution.py:861
  38.3 1.8 %shard_map.70 = (f32[32,11,2,8,128]{4,3,2,1,0:T(8,128)S(1)}, f32[8,8,128]{2,1,0:T(8,128)S(1)}) custom-call(f32[40,8,128]{2,1,0:T(8,128)S(1)} %bitcast.27, f32[40,2,128]{2,1,0:T(2,128)S(1)} %bitcast.41, f32[32,11,8,8,128]{4,3,2,1,0:T(8,128)S(1)} %get-tuple-element.62.stored), custom_call_target="tpu_custom_call" | custom-call | flops 21626880 | bytes 5767168 | tf_op jit(solution)/shard_map/pallas_call | solution.py:481
  40.1 0.0 collective-permute-done.7
  40.1 1.3 %collective-permute-done.6 = f32[2,10,2,128]{3,2,1,0:T(2,128)S(1)} collective-permute-done((f32[2,10,2,128]{3,2,1,0:T(2,128)S(1)}, f32[2,10,2,128]{3,2,1,0:T(2,128)S(1)}, u32[]{:S(2)}, u32[]{:S(2)}) %collective-permute-start.6) | collective-permute-done | bytes 20512 | tf_op jit(solution)/shard_map/ppermute | solution.py:887
  41.5 1.6 %collective-permute-start.8 = (f32[4,10,2,128]{3,2,1,0:T(2,128)S(1)}, f32[4,10,2,128]{3,2,1,0:T(2,128)S(1)}, u32[]{:S(2)}, u32[]{:S(2)}) collective-permute-start(f32[4,10,2,128]{3,2,1,0:T(2,128)S(1)} %pad_maximum_fusion.1), channel_id=1, source_target_pairs={{0,2},{1,3},{2,0},{3,1},{4,6},{5,7},{6,4},{7,5},{8,10},{9,11},{10,... | collective-permute-start | bytes 122888 | tf_op jit(solution)/shard_map/ppermute | solution.py:861
  43.1 0.0 collective-permute-done.9
  43.1 2.2 %shard_map.71 = (f32[32,11,2,8,128]{4,3,2,1,0:T(8,128)S(1)}, f32[32,8,128]{2,1,0:T(8,128)S(1)}) custom-call(f32[20,8,128]{2,1,0:T(8,128)S(1)} %bitcast.40, f32[20,8,128]{2,1,0:T(8,128)S(1)} %bitcast.37, f32[40,8,128]{2,1,0:T(8,128)S(1)} %bitcast.43, f32[20,2,128]{2,1,0:T(2,128)S(1)} %bitcast.47, f32[20,2,128]{2,1,0:T(2,128)S(1)} %bitcast.48, ...), custom_call_target="tpu_custom_call" | custom-call | flops 21626880 | bytes 5767168 | tf_op jit(solution)/shard_map/pallas_call | solution.py:481
  45.3 0.2 collective-permute-done.8
  45.6 0.7 shard_map.72
  46.3 0.1 collective-permute-start.10
  46.3 1.6 %shard_map.73 = f32[24,2,128]{2,1,0:T(2,128)S(1)} custom-call(f32[40,8,128]{2,1,0:T(8,128)S(1)} %bitcast.34, f32[40,2,128]{2,1,0:T(2,128)S(1)} %bitcast.52, f32[24,11,3,8,128]{4,3,2,1,0:T(8,128)S(1)} %get-tuple-element.72.stored.inner, f32[32,11,2,8,128]{4,3,2,1,0:T(8,128)S(1)} %get-tuple-element.70.before, ...), custom_call_target="tpu_custom_call" | custom-call | flops 21626880 | bytes 5767168 | tf_op jit(solution)/shard_map/pallas_call | solution.py:481
  48.0 0.0 collective-permute-done.10
  48.1 1.6 %collective-permute-start.13 = (f32[4,10,2,128]{3,2,1,0:T(2,128)S(1)}, f32[4,10,2,128]{3,2,1,0:T(2,128)S(1)}, u32[]{:S(2)}, u32[]{:S(2)}) collective-permute-start(f32[4,10,2,128]{3,2,1,0:T(2,128)S(1)} %constant_dynamic-update-slice_fusion.10.second), channel_id=1, source_target_pairs={{0,2},{1,3},{2,0},{3,1},{4,6},{5,7},{6,4},{7,5},{8,10},{9,11},{10,... | collective-permute-start | bytes 122888 | tf_op jit(solution)/shard_map/ppermute | solution.py:861
  49.6 0.9 %collective-permute-start.12 = (f32[2,10,2,128]{3,2,1,0:T(2,128)S(1)}, f32[2,10,2,128]{3,2,1,0:T(2,128)S(1)}, u32[]{:S(2)}, u32[]{:S(2)}) collective-permute-start(f32[2,10,2,128]{3,2,1,0:T(2,128)S(1)} %slice.89), channel_id=1, source_target_pairs={{0,12},{1,13},{2,14},{3,15},{4,0},{5,1},{6,2},{7,3},{8,4},{9,5},{1... | collective-permute-start | bytes 61448 | tf_op jit(solution)/shard_map/ppermute | solution.py:867
  50.5 1.1 %collective-permute-start.11 = (f32[2,10,2,128]{3,2,1,0:T(2,128)S(1)}, f32[2,10,2,128]{3,2,1,0:T(2,128)S(1)}, u32[]{:S(2)}, u32[]{:S(2)}) collective-permute-start(f32[2,10,2,128]{3,2,1,0:T(2,128)S(1)} %slice.89), channel_id=1, source_target_pairs={{0,14},{1,15},{2,12},{3,13},{4,2},{5,3},{6,0},{7,1},{8,6},{9,7},{1... | collective-permute-start | bytes 61448 | tf_op jit(solution)/shard_map/ppermute | solution.py:867
  51.7 2.4 %shard_map.74 = (f32[32,11,2,8,128]{4,3,2,1,0:T(8,128)S(1)}, f32[8,8,128]{2,1,0:T(8,128)S(1)}, f32[32,11,2,8,128]{4,3,2,1,0:T(8,128)S(1)}, f32[2,128]{1,0:T(2,128)S(1)}) custom-call(f32[40,8,128]{2,1,0:T(8,128)S(1)} %bitcast.30, f32[40,2,128]{2,1,0:T(2,128)S(1)} %bitcast.45, f32[32,11,8,8,128]{4,3,2,1,0:T(8,128)S(1)} %get-tuple-element.62.stored, ...), custom_call_target="tpu_custom_call" | custom-call | flops 21626880 | bytes 5767168 | tf_op jit(solution)/shard_map/pallas_call | solution.py:481
  54.1 0.0 collective-permute-done.12
  54.1 0.0 collective-permute-done.13
  54.1 1.1 %shard_map.75 = (f32[32,11,2,8,128]{4,3,2,1,0:T(8,128)S(1)}, f32[32,8,128]{2,1,0:T(8,128)S(1)}) custom-call(f32[20,8,128]{2,1,0:T(8,128)S(1)} %bitcast.38, f32[40,8,128]{2,1,0:T(8,128)S(1)} %bitcast.44, f32[20,2,128]{2,1,0:T(2,128)S(1)} %bitcast.59, f32[40,2,128]{2,1,0:T(2,128)S(1)} %bitcast.53, f32[32,11,8,8,128]{4,3,2,1,0:T(8,128)S(1)} %get-tuple-element.67.refs_6_.stored, ...), custom_call_target="tpu_custom_call" | custom-call | flops 21626880 | bytes 5767168 | tf_op jit(solution)/shard_map/pallas_call | solution.py:481
  55.2 0.0 collective-permute-done.11
  55.2 0.0 copy-start
  55.2 0.0 copy-start.1
  55.2 1.0 %shard_map.76 = f32[1,128]{1,0:T(1,128)S(1)} custom-call(f32[40,8,128]{2,1,0:T(8,128)S(1)} %bitcast.35, f32[20,2,128]{2,1,0:T(2,128)S(1)} %bitcast.58, f32[8,11,3,8,128]{4,3,2,1,0:T(8,128)S(1)} %get-tuple-element.66.stored.edge, f32[24,11,3,8,128]{4,3,2,1,0:T(8,128)S(1)} %get-tuple-element.72.stored.inner, ...), custom_call_target="tpu_custom_call" | custom-call | flops 21626880 | bytes 5767168 | tf_op jit(solution)/shard_map/pallas_call | solution.py:481
  56.3 0.0 collective-permute-start.14
  56.3 1.1 %collective-permute-done.14 = f32[1,128]{1,0:T(1,128)S(1)} collective-permute-done((f32[1,128]{1,0:T(1,128)S(1)}, f32[1,128]{1,0:T(1,128)S(1)}, u32[]{:S(2)}, u32[]{:S(2)}) %collective-permute-start.14) | collective-permute-done | bytes 544 | tf_op jit(solution)/shard_map/ppermute | solution.py:861
  57.4 1.2 %collective-permute-start.17 = (f32[1,128]{1,0:T(1,128)S(1)}, f32[1,128]{1,0:T(1,128)S(1)}, u32[]{:S(2)}, u32[]{:S(2)}) collective-permute-start(f32[1,128]{1,0:T(1,128)S(1)} %add.24), channel_id=1, source_target_pairs={{0,2},{1,3},{2,0},{3,1},{4,6},{5,7},{6,4},{7,5},{8,10},{9,11},{10,... | collective-permute-start | bytes 1544 | tf_op jit(solution)/shard_map/ppermute | solution.py:861
  58.6 1.2 %collective-permute-start.16 = (f32[1,128]{1,0:T(1,128)S(1)}, f32[1,128]{1,0:T(1,128)S(1)}, u32[]{:S(2)}, u32[]{:S(2)}) collective-permute-start(f32[1,128]{1,0:T(1,128)S(1)} %add.24), channel_id=1, source_target_pairs={{0,4},{1,5},{2,6},{3,7},{4,0},{5,1},{6,2},{7,3},{8,12},{9,13},{10,... | collective-permute-start | bytes 1544 | tf_op jit(solution)/shard_map/ppermute | solution.py:861
  59.8 1.1 %collective-permute-start.15 = (f32[1,128]{1,0:T(1,128)S(1)}, f32[1,128]{1,0:T(1,128)S(1)}, u32[]{:S(2)}, u32[]{:S(2)}) collective-permute-start(f32[1,128]{1,0:T(1,128)S(1)} %add.24), channel_id=1, source_target_pairs={{0,6},{1,7},{2,4},{3,5},{4,2},{5,3},{6,0},{7,1},{8,14},{9,15},{10,... | collective-permute-start | bytes 1544 | tf_op jit(solution)/shard_map/ppermute | solution.py:861
  60.9 0.1 collective-permute-done.17
  60.9 1.2 %collective-permute-done.16 = f32[1,128]{1,0:T(1,128)S(1)} collective-permute-done((f32[1,128]{1,0:T(1,128)S(1)}, f32[1,128]{1,0:T(1,128)S(1)}, u32[]{:S(2)}, u32[]{:S(2)}) %collective-permute-start.16) | collective-permute-done | bytes 544 | tf_op jit(solution)/shard_map/ppermute | solution.py:861
  62.1 2.1 %collective-permute-done.15 = f32[1,128]{1,0:T(1,128)S(1)} collective-permute-done((f32[1,128]{1,0:T(1,128)S(1)}, f32[1,128]{1,0:T(1,128)S(1)}, u32[]{:S(2)}, u32[]{:S(2)}) %collective-permute-start.15) | collective-permute-done | bytes 544 | tf_op jit(solution)/shard_map/ppermute | solution.py:861
  64.2 1.6 %collective-permute-start.18 = (f32[1,128]{1,0:T(1,128)S(1)}, f32[1,128]{1,0:T(1,128)S(1)}, u32[]{:S(2)}, u32[]{:S(2)}) collective-permute-start(f32[1,128]{1,0:T(1,128)S(1)} %add_add_fusion), channel_id=1, source_target_pairs={{0,8},{1,9},{2,10},{3,11},{4,12},{5,13},{6,14},{7,15},{8,0},{9,1},... | collective-permute-start | bytes 1544 | tf_op jit(solution)/shard_map/ppermute | solution.py:861
  65.8 0.0 copy-done
  65.8 0.0 copy-done.1
  65.8 1.7 %shard_map.77.places = s32[2,32,128]{2,1,0:T(8,128)S(1)} custom-call(s32[32]{0:T(128)S(1)} %copy-done.1, s32[32,128]{1,0:T(8,128)S(1)} %copy-done), custom_call_target="tpu_custom_call" | custom-call | flops 21626880 | bytes 5767168 | tf_op jit(solution)/shard_map/pallas_call | solution.py:481
  67.6 1.1 %collective-permute-done.18 = f32[1,128]{1,0:T(1,128)S(1)} collective-permute-done((f32[1,128]{1,0:T(1,128)S(1)}, f32[1,128]{1,0:T(1,128)S(1)}, u32[]{:S(2)}, u32[]{:S(2)}) %collective-permute-start.18) | collective-permute-done | bytes 544 | tf_op jit(solution)/shard_map/ppermute | solution.py:861
  68.6 1.1 %shard_map.78 = f32[20,128]{1,0:T(8,128)} custom-call(f32[1,128]{1,0:T(1,128)S(1)} %add.28.moments, f32[4,10,8,128]{3,2,1,0:T(8,128)S(1)} %constant_dynamic-update-slice_fusion.slots, f32[4,10,2,128]{3,2,1,0:T(2,128)S(1)} %constant_dynamic-update-slice_fusion.5.first, f32[4,10,2,128]{3,2,1,0:T(2,128)S(1)} %constant_dynamic-update-slice_fusion.10.second, ...), custom_call_target="tpu_custom_call" | custom-call | tf_op jit(solution)/shard_map/pallas_call | solution.py:849
  (25 shorter events, 0.2 us)
Async XLA Ops:
  1.1 1.4 %collective-permute-start = (f32[4,2,8,128]{3,2,1,0:T(8,128)S(1)}, f32[4,2,8,128]{3,2,1,0:T(8,128)S(1)}, u32[]{:S(2)}, u32[]{:S(2)}) collective-permute-start(f32[4,2,8,128]{3,2,1,0:T(8,128)S(1)} %bitcast.54), channel_id=1, source_target_pairs={{0,1},{1,0},{2,3},{3,2},{4,5},{5,4},{6,7},{7,6},{8,9},{9,8},{10,11... | collective-permute-start | bytes 98312 | tf_op jit(solution)/shard_map/ppermute | solution.py:861
  2.5 17.5 %collective-permute-start.3 = (f32[4,10,8,128]{3,2,1,0:T(8,128)S(1)}, f32[4,10,8,128]{3,2,1,0:T(8,128)S(1)}, u32[]{:S(2)}, u32[]{:S(2)}) collective-permute-start(f32[4,10,8,128]{3,2,1,0:T(8,128)S(1)} %constant_dynamic-update-slice_fusion.slots), channel_id=1, source_target_pairs={{0,2},{1,3},{2,0},{3,1},{4,6},{5,7},{6,4},{7,5},{8,10},{9,11},{10,... | collective-permute-start | bytes 491528 | tf_op jit(solution)/shard_map/ppermute | solution.py:861
  5.5 14.6 %collective-permute-start.2 = (f32[2,10,8,128]{3,2,1,0:T(8,128)S(1)}, f32[2,10,8,128]{3,2,1,0:T(8,128)S(1)}, u32[]{:S(2)}, u32[]{:S(2)}) collective-permute-start(f32[2,10,8,128]{3,2,1,0:T(8,128)S(1)} %get-tuple-element.89), channel_id=1, source_target_pairs={{0,4},{1,5},{2,6},{3,7},{4,0},{5,1},{6,2},{7,3},{8,12},{9,13},{10,... | collective-permute-start | bytes 245768 | tf_op jit(solution)/shard_map/ppermute | solution.py:888
  7.1 12.9 %collective-permute-start.1 = (f32[2,10,8,128]{3,2,1,0:T(8,128)S(1)}, f32[2,10,8,128]{3,2,1,0:T(8,128)S(1)}, u32[]{:S(2)}, u32[]{:S(2)}) collective-permute-start(f32[2,10,8,128]{3,2,1,0:T(8,128)S(1)} %get-tuple-element.90), channel_id=1, source_target_pairs={{0,12},{1,13},{2,14},{3,15},{4,8},{5,9},{6,10},{7,11},{8,4},{9,5},... | collective-permute-start | bytes 245768 | tf_op jit(solution)/shard_map/ppermute | solution.py:887
  20.1 10.4 %collective-permute-start.4 = (f32[4,10,8,128]{3,2,1,0:T(8,128)S(1)}, f32[4,10,8,128]{3,2,1,0:T(8,128)S(1)}, u32[]{:S(2)}, u32[]{:S(2)}) collective-permute-start(f32[4,10,8,128]{3,2,1,0:T(8,128)S(1)} %pad_maximum_fusion), channel_id=1, source_target_pairs={{0,2},{1,3},{2,0},{3,1},{4,6},{5,7},{6,4},{7,5},{8,10},{9,11},{10,... | collective-permute-start | bytes 491528 | tf_op jit(solution)/shard_map/ppermute | solution.py:861
  31.7 3.3 %collective-permute-start.5 = (f32[4,2,2,128]{3,2,1,0:T(2,128)S(1)}, f32[4,2,2,128]{3,2,1,0:T(2,128)S(1)}, u32[]{:S(2)}, u32[]{:S(2)}) collective-permute-start(f32[4,2,2,128]{3,2,1,0:T(2,128)S(1)} %bitcast.60), channel_id=1, source_target_pairs={{0,1},{1,0},{2,3},{3,2},{4,5},{5,4},{6,7},{7,6},{8,9},{9,8},{10,11... | collective-permute-start | bytes 24584 | tf_op jit(solution)/shard_map/ppermute | solution.py:861
  35.1 5.0 %collective-permute-start.7 = (f32[2,10,2,128]{3,2,1,0:T(2,128)S(1)}, f32[2,10,2,128]{3,2,1,0:T(2,128)S(1)}, u32[]{:S(2)}, u32[]{:S(2)}) collective-permute-start(f32[2,10,2,128]{3,2,1,0:T(2,128)S(1)} %get-tuple-element.93), channel_id=1, source_target_pairs={{0,4},{1,5},{2,6},{3,7},{4,0},{5,1},{6,2},{7,3},{8,12},{9,13},{10,... | collective-permute-start | bytes 61448 | tf_op jit(solution)/shard_map/ppermute | solution.py:888
  35.9 5.6 %collective-permute-start.6 = (f32[2,10,2,128]{3,2,1,0:T(2,128)S(1)}, f32[2,10,2,128]{3,2,1,0:T(2,128)S(1)}, u32[]{:S(2)}, u32[]{:S(2)}) collective-permute-start(f32[2,10,2,128]{3,2,1,0:T(2,128)S(1)} %get-tuple-element.94), channel_id=1, source_target_pairs={{0,12},{1,13},{2,14},{3,15},{4,8},{5,9},{6,10},{7,11},{8,4},{9,5},... | collective-permute-start | bytes 61448 | tf_op jit(solution)/shard_map/ppermute | solution.py:887
  36.8 6.3 %collective-permute-start.9 = (f32[4,10,2,128]{3,2,1,0:T(2,128)S(1)}, f32[4,10,2,128]{3,2,1,0:T(2,128)S(1)}, u32[]{:S(2)}, u32[]{:S(2)}) collective-permute-start(f32[4,10,2,128]{3,2,1,0:T(2,128)S(1)} %constant_dynamic-update-slice_fusion.5.first), channel_id=1, source_target_pairs={{0,2},{1,3},{2,0},{3,1},{4,6},{5,7},{6,4},{7,5},{8,10},{9,11},{10,... | collective-permute-start | bytes 122888 | tf_op jit(solution)/shard_map/ppermute | solution.py:861
  41.5 4.1 %collective-permute-start.8 = (f32[4,10,2,128]{3,2,1,0:T(2,128)S(1)}, f32[4,10,2,128]{3,2,1,0:T(2,128)S(1)}, u32[]{:S(2)}, u32[]{:S(2)}) collective-permute-start(f32[4,10,2,128]{3,2,1,0:T(2,128)S(1)} %pad_maximum_fusion.1), channel_id=1, source_target_pairs={{0,2},{1,3},{2,0},{3,1},{4,6},{5,7},{6,4},{7,5},{8,10},{9,11},{10,... | collective-permute-start | bytes 122888 | tf_op jit(solution)/shard_map/ppermute | solution.py:861
  46.3 1.7 %collective-permute-start.10 = (f32[4,2,2,128]{3,2,1,0:T(2,128)S(1)}, f32[4,2,2,128]{3,2,1,0:T(2,128)S(1)}, u32[]{:S(2)}, u32[]{:S(2)}) collective-permute-start(f32[4,2,2,128]{3,2,1,0:T(2,128)S(1)} %bitcast.63), channel_id=1, source_target_pairs={{0,1},{1,0},{2,3},{3,2},{4,5},{5,4},{6,7},{7,6},{8,9},{9,8},{10,11... | collective-permute-start | bytes 24584 | tf_op jit(solution)/shard_map/ppermute | solution.py:861
  48.1 6.0 %collective-permute-start.13 = (f32[4,10,2,128]{3,2,1,0:T(2,128)S(1)}, f32[4,10,2,128]{3,2,1,0:T(2,128)S(1)}, u32[]{:S(2)}, u32[]{:S(2)}) collective-permute-start(f32[4,10,2,128]{3,2,1,0:T(2,128)S(1)} %constant_dynamic-update-slice_fusion.10.second), channel_id=1, source_target_pairs={{0,2},{1,3},{2,0},{3,1},{4,6},{5,7},{6,4},{7,5},{8,10},{9,11},{10,... | collective-permute-start | bytes 122888 | tf_op jit(solution)/shard_map/ppermute | solution.py:861
  49.6 4.4 %collective-permute-start.12 = (f32[2,10,2,128]{3,2,1,0:T(2,128)S(1)}, f32[2,10,2,128]{3,2,1,0:T(2,128)S(1)}, u32[]{:S(2)}, u32[]{:S(2)}) collective-permute-start(f32[2,10,2,128]{3,2,1,0:T(2,128)S(1)} %slice.89), channel_id=1, source_target_pairs={{0,12},{1,13},{2,14},{3,15},{4,0},{5,1},{6,2},{7,3},{8,4},{9,5},{1... | collective-permute-start | bytes 61448 | tf_op jit(solution)/shard_map/ppermute | solution.py:867
  50.5 4.7 %collective-permute-start.11 = (f32[2,10,2,128]{3,2,1,0:T(2,128)S(1)}, f32[2,10,2,128]{3,2,1,0:T(2,128)S(1)}, u32[]{:S(2)}, u32[]{:S(2)}) collective-permute-start(f32[2,10,2,128]{3,2,1,0:T(2,128)S(1)} %slice.89), channel_id=1, source_target_pairs={{0,14},{1,15},{2,12},{3,13},{4,2},{5,3},{6,0},{7,1},{8,6},{9,7},{1... | collective-permute-start | bytes 61448 | tf_op jit(solution)/shard_map/ppermute | solution.py:867
  55.2 10.6 %copy-start = (s32[32,128]{1,0:T(8,128)S(1)}, s32[32,128]{1,0:T(8,128)}, u32[]{:S(2)}) copy-start(s32[32,128]{1,0:T(8,128)} %atoms) | copy-start | bytes 49156
  55.2 10.6 %copy-start.1 = (s32[32]{0:T(128)S(1)}, s32[32]{0:T(128)}, u32[]{:S(2)}) copy-start(s32[32]{0:T(128)} %counts) | copy-start | bytes 388
  56.3 1.1 %collective-permute-start.14 = (f32[1,128]{1,0:T(1,128)S(1)}, f32[1,128]{1,0:T(1,128)S(1)}, u32[]{:S(2)}, u32[]{:S(2)}) collective-permute-start(f32[1,128]{1,0:T(1,128)S(1)} %shard_map.76), channel_id=1, source_target_pairs={{0,1},{1,0},{2,3},{3,2},{4,5},{5,4},{6,7},{7,6},{8,9},{9,8},{10,11... | collective-permute-start | bytes 1544 | tf_op jit(solution)/shard_map/ppermute | solution.py:861
  57.4 3.5 %collective-permute-start.17 = (f32[1,128]{1,0:T(1,128)S(1)}, f32[1,128]{1,0:T(1,128)S(1)}, u32[]{:S(2)}, u32[]{:S(2)}) collective-permute-start(f32[1,128]{1,0:T(1,128)S(1)} %add.24), channel_id=1, source_target_pairs={{0,2},{1,3},{2,0},{3,1},{4,6},{5,7},{6,4},{7,5},{8,10},{9,11},{10,... | collective-permute-start | bytes 1544 | tf_op jit(solution)/shard_map/ppermute | solution.py:861
  58.6 3.5 %collective-permute-start.16 = (f32[1,128]{1,0:T(1,128)S(1)}, f32[1,128]{1,0:T(1,128)S(1)}, u32[]{:S(2)}, u32[]{:S(2)}) collective-permute-start(f32[1,128]{1,0:T(1,128)S(1)} %add.24), channel_id=1, source_target_pairs={{0,4},{1,5},{2,6},{3,7},{4,0},{5,1},{6,2},{7,3},{8,12},{9,13},{10,... | collective-permute-start | bytes 1544 | tf_op jit(solution)/shard_map/ppermute | solution.py:861
  59.8 4.4 %collective-permute-start.15 = (f32[1,128]{1,0:T(1,128)S(1)}, f32[1,128]{1,0:T(1,128)S(1)}, u32[]{:S(2)}, u32[]{:S(2)}) collective-permute-start(f32[1,128]{1,0:T(1,128)S(1)} %add.24), channel_id=1, source_target_pairs={{0,6},{1,7},{2,4},{3,5},{4,2},{5,3},{6,0},{7,1},{8,14},{9,15},{10,... | collective-permute-start | bytes 1544 | tf_op jit(solution)/shard_map/ppermute | solution.py:861
  64.2 4.4 %collective-permute-start.18 = (f32[1,128]{1,0:T(1,128)S(1)}, f32[1,128]{1,0:T(1,128)S(1)}, u32[]{:S(2)}, u32[]{:S(2)}) collective-permute-start(f32[1,128]{1,0:T(1,128)S(1)} %add_add_fusion), channel_id=1, source_target_pairs={{0,8},{1,9},{2,10},{3,11},{4,12},{5,13},{6,14},{7,15},{8,0},{9,1},... | collective-permute-start | bytes 1544 | tf_op jit(solution)/shard_map/ppermute | solution.py:861
where the time goes:
time: 70 us; the launch traced here: 69.7 us
  Pallas kernels  40.2 us (57%)
  starting transfers between devices  21.7 us (31%)
  waiting for transfers between devices  7.25 us (10%)
    pallas_call x12, Pallas kernels, call(): pl.pallas_call(kernel, out_shape=outs, in_specs=[IN_SMEM if array.ndim ==...  37.3 us
    ppermute x13, starting transfers between devices, partner(): lax.ppermute(block, axis, [(low, low ^ mask) for low in range(count)])  14 us
    ppermute x13, waiting for transfers between devices, partner(): lax.ppermute(block, axis, [(low, low ^ mask) for low in range(count)])  5.9 us
    ppermute x2, starting transfers between devices, x_faces(): second = lax.ppermute(jnp.where(odd, core[2:], core[:2]), 'gx', route)  3.38 us
    ppermute x2, starting transfers between devices, x_faces(): lax.ppermute(jnp.where(odd, core[:2], core[2:]), 'gx', [(i, i ^ 4) for i...  2.39 us
    ppermute x2, starting transfers between devices, shifted(): return lax.ppermute(block, 'gx', route)  2.01 us
  transfers between devices with their start and end apart: 19, of which 8 were waited for; matrix products, arithmetic and copies ran while one was open for 0% of the time, Pallas kernels for 50%

commit v1 on v0

--- a/solution.py
+++ b/solution.py
@@ -877,15 +877,16 @@
     return columns.reshape((-1,) + columns.shape[-2:])
 
 
-def x_faces(core):
+def x_faces(core, across_y=0):
     count = lax.axis_size("gx")
-    rows = count // 4
+    flip = 2 * across_y
     odd = (lax.axis_index("gx") // 4) % 2 == 1
-    if rows % 2:
-        return shifted(core[2:], 1), shifted(core[:2], -1)
-    route = [(i, (i + (4 if (i // 4) % 2 else -4)) % count) for i in range(count)]
+    if (count // 4) % 2:
+        return shifted(core[2:], 1, across_y), shifted(core[:2], -1, across_y)
+    route = [(i, ((i + (4 if (i // 4) % 2 else -4)) % count) ^ flip) for i in range(count)]
     second = lax.ppermute(jnp.where(odd, core[2:], core[:2]), "gx", route)
-    first = lax.ppermute(jnp.where(odd, core[:2], core[2:]), "gx", [(i, i ^ 4) for i in range(count)])
+    route = [(i, i ^ 4 ^ flip) for i in range(count)]
+    first = lax.ppermute(jnp.where(odd, core[:2], core[2:]), "gx", route)
     return first, second
 
 
@@ -896,19 +897,24 @@
     return jnp.where(odd, first, second), jnp.where(odd, second, first)
 
 
-def exchange(edge, inner, on_core, on_faces, on_corners, faces_last=False):
+def exchange(edge, inner, on_core, on_faces, on_corners, forward=False):
     core = with_z_faces(edge, inner)
     first, second = x_faces(core)
     beyond = partner(core, "gx", 2)
+    diagonal = None if forward else x_faces(core, 1)
     sums, spill, *more = on_core(flat(core))
-    if faces_last:
+    if forward:
         second, first, beyond, sums = lax.optimization_barrier((second, first, beyond, sums))
     else:
         second, first, sums = lax.optimization_barrier((second, first, sums))
     low, high = sorted_faces(first, second)
-    corners = partner(jnp.concatenate([low, high], axis=0), "gx", 2)
+    if forward:
+        corners = partner(jnp.concatenate([low, high], axis=0), "gx", 2)
     pieces = [flat(part) for part in (low, high, beyond)]
     sums, spill, *more = on_faces(pieces, sums, spill, *more)
+    if not forward:
+        first, second, sums = lax.optimization_barrier((*diagonal, sums))
+        corners = jnp.concatenate(sorted_faces(first, second), axis=0)
     corners = flat(corners)
     return core, pieces, corners, on_corners(corners, sums, spill, core, *more)
 
@@ -953,7 +959,7 @@
         lambda core: keep(*build_core(core)),
         lambda faces, sums, spill, *own: keep(*build_faces(faces, *own, sums, spill)) + own,
         build_ends,
-        faces_last=True,
+        forward=True,
     )
     info = flat(slots)
 

time: 70 us -> 72.2 us (1.031)
  starting transfers between devices: 21.7 us -> 24.7 us
  waiting for transfers between devices: 7.25 us -> 6.48 us
    ppermute x2 -> x3, starting transfers between devices: 3.38 us -> 7.32 us  [x_faces(): second = lax.ppermute(jnp.where(odd, core[2:], core[:2]), 'gx', route)]
    ppermute x13 -> x12, starting transfers between devices: 14 us -> 12.3 us  [partner(): lax.ppermute(block, axis, [(low, low ^ mask) for low in range(count)])]
    ppermute x2 -> x3, waiting for transfers between devices: 1.33 us -> 0.01 us  [x_faces(): second = lax.ppermute(jnp.where(odd, core[2:], core[:2]), 'gx', route)]
    ppermute x13 -> x12, waiting for transfers between devices: 5.9 us -> 6.4 us  [partner(): lax.ppermute(block, axis, [(low, low ^ mask) for low in range(count)])]
    ppermute x2 -> x3, starting transfers between devices: 2.39 us -> 2.71 us  [x_faces(): first = lax.ppermute(jnp.where(odd, core[:2], core[2:]), 'gx', route)]
  transfers between devices with their start and end apart: 19 -> 20, of which waited for: 8 -> 8; matrix products, arithmetic and copies ran while one was open for 0% -> 0% of each run, Pallas kernels for 50% -> 49%
where the time goes in v1:
time: 72.2 us; the launch traced here: 72 us
  Pallas kernels  40.2 us (56%)
  starting transfers between devices  24.7 us (34%)
  waiting for transfers between devices  6.48 us (9%)
    pallas_call x12, Pallas kernels, call(): pl.pallas_call(kernel, out_shape=outs, in_specs=[IN_SMEM if array.ndim ==...  37.3 us
    ppermute x12, starting transfers between devices, partner(): lax.ppermute(block, axis, [(low, low ^ mask) for low in range(count)])  12.3 us
    ppermute x3, starting transfers between devices, x_faces(): second = lax.ppermute(jnp.where(odd, core[2:], core[:2]), 'gx', route)  7.32 us
    ppermute x12, waiting for transfers between devices, partner(): lax.ppermute(block, axis, [(low, low ^ mask) for low in range(count)])  6.4 us
    ppermute x3, starting transfers between devices, x_faces(): first = lax.ppermute(jnp.where(odd, core[:2], core[2:]), 'gx', route)  2.71 us
    ppermute x2, starting transfers between devices, shifted(): return lax.ppermute(block, 'gx', route)  2.41 us
  transfers between devices with their start and end apart: 20, of which 8 were waited for; matrix products, arithmetic and copies ran while one was open for 0% of the time, Pallas kernels for 49%

profile of v1, /device:TPU:0, one launch (start us, length us, event | category | flops | bytes accessed | tf_op | source)
XLA Modules:
  0.0 72.0 jit_solution(7031003349208214496)
XLA Ops:
  0.0 1.1 %shard_map.64 = (f32[8,8,128]{2,1,0:T(8,128)S(1)}, s32[32,128]{1,0:T(8,128)S(1)}, s32[32,128]{1,0:T(8,128)S(1)}, f32[20,8,128]{2,1,0:T(8,128)S(1)}, f32[20,8,128]{2,1,0:T(8,128)S(1)}) custom-call(s32[32]{0:T(128)} %counts, f32[3,2560]{1,0:T(4,128)} %offsets.1, f32[20,128]{1,0:T(8,128)} %bitcast.66, f32[20,128]{1,0:T(8,128)} %bitcast.67, f32[20,128]{1,0:T(8,128)} %bitcast.68, ...), custom_call_target="tpu_custom_call" | custom-call | tf_op jit(solution)/shard_map/pallas_call | solution.py:153
  1.1 0.5 collective-permute-start
  1.6 0.7 shard_map.65
  2.4 0.1 collective-permute-done
  2.5 2.9 %collective-permute-start.3 = (f32[4,10,8,128]{3,2,1,0:T(8,128)S(1)}, f32[4,10,8,128]{3,2,1,0:T(8,128)S(1)}, u32[]{:S(2)}, u32[]{:S(2)}) collective-permute-start(f32[4,10,8,128]{3,2,1,0:T(8,128)S(1)} %constant_dynamic-update-slice_fusion.slots), channel_id=1, source_target_pairs={{0,2},{1,3},{2,0},{3,1},{4,6},{5,7},{6,4},{7,5},{8,10},{9,11},{10,... | collective-permute-start | bytes 491528 | tf_op jit(solution)/shard_map/ppermute | solution.py:861
  5.5 1.6 %collective-permute-start.2 = (f32[2,10,8,128]{3,2,1,0:T(8,128)S(1)}, f32[2,10,8,128]{3,2,1,0:T(8,128)S(1)}, u32[]{:S(2)}, u32[]{:S(2)}) collective-permute-start(f32[2,10,8,128]{3,2,1,0:T(8,128)S(1)} %get-tuple-element.95), channel_id=1, source_target_pairs={{0,4},{1,5},{2,6},{3,7},{4,0},{5,1},{6,2},{7,3},{8,12},{9,13},{10,... | collective-permute-start | bytes 245768 | tf_op jit(solution)/shard_map/ppermute | solution.py:889
  7.1 2.5 %collective-permute-start.1 = (f32[2,10,8,128]{3,2,1,0:T(8,128)S(1)}, f32[2,10,8,128]{3,2,1,0:T(8,128)S(1)}, u32[]{:S(2)}, u32[]{:S(2)}) collective-permute-start(f32[2,10,8,128]{3,2,1,0:T(8,128)S(1)} %get-tuple-element.96), channel_id=1, source_target_pairs={{0,12},{1,13},{2,14},{3,15},{4,8},{5,9},{6,10},{7,11},{8,4},{9,5},... | collective-permute-start | bytes 245768 | tf_op jit(solution)/shard_map/ppermute | solution.py:887
  9.6 10.5 %shard_map.66 = (f32[32,11,8,8,128]{4,3,2,1,0:T(8,128)S(1)}, f32[32,11,2,8,128]{4,3,2,1,0:T(8,128)S(1)}, f32[8,8,128]{2,1,0:T(8,128)S(1)}, f32[32,11,4,8,128]{4,3,2,1,0:T(8,128)S(1)}) custom-call(f32[40,8,128]{2,1,0:T(8,128)S(1)} %bitcast.24), custom_call_target="tpu_custom_call" | custom-call | flops 86507520 | bytes 23068672 | tf_op jit(solution)/shard_map/pallas_call | solution.py:481
  20.1 0.0 collective-permute-done.2
  20.1 0.0 collective-permute-done.1
  20.1 0.0 collective-permute-done.3
  20.1 0.6 collective-permute-start.4
  20.7 9.8 %shard_map.67 = (f32[32,11,8,8,128]{4,3,2,1,0:T(8,128)S(1)}, f32[32,11,2,8,128]{4,3,2,1,0:T(8,128)S(1)}, f32[32,8,128]{2,1,0:T(8,128)S(1)}) custom-call(f32[20,8,128]{2,1,0:T(8,128)S(1)} %bitcast.39, f32[20,8,128]{2,1,0:T(8,128)S(1)} %bitcast.36, f32[40,8,128]{2,1,0:T(8,128)S(1)} %bitcast.42, f32[32,11,4,8,128]{4,3,2,1,0:T(8,128)S(1)} %get-tuple-element.57.turned, ...), custom_call_target="tpu_custom_call" | custom-call | flops 86507520 | bytes 23068672 | tf_op jit(solution)/shard_map/pallas_call | solution.py:481
  30.5 0.0 collective-permute-done.4
  30.5 1.2 %shard_map.68 = (f32[8,11,3,8,128]{4,3,2,1,0:T(8,128)S(1)}, f32[8,2,128]{2,1,0:T(2,128)S(1)}) custom-call(f32[40,8,128]{2,1,0:T(8,128)S(1)} %bitcast.31, f32[32,11,4,8,128]{4,3,2,1,0:T(8,128)S(1)} %get-tuple-element.57.turned, f32[32,11,2,8,128]{4,3,2,1,0:T(8,128)S(1)} %get-tuple-element.61.before, f32[32,8,128]{2,1,0:T(8,128)S(1)} %get-tuple-element.62.spill_before, ...), custom_call_target="tpu_custom_call" | custom-call | flops 32440320 | bytes 8650752 | tf_op jit(solution)/shard_map/pallas_call | solution.py:481
  31.7 0.1 collective-permute-start.5
  31.8 3.2 %shard_map.69 = (f32[24,11,3,8,128]{4,3,2,1,0:T(8,128)S(1)}, f32[24,2,128]{2,1,0:T(2,128)S(1)}) custom-call(f32[40,8,128]{2,1,0:T(8,128)S(1)} %bitcast.32, f32[32,11,4,8,128]{4,3,2,1,0:T(8,128)S(1)} %get-tuple-element.57.turned, f32[32,11,2,8,128]{4,3,2,1,0:T(8,128)S(1)} %get-tuple-element.61.before, f32[32,8,128]{2,1,0:T(8,128)S(1)} %get-tuple-element.62.spill_before, ...), custom_call_target="tpu_custom_call" | custom-call | flops 32440320 | bytes 8650752 | tf_op jit(solution)/shard_map/pallas_call | solution.py:481
  35.0 0.0 collective-permute-done.5
  35.1 1.4 %collective-permute-start.8 = (f32[2,10,2,128]{3,2,1,0:T(2,128)S(1)}, f32[2,10,2,128]{3,2,1,0:T(2,128)S(1)}, u32[]{:S(2)}, u32[]{:S(2)}) collective-permute-start(f32[2,10,2,128]{3,2,1,0:T(2,128)S(1)} %get-tuple-element.101), channel_id=1, source_target_pairs={{0,12},{1,13},{2,14},{3,15},{4,8},{5,9},{6,10},{7,11},{8,4},{9,5},... | collective-permute-start | bytes 61448 | tf_op jit(solution)/shard_map/ppermute | solution.py:887
  36.5 0.0 collective-permute-start.9
  36.5 3.4 %collective-permute-start.7 = (f32[2,10,2,128]{3,2,1,0:T(2,128)S(1)}, f32[2,10,2,128]{3,2,1,0:T(2,128)S(1)}, u32[]{:S(2)}, u32[]{:S(2)}) collective-permute-start(f32[2,10,2,128]{3,2,1,0:T(2,128)S(1)} %get-tuple-element.101), channel_id=1, source_target_pairs={{0,14},{1,15},{2,12},{3,13},{4,10},{5,11},{6,8},{7,9},{8,6},{9,7},... | collective-permute-start | bytes 61448 | tf_op jit(solution)/shard_map/ppermute | solution.py:887
  40.0 1.1 %collective-permute-start.6 = (f32[2,10,2,128]{3,2,1,0:T(2,128)S(1)}, f32[2,10,2,128]{3,2,1,0:T(2,128)S(1)}, u32[]{:S(2)}, u32[]{:S(2)}) collective-permute-start(f32[2,10,2,128]{3,2,1,0:T(2,128)S(1)} %get-tuple-element.102), channel_id=1, source_target_pairs={{0,6},{1,7},{2,4},{3,5},{4,2},{5,3},{6,0},{7,1},{8,14},{9,15},{10,... | collective-permute-start | bytes 61448 | tf_op jit(solution)/shard_map/ppermute | solution.py:889
  41.0 1.5 %collective-permute-start.10 = (f32[4,10,2,128]{3,2,1,0:T(2,128)S(1)}, f32[4,10,2,128]{3,2,1,0:T(2,128)S(1)}, u32[]{:S(2)}, u32[]{:S(2)}) collective-permute-start(f32[4,10,2,128]{3,2,1,0:T(2,128)S(1)} %constant_dynamic-update-slice_fusion.5.first), channel_id=1, source_target_pairs={{0,2},{1,3},{2,0},{3,1},{4,6},{5,7},{6,4},{7,5},{8,10},{9,11},{10,... | collective-permute-start | bytes 122888 | tf_op jit(solution)/shard_map/ppermute | solution.py:861
  42.6 1.8 %shard_map.70 = (f32[32,11,2,8,128]{4,3,2,1,0:T(8,128)S(1)}, f32[8,8,128]{2,1,0:T(8,128)S(1)}) custom-call(f32[40,8,128]{2,1,0:T(8,128)S(1)} %bitcast.27, f32[40,2,128]{2,1,0:T(2,128)S(1)} %bitcast.41, f32[32,11,8,8,128]{4,3,2,1,0:T(8,128)S(1)} %get-tuple-element.65.stored), custom_call_target="tpu_custom_call" | custom-call | flops 21626880 | bytes 5767168 | tf_op jit(solution)/shard_map/pallas_call | solution.py:481
  44.4 0.0 collective-permute-done.8
  44.4 0.0 collective-permute-done.9
  44.4 0.7 collective-permute-done.10
  45.1 2.2 %shard_map.71 = (f32[32,11,2,8,128]{4,3,2,1,0:T(8,128)S(1)}, f32[32,8,128]{2,1,0:T(8,128)S(1)}) custom-call(f32[20,8,128]{2,1,0:T(8,128)S(1)} %bitcast.40, f32[20,8,128]{2,1,0:T(8,128)S(1)} %bitcast.37, f32[40,8,128]{2,1,0:T(8,128)S(1)} %bitcast.43, f32[20,2,128]{2,1,0:T(2,128)S(1)} %bitcast.51, f32[20,2,128]{2,1,0:T(2,128)S(1)} %bitcast.50, ...), custom_call_target="tpu_custom_call" | custom-call | flops 21626880 | bytes 5767168 | tf_op jit(solution)/shard_map/pallas_call | solution.py:481
  47.4 0.0 collective-permute-done.7
  47.4 0.0 collective-permute-done.6
  47.4 0.7 shard_map.72
  48.1 0.1 collective-permute-start.11
  48.2 1.6 %shard_map.73 = f32[24,2,128]{2,1,0:T(2,128)S(1)} custom-call(f32[40,8,128]{2,1,0:T(8,128)S(1)} %bitcast.34, f32[40,2,128]{2,1,0:T(2,128)S(1)} %bitcast.48, f32[24,11,3,8,128]{4,3,2,1,0:T(8,128)S(1)} %get-tuple-element.78.stored.inner, f32[32,11,2,8,128]{4,3,2,1,0:T(8,128)S(1)} %get-tuple-element.76.before, ...), custom_call_target="tpu_custom_call" | custom-call | flops 21626880 | bytes 5767168 | tf_op jit(solution)/shard_map/pallas_call | solution.py:481
  49.8 0.0 collective-permute-done.11
  49.9 1.5 %collective-permute-start.14 = (f32[4,10,2,128]{3,2,1,0:T(2,128)S(1)}, f32[4,10,2,128]{3,2,1,0:T(2,128)S(1)}, u32[]{:S(2)}, u32[]{:S(2)}) collective-permute-start(f32[4,10,2,128]{3,2,1,0:T(2,128)S(1)} %constant_dynamic-update-slice_fusion.10.second), channel_id=1, source_target_pairs={{0,2},{1,3},{2,0},{3,1},{4,6},{5,7},{6,4},{7,5},{8,10},{9,11},{10,... | collective-permute-start | bytes 122888 | tf_op jit(solution)/shard_map/ppermute | solution.py:861
  51.4 1.3 %collective-permute-start.13 = (f32[2,10,2,128]{3,2,1,0:T(2,128)S(1)}, f32[2,10,2,128]{3,2,1,0:T(2,128)S(1)}, u32[]{:S(2)}, u32[]{:S(2)}) collective-permute-start(f32[2,10,2,128]{3,2,1,0:T(2,128)S(1)} %slice.93), channel_id=1, source_target_pairs={{0,12},{1,13},{2,14},{3,15},{4,0},{5,1},{6,2},{7,3},{8,4},{9,5},{1... | collective-permute-start | bytes 61448 | tf_op jit(solution)/shard_map/ppermute | solution.py:867
  52.8 1.1 %collective-permute-start.12 = (f32[2,10,2,128]{3,2,1,0:T(2,128)S(1)}, f32[2,10,2,128]{3,2,1,0:T(2,128)S(1)}, u32[]{:S(2)}, u32[]{:S(2)}) collective-permute-start(f32[2,10,2,128]{3,2,1,0:T(2,128)S(1)} %slice.93), channel_id=1, source_target_pairs={{0,14},{1,15},{2,12},{3,13},{4,2},{5,3},{6,0},{7,1},{8,6},{9,7},{1... | collective-permute-start | bytes 61448 | tf_op jit(solution)/shard_map/ppermute | solution.py:867
  53.9 2.4 %shard_map.74 = (f32[32,11,2,8,128]{4,3,2,1,0:T(8,128)S(1)}, f32[8,8,128]{2,1,0:T(8,128)S(1)}, f32[32,11,2,8,128]{4,3,2,1,0:T(8,128)S(1)}, f32[2,128]{1,0:T(2,128)S(1)}) custom-call(f32[40,8,128]{2,1,0:T(8,128)S(1)} %bitcast.30, f32[40,2,128]{2,1,0:T(2,128)S(1)} %bitcast.45, f32[32,11,8,8,128]{4,3,2,1,0:T(8,128)S(1)} %get-tuple-element.65.stored, ...), custom_call_target="tpu_custom_call" | custom-call | flops 21626880 | bytes 5767168 | tf_op jit(solution)/shard_map/pallas_call | solution.py:481
  56.3 0.0 collective-permute-done.13
  56.3 0.0 collective-permute-done.14
  56.3 1.1 %shard_map.75 = (f32[32,11,2,8,128]{4,3,2,1,0:T(8,128)S(1)}, f32[32,8,128]{2,1,0:T(8,128)S(1)}) custom-call(f32[20,8,128]{2,1,0:T(8,128)S(1)} %bitcast.38, f32[40,8,128]{2,1,0:T(8,128)S(1)} %bitcast.44, f32[20,2,128]{2,1,0:T(2,128)S(1)} %bitcast.59, f32[40,2,128]{2,1,0:T(2,128)S(1)} %bitcast.52, f32[32,11,8,8,128]{4,3,2,1,0:T(8,128)S(1)} %get-tuple-element.69.refs_6_.stored, ...), custom_call_target="tpu_custom_call" | custom-call | flops 21626880 | bytes 5767168 | tf_op jit(solution)/shard_map/pallas_call | solution.py:481
  57.4 0.1 collective-permute-done.12
  57.5 0.0 copy-start
  57.5 0.0 copy-start.1
  57.5 1.0 %shard_map.76 = f32[1,128]{1,0:T(1,128)S(1)} custom-call(f32[40,8,128]{2,1,0:T(8,128)S(1)} %bitcast.35, f32[20,2,128]{2,1,0:T(2,128)S(1)} %bitcast.58, f32[8,11,3,8,128]{4,3,2,1,0:T(8,128)S(1)} %get-tuple-element.75.stored.edge, f32[24,11,3,8,128]{4,3,2,1,0:T(8,128)S(1)} %get-tuple-element.78.stored.inner, ...), custom_call_target="tpu_custom_call" | custom-call | flops 21626880 | bytes 5767168 | tf_op jit(solution)/shard_map/pallas_call | solution.py:481
  58.5 0.0 collective-permute-start.15
  58.5 1.1 %collective-permute-done.15 = f32[1,128]{1,0:T(1,128)S(1)} collective-permute-done((f32[1,128]{1,0:T(1,128)S(1)}, f32[1,128]{1,0:T(1,128)S(1)}, u32[]{:S(2)}, u32[]{:S(2)}) %collective-permute-start.15) | collective-permute-done | bytes 544 | tf_op jit(solution)/shard_map/ppermute | solution.py:861
  59.6 1.3 %collective-permute-start.18 = (f32[1,128]{1,0:T(1,128)S(1)}, f32[1,128]{1,0:T(1,128)S(1)}, u32[]{:S(2)}, u32[]{:S(2)}) collective-permute-start(f32[1,128]{1,0:T(1,128)S(1)} %add.26), channel_id=1, source_target_pairs={{0,2},{1,3},{2,0},{3,1},{4,6},{5,7},{6,4},{7,5},{8,10},{9,11},{10,... | collective-permute-start | bytes 1544 | tf_op jit(solution)/shard_map/ppermute | solution.py:861
  60.9 1.1 %collective-permute-start.17 = (f32[1,128]{1,0:T(1,128)S(1)}, f32[1,128]{1,0:T(1,128)S(1)}, u32[]{:S(2)}, u32[]{:S(2)}) collective-permute-start(f32[1,128]{1,0:T(1,128)S(1)} %add.26), channel_id=1, source_target_pairs={{0,4},{1,5},{2,6},{3,7},{4,0},{5,1},{6,2},{7,3},{8,12},{9,13},{10,... | collective-permute-start | bytes 1544 | tf_op jit(solution)/shard_map/ppermute | solution.py:861
  62.0 1.1 %collective-permute-start.16 = (f32[1,128]{1,0:T(1,128)S(1)}, f32[1,128]{1,0:T(1,128)S(1)}, u32[]{:S(2)}, u32[]{:S(2)}) collective-permute-start(f32[1,128]{1,0:T(1,128)S(1)} %add.26), channel_id=1, source_target_pairs={{0,6},{1,7},{2,4},{3,5},{4,2},{5,3},{6,0},{7,1},{8,14},{9,15},{10,... | collective-permute-start | bytes 1544 | tf_op jit(solution)/shard_map/ppermute | solution.py:861
  63.1 0.1 collective-permute-done.18
  63.1 1.3 %collective-permute-done.17 = f32[1,128]{1,0:T(1,128)S(1)} collective-permute-done((f32[1,128]{1,0:T(1,128)S(1)}, f32[1,128]{1,0:T(1,128)S(1)}, u32[]{:S(2)}, u32[]{:S(2)}) %collective-permute-start.17) | collective-permute-done | bytes 544 | tf_op jit(solution)/shard_map/ppermute | solution.py:861
  64.4 2.0 %collective-permute-done.16 = f32[1,128]{1,0:T(1,128)S(1)} collective-permute-done((f32[1,128]{1,0:T(1,128)S(1)}, f32[1,128]{1,0:T(1,128)S(1)}, u32[]{:S(2)}, u32[]{:S(2)}) %collective-permute-start.16) | collective-permute-done | bytes 544 | tf_op jit(solution)/shard_map/ppermute | solution.py:861
  66.4 1.6 %collective-permute-start.19 = (f32[1,128]{1,0:T(1,128)S(1)}, f32[1,128]{1,0:T(1,128)S(1)}, u32[]{:S(2)}, u32[]{:S(2)}) collective-permute-start(f32[1,128]{1,0:T(1,128)S(1)} %add_add_fusion), channel_id=1, source_target_pairs={{0,8},{1,9},{2,10},{3,11},{4,12},{5,13},{6,14},{7,15},{8,0},{9,1},... | collective-permute-start | bytes 1544 | tf_op jit(solution)/shard_map/ppermute | solution.py:861
  68.0 0.0 copy-done
  68.0 0.0 copy-done.1
  68.0 1.7 %shard_map.77.places = s32[2,32,128]{2,1,0:T(8,128)S(1)} custom-call(s32[32]{0:T(128)S(1)} %copy-done.1, s32[32,128]{1,0:T(8,128)S(1)} %copy-done), custom_call_target="tpu_custom_call" | custom-call | flops 21626880 | bytes 5767168 | tf_op jit(solution)/shard_map/pallas_call | solution.py:481
  69.8 1.1 %collective-permute-done.19 = f32[1,128]{1,0:T(1,128)S(1)} collective-permute-done((f32[1,128]{1,0:T(1,128)S(1)}, f32[1,128]{1,0:T(1,128)S(1)}, u32[]{:S(2)}, u32[]{:S(2)}) %collective-permute-start.19) | collective-permute-done | bytes 544 | tf_op jit(solution)/shard_map/ppermute | solution.py:861
  70.9 1.1 %shard_map.78 = f32[20,128]{1,0:T(8,128)} custom-call(f32[1,128]{1,0:T(1,128)S(1)} %add.30.moments, f32[4,10,8,128]{3,2,1,0:T(8,128)S(1)} %constant_dynamic-update-slice_fusion.slots, f32[4,10,2,128]{3,2,1,0:T(2,128)S(1)} %constant_dynamic-update-slice_fusion.5.first, f32[4,10,2,128]{3,2,1,0:T(2,128)S(1)} %constant_dynamic-update-slice_fusion.10.second, ...), custom_call_target="tpu_custom_call" | custom-call | tf_op jit(solution)/shard_map/pallas_call | solution.py:849
  (26 shorter events, 0.2 us)
Async XLA Ops:
  1.1 1.4 %collective-permute-start = (f32[4,2,8,128]{3,2,1,0:T(8,128)S(1)}, f32[4,2,8,128]{3,2,1,0:T(8,128)S(1)}, u32[]{:S(2)}, u32[]{:S(2)}) collective-permute-start(f32[4,2,8,128]{3,2,1,0:T(8,128)S(1)} %bitcast.54), channel_id=1, source_target_pairs={{0,1},{1,0},{2,3},{3,2},{4,5},{5,4},{6,7},{7,6},{8,9},{9,8},{10,11... | collective-permute-start | bytes 98312 | tf_op jit(solution)/shard_map/ppermute | solution.py:861
  2.5 17.5 %collective-permute-start.3 = (f32[4,10,8,128]{3,2,1,0:T(8,128)S(1)}, f32[4,10,8,128]{3,2,1,0:T(8,128)S(1)}, u32[]{:S(2)}, u32[]{:S(2)}) collective-permute-start(f32[4,10,8,128]{3,2,1,0:T(8,128)S(1)} %constant_dynamic-update-slice_fusion.slots), channel_id=1, source_target_pairs={{0,2},{1,3},{2,0},{3,1},{4,6},{5,7},{6,4},{7,5},{8,10},{9,11},{10,... | collective-permute-start | bytes 491528 | tf_op jit(solution)/shard_map/ppermute | solution.py:861
  5.5 14.6 %collective-permute-start.2 = (f32[2,10,8,128]{3,2,1,0:T(8,128)S(1)}, f32[2,10,8,128]{3,2,1,0:T(8,128)S(1)}, u32[]{:S(2)}, u32[]{:S(2)}) collective-permute-start(f32[2,10,8,128]{3,2,1,0:T(8,128)S(1)} %get-tuple-element.95), channel_id=1, source_target_pairs={{0,4},{1,5},{2,6},{3,7},{4,0},{5,1},{6,2},{7,3},{8,12},{9,13},{10,... | collective-permute-start | bytes 245768 | tf_op jit(solution)/shard_map/ppermute | solution.py:889
  7.1 12.9 %collective-permute-start.1 = (f32[2,10,8,128]{3,2,1,0:T(8,128)S(1)}, f32[2,10,8,128]{3,2,1,0:T(8,128)S(1)}, u32[]{:S(2)}, u32[]{:S(2)}) collective-permute-start(f32[2,10,8,128]{3,2,1,0:T(8,128)S(1)} %get-tuple-element.96), channel_id=1, source_target_pairs={{0,12},{1,13},{2,14},{3,15},{4,8},{5,9},{6,10},{7,11},{8,4},{9,5},... | collective-permute-start | bytes 245768 | tf_op jit(solution)/shard_map/ppermute | solution.py:887
  20.1 10.4 %collective-permute-start.4 = (f32[4,10,8,128]{3,2,1,0:T(8,128)S(1)}, f32[4,10,8,128]{3,2,1,0:T(8,128)S(1)}, u32[]{:S(2)}, u32[]{:S(2)}) collective-permute-start(f32[4,10,8,128]{3,2,1,0:T(8,128)S(1)} %pad_maximum_fusion), channel_id=1, source_target_pairs={{0,2},{1,3},{2,0},{3,1},{4,6},{5,7},{6,4},{7,5},{8,10},{9,11},{10,... | collective-permute-start | bytes 491528 | tf_op jit(solution)/shard_map/ppermute | solution.py:861
  31.7 3.3 %collective-permute-start.5 = (f32[4,2,2,128]{3,2,1,0:T(2,128)S(1)}, f32[4,2,2,128]{3,2,1,0:T(2,128)S(1)}, u32[]{:S(2)}, u32[]{:S(2)}) collective-permute-start(f32[4,2,2,128]{3,2,1,0:T(2,128)S(1)} %bitcast.60), channel_id=1, source_target_pairs={{0,1},{1,0},{2,3},{3,2},{4,5},{5,4},{6,7},{7,6},{8,9},{9,8},{10,11... | collective-permute-start | bytes 24584 | tf_op jit(solution)/shard_map/ppermute | solution.py:861
  35.1 9.3 %collective-permute-start.8 = (f32[2,10,2,128]{3,2,1,0:T(2,128)S(1)}, f32[2,10,2,128]{3,2,1,0:T(2,128)S(1)}, u32[]{:S(2)}, u32[]{:S(2)}) collective-permute-start(f32[2,10,2,128]{3,2,1,0:T(2,128)S(1)} %get-tuple-element.101), channel_id=1, source_target_pairs={{0,12},{1,13},{2,14},{3,15},{4,8},{5,9},{6,10},{7,11},{8,4},{9,5},... | collective-permute-start | bytes 61448 | tf_op jit(solution)/shard_map/ppermute | solution.py:887
  36.5 7.9 %collective-permute-start.9 = (f32[2,10,2,128]{3,2,1,0:T(2,128)S(1)}, f32[2,10,2,128]{3,2,1,0:T(2,128)S(1)}, u32[]{:S(2)}, u32[]{:S(2)}) collective-permute-start(f32[2,10,2,128]{3,2,1,0:T(2,128)S(1)} %get-tuple-element.102), channel_id=1, source_target_pairs={{0,4},{1,5},{2,6},{3,7},{4,0},{5,1},{6,2},{7,3},{8,12},{9,13},{10,... | collective-permute-start | bytes 61448 | tf_op jit(solution)/shard_map/ppermute | solution.py:889
  36.5 10.8 %collective-permute-start.7 = (f32[2,10,2,128]{3,2,1,0:T(2,128)S(1)}, f32[2,10,2,128]{3,2,1,0:T(2,128)S(1)}, u32[]{:S(2)}, u32[]{:S(2)}) collective-permute-start(f32[2,10,2,128]{3,2,1,0:T(2,128)S(1)} %get-tuple-element.101), channel_id=1, source_target_pairs={{0,14},{1,15},{2,12},{3,13},{4,10},{5,11},{6,8},{7,9},{8,6},{9,7},... | collective-permute-start | bytes 61448 | tf_op jit(solution)/shard_map/ppermute | solution.py:887
  40.0 7.4 %collective-permute-start.6 = (f32[2,10,2,128]{3,2,1,0:T(2,128)S(1)}, f32[2,10,2,128]{3,2,1,0:T(2,128)S(1)}, u32[]{:S(2)}, u32[]{:S(2)}) collective-permute-start(f32[2,10,2,128]{3,2,1,0:T(2,128)S(1)} %get-tuple-element.102), channel_id=1, source_target_pairs={{0,6},{1,7},{2,4},{3,5},{4,2},{5,3},{6,0},{7,1},{8,14},{9,15},{10,... | collective-permute-start | bytes 61448 | tf_op jit(solution)/shard_map/ppermute | solution.py:889
  41.0 4.1 %collective-permute-start.10 = (f32[4,10,2,128]{3,2,1,0:T(2,128)S(1)}, f32[4,10,2,128]{3,2,1,0:T(2,128)S(1)}, u32[]{:S(2)}, u32[]{:S(2)}) collective-permute-start(f32[4,10,2,128]{3,2,1,0:T(2,128)S(1)} %constant_dynamic-update-slice_fusion.5.first), channel_id=1, source_target_pairs={{0,2},{1,3},{2,0},{3,1},{4,6},{5,7},{6,4},{7,5},{8,10},{9,11},{10,... | collective-permute-start | bytes 122888 | tf_op jit(solution)/shard_map/ppermute | solution.py:861
  48.1 1.7 %collective-permute-start.11 = (f32[4,2,2,128]{3,2,1,0:T(2,128)S(1)}, f32[4,2,2,128]{3,2,1,0:T(2,128)S(1)}, u32[]{:S(2)}, u32[]{:S(2)}) collective-permute-start(f32[4,2,2,128]{3,2,1,0:T(2,128)S(1)} %bitcast.63), channel_id=1, source_target_pairs={{0,1},{1,0},{2,3},{3,2},{4,5},{5,4},{6,7},{7,6},{8,9},{9,8},{10,11... | collective-permute-start | bytes 24584 | tf_op jit(solution)/shard_map/ppermute | solution.py:861
  49.9 6.4 %collective-permute-start.14 = (f32[4,10,2,128]{3,2,1,0:T(2,128)S(1)}, f32[4,10,2,128]{3,2,1,0:T(2,128)S(1)}, u32[]{:S(2)}, u32[]{:S(2)}) collective-permute-start(f32[4,10,2,128]{3,2,1,0:T(2,128)S(1)} %constant_dynamic-update-slice_fusion.10.second), channel_id=1, source_target_pairs={{0,2},{1,3},{2,0},{3,1},{4,6},{5,7},{6,4},{7,5},{8,10},{9,11},{10,... | collective-permute-start | bytes 122888 | tf_op jit(solution)/shard_map/ppermute | solution.py:861
  51.4 4.8 %collective-permute-start.13 = (f32[2,10,2,128]{3,2,1,0:T(2,128)S(1)}, f32[2,10,2,128]{3,2,1,0:T(2,128)S(1)}, u32[]{:S(2)}, u32[]{:S(2)}) collective-permute-start(f32[2,10,2,128]{3,2,1,0:T(2,128)S(1)} %slice.93), channel_id=1, source_target_pairs={{0,12},{1,13},{2,14},{3,15},{4,0},{5,1},{6,2},{7,3},{8,4},{9,5},{1... | collective-permute-start | bytes 61448 | tf_op jit(solution)/shard_map/ppermute | solution.py:867
  52.8 4.7 %collective-permute-start.12 = (f32[2,10,2,128]{3,2,1,0:T(2,128)S(1)}, f32[2,10,2,128]{3,2,1,0:T(2,128)S(1)}, u32[]{:S(2)}, u32[]{:S(2)}) collective-permute-start(f32[2,10,2,128]{3,2,1,0:T(2,128)S(1)} %slice.93), channel_id=1, source_target_pairs={{0,14},{1,15},{2,12},{3,13},{4,2},{5,3},{6,0},{7,1},{8,6},{9,7},{1... | collective-permute-start | bytes 61448 | tf_op jit(solution)/shard_map/ppermute | solution.py:867
  57.5 10.6 %copy-start = (s32[32,128]{1,0:T(8,128)S(1)}, s32[32,128]{1,0:T(8,128)}, u32[]{:S(2)}) copy-start(s32[32,128]{1,0:T(8,128)} %atoms) | copy-start | bytes 49156
  57.5 10.6 %copy-start.1 = (s32[32]{0:T(128)S(1)}, s32[32]{0:T(128)}, u32[]{:S(2)}) copy-start(s32[32]{0:T(128)} %counts) | copy-start | bytes 388
  58.5 1.1 %collective-permute-start.15 = (f32[1,128]{1,0:T(1,128)S(1)}, f32[1,128]{1,0:T(1,128)S(1)}, u32[]{:S(2)}, u32[]{:S(2)}) collective-permute-start(f32[1,128]{1,0:T(1,128)S(1)} %shard_map.76), channel_id=1, source_target_pairs={{0,1},{1,0},{2,3},{3,2},{4,5},{5,4},{6,7},{7,6},{8,9},{9,8},{10,11... | collective-permute-start | bytes 1544 | tf_op jit(solution)/shard_map/ppermute | solution.py:861
  59.6 3.5 %collective-permute-start.18 = (f32[1,128]{1,0:T(1,128)S(1)}, f32[1,128]{1,0:T(1,128)S(1)}, u32[]{:S(2)}, u32[]{:S(2)}) collective-permute-start(f32[1,128]{1,0:T(1,128)S(1)} %add.26), channel_id=1, source_target_pairs={{0,2},{1,3},{2,0},{3,1},{4,6},{5,7},{6,4},{7,5},{8,10},{9,11},{10,... | collective-permute-start | bytes 1544 | tf_op jit(solution)/shard_map/ppermute | solution.py:861
  60.9 3.5 %collective-permute-start.17 = (f32[1,128]{1,0:T(1,128)S(1)}, f32[1,128]{1,0:T(1,128)S(1)}, u32[]{:S(2)}, u32[]{:S(2)}) collective-permute-start(f32[1,128]{1,0:T(1,128)S(1)} %add.26), channel_id=1, source_target_pairs={{0,4},{1,5},{2,6},{3,7},{4,0},{5,1},{6,2},{7,3},{8,12},{9,13},{10,... | collective-permute-start | bytes 1544 | tf_op jit(solution)/shard_map/ppermute | solution.py:861
  62.0 4.4 %collective-permute-start.16 = (f32[1,128]{1,0:T(1,128)S(1)}, f32[1,128]{1,0:T(1,128)S(1)}, u32[]{:S(2)}, u32[]{:S(2)}) collective-permute-start(f32[1,128]{1,0:T(1,128)S(1)} %add.26), channel_id=1, source_target_pairs={{0,6},{1,7},{2,4},{3,5},{4,2},{5,3},{6,0},{7,1},{8,14},{9,15},{10,... | collective-permute-start | bytes 1544 | tf_op jit(solution)/shard_map/ppermute | solution.py:861
  66.4 4.4 %collective-permute-start.19 = (f32[1,128]{1,0:T(1,128)S(1)}, f32[1,128]{1,0:T(1,128)S(1)}, u32[]{:S(2)}, u32[]{:S(2)}) collective-permute-start(f32[1,128]{1,0:T(1,128)S(1)} %add_add_fusion), channel_id=1, source_target_pairs={{0,8},{1,9},{2,10},{3,11},{4,12},{5,13},{6,14},{7,15},{8,0},{9,1},... | collective-permute-start | bytes 1544 | tf_op jit(solution)/shard_map/ppermute | solution.py:861

commit v2 on v0

--- a/solution.py
+++ b/solution.py
@@ -835,7 +835,7 @@
         q, z = cell // CZ, cell % CZ + 1
         mixed = c_0 * slots[q, z, 4:6, :] + c_1 * first[q, z] + c_2 * second[q, z]
         charges[cell : cell + 1, :] = jnp.sum(mixed, axis=0, keepdims=True)
-    tiles = [jnp.zeros((8, LANES), jnp.float32) for _ in range(places.shape[1] // 8)]
+    tiles = [jnp.zeros((8, LANES), jnp.float32) for _ in range((out.shape[0] + 7) // 8)]
     for cell in range(CELLS):
         line = spread(charges[cell : cell + 1, :])
         for at in range(len(tiles)):
@@ -920,7 +920,7 @@
     step = 1
     while step < count:
         if step >= 2 and 4 * step <= count:
-            others = [partner(values, "gx", k * step) for k in (3, 2, 1)]
+            others = [partner(values, "gx", k * step) for k in (1, 2, 3)]
             values = (values + others[0]) + (others[1] + others[2])
             step *= 4
         else:

time: 70 us -> 69.3 us (0.990)
  waiting for transfers between devices: 7.25 us -> 6.53 us
    ppermute x13, waiting for transfers between devices: 5.9 us -> 5.19 us  [partner(): lax.ppermute(block, axis, [(low, low ^ mask) for low in range(count)])]
  transfers between devices with their start and end apart: 19 -> 19, of which waited for: 8 -> 8; matrix products, arithmetic and copies ran while one was open for 0% -> 0% of each run, Pallas kernels for 50% -> 51%
where the time goes in v2:
time: 69.3 us; the launch traced here: 69.1 us
  Pallas kernels  40.2 us (58%)
  starting transfers between devices  21.8 us (31%)
  waiting for transfers between devices  6.53 us (9%)
    pallas_call x12, Pallas kernels, call(): pl.pallas_call(kernel, out_shape=outs, in_specs=[IN_SMEM if array.ndim ==...  37.3 us
    ppermute x13, starting transfers between devices, partner(): lax.ppermute(block, axis, [(low, low ^ mask) for low in range(count)])  14.1 us
    ppermute x13, waiting for transfers between devices, partner(): lax.ppermute(block, axis, [(low, low ^ mask) for low in range(count)])  5.19 us
    ppermute x2, starting transfers between devices, x_faces(): second = lax.ppermute(jnp.where(odd, core[2:], core[:2]), 'gx', route)  3.38 us
    ppermute x2, starting transfers between devices, x_faces(): lax.ppermute(jnp.where(odd, core[:2], core[2:]), 'gx', [(i, i ^ 4) for i...  2.39 us
    ppermute x2, starting transfers between devices, shifted(): return lax.ppermute(block, 'gx', route)  2.01 us
  transfers between devices with their start and end apart: 19, of which 8 were waited for; matrix products, arithmetic and copies ran while one was open for 0% of the time, Pallas kernels for 51%

profile of v2, /device:TPU:0, one launch (start us, length us, event | category | flops | bytes accessed | tf_op | source)
XLA Modules:
  0.0 69.1 jit_solution(13629076020653159284)
XLA Ops:
  0.0 1.1 %shard_map.64 = (f32[8,8,128]{2,1,0:T(8,128)S(1)}, s32[32,128]{1,0:T(8,128)S(1)}, s32[32,128]{1,0:T(8,128)S(1)}, f32[20,8,128]{2,1,0:T(8,128)S(1)}, f32[20,8,128]{2,1,0:T(8,128)S(1)}) custom-call(s32[32]{0:T(128)} %counts, f32[3,2560]{1,0:T(4,128)} %offsets.1, f32[20,128]{1,0:T(8,128)} %bitcast.66, f32[20,128]{1,0:T(8,128)} %bitcast.67, f32[20,128]{1,0:T(8,128)} %bitcast.68, ...), custom_call_target="tpu_custom_call" | custom-call | tf_op jit(solution)/shard_map/pallas_call | solution.py:153
  1.1 0.5 collective-permute-start
  1.6 0.7 %shard_map.65 = f32[24,8,128]{2,1,0:T(8,128)S(1)} custom-call(s32[32,128]{1,0:T(8,128)S(1)} %get-tuple-element.47.counted, s32[32,128]{1,0:T(8,128)S(1)} %get-tuple-element.48.atoms, f32[20,8,128]{2,1,0:T(8,128)S(1)} %get-tuple-element.49.table, f32[20,8,128]{2,1,0:T(8,128)S(1)} %get-tuple-element.50.others), custom_call_target="tpu_custom_call" | custom-call | flops 1048576 | bytes 4194304 | tf_op jit(solution)/shard_map/pallas_call | solution.py:186
  2.4 0.1 collective-permute-done
  2.5 2.9 %collective-permute-start.3 = (f32[4,10,8,128]{3,2,1,0:T(8,128)S(1)}, f32[4,10,8,128]{3,2,1,0:T(8,128)S(1)}, u32[]{:S(2)}, u32[]{:S(2)}) collective-permute-start(f32[4,10,8,128]{3,2,1,0:T(8,128)S(1)} %constant_dynamic-update-slice_fusion.slots), channel_id=1, source_target_pairs={{0,2},{1,3},{2,0},{3,1},{4,6},{5,7},{6,4},{7,5},{8,10},{9,11},{10,... | collective-permute-start | bytes 491528 | tf_op jit(solution)/shard_map/ppermute | solution.py:861
  5.5 1.6 %collective-permute-start.2 = (f32[2,10,8,128]{3,2,1,0:T(8,128)S(1)}, f32[2,10,8,128]{3,2,1,0:T(8,128)S(1)}, u32[]{:S(2)}, u32[]{:S(2)}) collective-permute-start(f32[2,10,8,128]{3,2,1,0:T(8,128)S(1)} %get-tuple-element.89), channel_id=1, source_target_pairs={{0,4},{1,5},{2,6},{3,7},{4,0},{5,1},{6,2},{7,3},{8,12},{9,13},{10,... | collective-permute-start | bytes 245768 | tf_op jit(solution)/shard_map/ppermute | solution.py:888
  7.1 2.5 %collective-permute-start.1 = (f32[2,10,8,128]{3,2,1,0:T(8,128)S(1)}, f32[2,10,8,128]{3,2,1,0:T(8,128)S(1)}, u32[]{:S(2)}, u32[]{:S(2)}) collective-permute-start(f32[2,10,8,128]{3,2,1,0:T(8,128)S(1)} %get-tuple-element.90), channel_id=1, source_target_pairs={{0,12},{1,13},{2,14},{3,15},{4,8},{5,9},{6,10},{7,11},{8,4},{9,5},... | collective-permute-start | bytes 245768 | tf_op jit(solution)/shard_map/ppermute | solution.py:887
  9.6 10.5 %shard_map.66 = (f32[32,11,8,8,128]{4,3,2,1,0:T(8,128)S(1)}, f32[32,11,2,8,128]{4,3,2,1,0:T(8,128)S(1)}, f32[8,8,128]{2,1,0:T(8,128)S(1)}, f32[32,11,4,8,128]{4,3,2,1,0:T(8,128)S(1)}) custom-call(f32[40,8,128]{2,1,0:T(8,128)S(1)} %bitcast.24), custom_call_target="tpu_custom_call" | custom-call | flops 86507520 | bytes 23068672 | tf_op jit(solution)/shard_map/pallas_call | solution.py:481
  20.1 0.0 collective-permute-done.2
  20.1 0.0 collective-permute-done.1
  20.1 0.0 collective-permute-done.3
  20.1 0.6 collective-permute-start.4
  20.7 9.8 %shard_map.67 = (f32[32,11,8,8,128]{4,3,2,1,0:T(8,128)S(1)}, f32[32,11,2,8,128]{4,3,2,1,0:T(8,128)S(1)}, f32[32,8,128]{2,1,0:T(8,128)S(1)}) custom-call(f32[20,8,128]{2,1,0:T(8,128)S(1)} %bitcast.39, f32[20,8,128]{2,1,0:T(8,128)S(1)} %bitcast.36, f32[40,8,128]{2,1,0:T(8,128)S(1)} %bitcast.42, f32[32,11,4,8,128]{4,3,2,1,0:T(8,128)S(1)} %get-tuple-element.54.turned, ...), custom_call_target="tpu_custom_call" | custom-call | flops 86507520 | bytes 23068672 | tf_op jit(solution)/shard_map/pallas_call | solution.py:481
  30.5 0.0 collective-permute-done.4
  30.5 1.2 %shard_map.68 = (f32[8,11,3,8,128]{4,3,2,1,0:T(8,128)S(1)}, f32[8,2,128]{2,1,0:T(2,128)S(1)}) custom-call(f32[40,8,128]{2,1,0:T(8,128)S(1)} %bitcast.31, f32[32,11,4,8,128]{4,3,2,1,0:T(8,128)S(1)} %get-tuple-element.54.turned, f32[32,11,2,8,128]{4,3,2,1,0:T(8,128)S(1)} %get-tuple-element.58.before, f32[32,8,128]{2,1,0:T(8,128)S(1)} %get-tuple-element.59.spill_before, ...), custom_call_target="tpu_custom_call" | custom-call | flops 32440320 | bytes 8650752 | tf_op jit(solution)/shard_map/pallas_call | solution.py:481
  31.7 0.1 collective-permute-start.5
  31.8 3.2 %shard_map.69 = (f32[24,11,3,8,128]{4,3,2,1,0:T(8,128)S(1)}, f32[24,2,128]{2,1,0:T(2,128)S(1)}) custom-call(f32[40,8,128]{2,1,0:T(8,128)S(1)} %bitcast.32, f32[32,11,4,8,128]{4,3,2,1,0:T(8,128)S(1)} %get-tuple-element.54.turned, f32[32,11,2,8,128]{4,3,2,1,0:T(8,128)S(1)} %get-tuple-element.58.before, f32[32,8,128]{2,1,0:T(8,128)S(1)} %get-tuple-element.59.spill_before, ...), custom_call_target="tpu_custom_call" | custom-call | flops 32440320 | bytes 8650752 | tf_op jit(solution)/shard_map/pallas_call | solution.py:481
  35.0 0.0 collective-permute-done.5
  35.1 0.7 %collective-permute-start.7 = (f32[2,10,2,128]{3,2,1,0:T(2,128)S(1)}, f32[2,10,2,128]{3,2,1,0:T(2,128)S(1)}, u32[]{:S(2)}, u32[]{:S(2)}) collective-permute-start(f32[2,10,2,128]{3,2,1,0:T(2,128)S(1)} %get-tuple-element.93), channel_id=1, source_target_pairs={{0,4},{1,5},{2,6},{3,7},{4,0},{5,1},{6,2},{7,3},{8,12},{9,13},{10,... | collective-permute-start | bytes 61448 | tf_op jit(solution)/shard_map/ppermute | solution.py:888
  35.9 0.9 %collective-permute-start.6 = (f32[2,10,2,128]{3,2,1,0:T(2,128)S(1)}, f32[2,10,2,128]{3,2,1,0:T(2,128)S(1)}, u32[]{:S(2)}, u32[]{:S(2)}) collective-permute-start(f32[2,10,2,128]{3,2,1,0:T(2,128)S(1)} %get-tuple-element.94), channel_id=1, source_target_pairs={{0,12},{1,13},{2,14},{3,15},{4,8},{5,9},{6,10},{7,11},{8,4},{9,5},... | collective-permute-start | bytes 61448 | tf_op jit(solution)/shard_map/ppermute | solution.py:887
  36.8 1.5 %collective-permute-start.9 = (f32[4,10,2,128]{3,2,1,0:T(2,128)S(1)}, f32[4,10,2,128]{3,2,1,0:T(2,128)S(1)}, u32[]{:S(2)}, u32[]{:S(2)}) collective-permute-start(f32[4,10,2,128]{3,2,1,0:T(2,128)S(1)} %constant_dynamic-update-slice_fusion.5.first), channel_id=1, source_target_pairs={{0,2},{1,3},{2,0},{3,1},{4,6},{5,7},{6,4},{7,5},{8,10},{9,11},{10,... | collective-permute-start | bytes 122888 | tf_op jit(solution)/shard_map/ppermute | solution.py:861
  38.3 1.8 %shard_map.70 = (f32[32,11,2,8,128]{4,3,2,1,0:T(8,128)S(1)}, f32[8,8,128]{2,1,0:T(8,128)S(1)}) custom-call(f32[40,8,128]{2,1,0:T(8,128)S(1)} %bitcast.27, f32[40,2,128]{2,1,0:T(2,128)S(1)} %bitcast.41, f32[32,11,8,8,128]{4,3,2,1,0:T(8,128)S(1)} %get-tuple-element.62.stored), custom_call_target="tpu_custom_call" | custom-call | flops 21626880 | bytes 5767168 | tf_op jit(solution)/shard_map/pallas_call | solution.py:481
  40.1 0.0 collective-permute-done.7
  40.1 1.3 %collective-permute-done.6 = f32[2,10,2,128]{3,2,1,0:T(2,128)S(1)} collective-permute-done((f32[2,10,2,128]{3,2,1,0:T(2,128)S(1)}, f32[2,10,2,128]{3,2,1,0:T(2,128)S(1)}, u32[]{:S(2)}, u32[]{:S(2)}) %collective-permute-start.6) | collective-permute-done | bytes 20512 | tf_op jit(solution)/shard_map/ppermute | solution.py:887
  41.5 1.6 %collective-permute-start.8 = (f32[4,10,2,128]{3,2,1,0:T(2,128)S(1)}, f32[4,10,2,128]{3,2,1,0:T(2,128)S(1)}, u32[]{:S(2)}, u32[]{:S(2)}) collective-permute-start(f32[4,10,2,128]{3,2,1,0:T(2,128)S(1)} %pad_maximum_fusion.1), channel_id=1, source_target_pairs={{0,2},{1,3},{2,0},{3,1},{4,6},{5,7},{6,4},{7,5},{8,10},{9,11},{10,... | collective-permute-start | bytes 122888 | tf_op jit(solution)/shard_map/ppermute | solution.py:861
  43.1 0.0 collective-permute-done.9
  43.1 2.2 %shard_map.71 = (f32[32,11,2,8,128]{4,3,2,1,0:T(8,128)S(1)}, f32[32,8,128]{2,1,0:T(8,128)S(1)}) custom-call(f32[20,8,128]{2,1,0:T(8,128)S(1)} %bitcast.40, f32[20,8,128]{2,1,0:T(8,128)S(1)} %bitcast.37, f32[40,8,128]{2,1,0:T(8,128)S(1)} %bitcast.43, f32[20,2,128]{2,1,0:T(2,128)S(1)} %bitcast.47, f32[20,2,128]{2,1,0:T(2,128)S(1)} %bitcast.48, ...), custom_call_target="tpu_custom_call" | custom-call | flops 21626880 | bytes 5767168 | tf_op jit(solution)/shard_map/pallas_call | solution.py:481
  45.3 0.2 collective-permute-done.8
  45.6 0.7 shard_map.72
  46.3 0.1 collective-permute-start.10
  46.3 1.6 %shard_map.73 = f32[24,2,128]{2,1,0:T(2,128)S(1)} custom-call(f32[40,8,128]{2,1,0:T(8,128)S(1)} %bitcast.34, f32[40,2,128]{2,1,0:T(2,128)S(1)} %bitcast.52, f32[24,11,3,8,128]{4,3,2,1,0:T(8,128)S(1)} %get-tuple-element.72.stored.inner, f32[32,11,2,8,128]{4,3,2,1,0:T(8,128)S(1)} %get-tuple-element.70.before, ...), custom_call_target="tpu_custom_call" | custom-call | flops 21626880 | bytes 5767168 | tf_op jit(solution)/shard_map/pallas_call | solution.py:481
  48.0 0.0 collective-permute-done.10
  48.1 1.6 %collective-permute-start.13 = (f32[4,10,2,128]{3,2,1,0:T(2,128)S(1)}, f32[4,10,2,128]{3,2,1,0:T(2,128)S(1)}, u32[]{:S(2)}, u32[]{:S(2)}) collective-permute-start(f32[4,10,2,128]{3,2,1,0:T(2,128)S(1)} %constant_dynamic-update-slice_fusion.10.second), channel_id=1, source_target_pairs={{0,2},{1,3},{2,0},{3,1},{4,6},{5,7},{6,4},{7,5},{8,10},{9,11},{10,... | collective-permute-start | bytes 122888 | tf_op jit(solution)/shard_map/ppermute | solution.py:861
  49.6 0.9 %collective-permute-start.12 = (f32[2,10,2,128]{3,2,1,0:T(2,128)S(1)}, f32[2,10,2,128]{3,2,1,0:T(2,128)S(1)}, u32[]{:S(2)}, u32[]{:S(2)}) collective-permute-start(f32[2,10,2,128]{3,2,1,0:T(2,128)S(1)} %slice.89), channel_id=1, source_target_pairs={{0,12},{1,13},{2,14},{3,15},{4,0},{5,1},{6,2},{7,3},{8,4},{9,5},{1... | collective-permute-start | bytes 61448 | tf_op jit(solution)/shard_map/ppermute | solution.py:867
  50.5 1.1 %collective-permute-start.11 = (f32[2,10,2,128]{3,2,1,0:T(2,128)S(1)}, f32[2,10,2,128]{3,2,1,0:T(2,128)S(1)}, u32[]{:S(2)}, u32[]{:S(2)}) collective-permute-start(f32[2,10,2,128]{3,2,1,0:T(2,128)S(1)} %slice.89), channel_id=1, source_target_pairs={{0,14},{1,15},{2,12},{3,13},{4,2},{5,3},{6,0},{7,1},{8,6},{9,7},{1... | collective-permute-start | bytes 61448 | tf_op jit(solution)/shard_map/ppermute | solution.py:867
  51.7 2.4 %shard_map.74 = (f32[32,11,2,8,128]{4,3,2,1,0:T(8,128)S(1)}, f32[8,8,128]{2,1,0:T(8,128)S(1)}, f32[32,11,2,8,128]{4,3,2,1,0:T(8,128)S(1)}, f32[2,128]{1,0:T(2,128)S(1)}) custom-call(f32[40,8,128]{2,1,0:T(8,128)S(1)} %bitcast.30, f32[40,2,128]{2,1,0:T(2,128)S(1)} %bitcast.45, f32[32,11,8,8,128]{4,3,2,1,0:T(8,128)S(1)} %get-tuple-element.62.stored, ...), custom_call_target="tpu_custom_call" | custom-call | flops 21626880 | bytes 5767168 | tf_op jit(solution)/shard_map/pallas_call | solution.py:481
  54.1 0.0 collective-permute-done.12
  54.1 0.0 collective-permute-done.13
  54.1 1.1 %shard_map.75 = (f32[32,11,2,8,128]{4,3,2,1,0:T(8,128)S(1)}, f32[32,8,128]{2,1,0:T(8,128)S(1)}) custom-call(f32[20,8,128]{2,1,0:T(8,128)S(1)} %bitcast.38, f32[40,8,128]{2,1,0:T(8,128)S(1)} %bitcast.44, f32[20,2,128]{2,1,0:T(2,128)S(1)} %bitcast.59, f32[40,2,128]{2,1,0:T(2,128)S(1)} %bitcast.53, f32[32,11,8,8,128]{4,3,2,1,0:T(8,128)S(1)} %get-tuple-element.67.refs_6_.stored, ...), custom_call_target="tpu_custom_call" | custom-call | flops 21626880 | bytes 5767168 | tf_op jit(solution)/shard_map/pallas_call | solution.py:481
  55.2 0.0 collective-permute-done.11
  55.2 0.0 copy-start
  55.2 0.0 copy-start.1
  55.2 1.0 %shard_map.76 = f32[1,128]{1,0:T(1,128)S(1)} custom-call(f32[40,8,128]{2,1,0:T(8,128)S(1)} %bitcast.35, f32[20,2,128]{2,1,0:T(2,128)S(1)} %bitcast.58, f32[8,11,3,8,128]{4,3,2,1,0:T(8,128)S(1)} %get-tuple-element.66.stored.edge, f32[24,11,3,8,128]{4,3,2,1,0:T(8,128)S(1)} %get-tuple-element.72.stored.inner, ...), custom_call_target="tpu_custom_call" | custom-call | flops 21626880 | bytes 5767168 | tf_op jit(solution)/shard_map/pallas_call | solution.py:481
  56.3 0.0 collective-permute-start.14
  56.3 1.1 %collective-permute-done.14 = f32[1,128]{1,0:T(1,128)S(1)} collective-permute-done((f32[1,128]{1,0:T(1,128)S(1)}, f32[1,128]{1,0:T(1,128)S(1)}, u32[]{:S(2)}, u32[]{:S(2)}) %collective-permute-start.14) | collective-permute-done | bytes 544 | tf_op jit(solution)/shard_map/ppermute | solution.py:861
  57.4 1.8 %collective-permute-start.17 = (f32[1,128]{1,0:T(1,128)S(1)}, f32[1,128]{1,0:T(1,128)S(1)}, u32[]{:S(2)}, u32[]{:S(2)}) collective-permute-start(f32[1,128]{1,0:T(1,128)S(1)} %add.24), channel_id=1, source_target_pairs={{0,6},{1,7},{2,4},{3,5},{4,2},{5,3},{6,0},{7,1},{8,14},{9,15},{10,... | collective-permute-start | bytes 1544 | tf_op jit(solution)/shard_map/ppermute | solution.py:861
  59.2 0.8 %collective-permute-start.16 = (f32[1,128]{1,0:T(1,128)S(1)}, f32[1,128]{1,0:T(1,128)S(1)}, u32[]{:S(2)}, u32[]{:S(2)}) collective-permute-start(f32[1,128]{1,0:T(1,128)S(1)} %add.24), channel_id=1, source_target_pairs={{0,4},{1,5},{2,6},{3,7},{4,0},{5,1},{6,2},{7,3},{8,12},{9,13},{10,... | collective-permute-start | bytes 1544 | tf_op jit(solution)/shard_map/ppermute | solution.py:861
  60.0 0.8 %collective-permute-start.15 = (f32[1,128]{1,0:T(1,128)S(1)}, f32[1,128]{1,0:T(1,128)S(1)}, u32[]{:S(2)}, u32[]{:S(2)}) collective-permute-start(f32[1,128]{1,0:T(1,128)S(1)} %add.24), channel_id=1, source_target_pairs={{0,2},{1,3},{2,0},{3,1},{4,6},{5,7},{6,4},{7,5},{8,10},{9,11},{10,... | collective-permute-start | bytes 1544 | tf_op jit(solution)/shard_map/ppermute | solution.py:861
  60.9 0.9 %collective-permute-done.17 = f32[1,128]{1,0:T(1,128)S(1)} collective-permute-done((f32[1,128]{1,0:T(1,128)S(1)}, f32[1,128]{1,0:T(1,128)S(1)}, u32[]{:S(2)}, u32[]{:S(2)}) %collective-permute-start.17) | collective-permute-done | bytes 544 | tf_op jit(solution)/shard_map/ppermute | solution.py:861
  61.8 0.9 %collective-permute-done.16 = f32[1,128]{1,0:T(1,128)S(1)} collective-permute-done((f32[1,128]{1,0:T(1,128)S(1)}, f32[1,128]{1,0:T(1,128)S(1)}, u32[]{:S(2)}, u32[]{:S(2)}) %collective-permute-start.16) | collective-permute-done | bytes 544 | tf_op jit(solution)/shard_map/ppermute | solution.py:861
  62.7 0.8 %collective-permute-done.15 = f32[1,128]{1,0:T(1,128)S(1)} collective-permute-done((f32[1,128]{1,0:T(1,128)S(1)}, f32[1,128]{1,0:T(1,128)S(1)}, u32[]{:S(2)}, u32[]{:S(2)}) %collective-permute-start.15) | collective-permute-done | bytes 544 | tf_op jit(solution)/shard_map/ppermute | solution.py:861
  63.6 1.7 %collective-permute-start.18 = (f32[1,128]{1,0:T(1,128)S(1)}, f32[1,128]{1,0:T(1,128)S(1)}, u32[]{:S(2)}, u32[]{:S(2)}) collective-permute-start(f32[1,128]{1,0:T(1,128)S(1)} %add_add_fusion), channel_id=1, source_target_pairs={{0,8},{1,9},{2,10},{3,11},{4,12},{5,13},{6,14},{7,15},{8,0},{9,1},... | collective-permute-start | bytes 1544 | tf_op jit(solution)/shard_map/ppermute | solution.py:861
  65.3 0.0 copy-done
  65.3 0.0 copy-done.1
  65.3 1.7 %shard_map.77.places = s32[2,32,128]{2,1,0:T(8,128)S(1)} custom-call(s32[32]{0:T(128)S(1)} %copy-done.1, s32[32,128]{1,0:T(8,128)S(1)} %copy-done), custom_call_target="tpu_custom_call" | custom-call | flops 21626880 | bytes 5767168 | tf_op jit(solution)/shard_map/pallas_call | solution.py:481
  67.1 1.0 %collective-permute-done.18 = f32[1,128]{1,0:T(1,128)S(1)} collective-permute-done((f32[1,128]{1,0:T(1,128)S(1)}, f32[1,128]{1,0:T(1,128)S(1)}, u32[]{:S(2)}, u32[]{:S(2)}) %collective-permute-start.18) | collective-permute-done | bytes 544 | tf_op jit(solution)/shard_map/ppermute | solution.py:861
  68.0 1.1 %shard_map.78 = f32[20,128]{1,0:T(8,128)} custom-call(f32[1,128]{1,0:T(1,128)S(1)} %add.28.moments, f32[4,10,8,128]{3,2,1,0:T(8,128)S(1)} %constant_dynamic-update-slice_fusion.slots, f32[4,10,2,128]{3,2,1,0:T(2,128)S(1)} %constant_dynamic-update-slice_fusion.5.first, f32[4,10,2,128]{3,2,1,0:T(2,128)S(1)} %constant_dynamic-update-slice_fusion.10.second, ...), custom_call_target="tpu_custom_call" | custom-call | tf_op jit(solution)/shard_map/pallas_call | solution.py:849
  (25 shorter events, 0.2 us)
Async XLA Ops:
  1.1 1.4 %collective-permute-start = (f32[4,2,8,128]{3,2,1,0:T(8,128)S(1)}, f32[4,2,8,128]{3,2,1,0:T(8,128)S(1)}, u32[]{:S(2)}, u32[]{:S(2)}) collective-permute-start(f32[4,2,8,128]{3,2,1,0:T(8,128)S(1)} %bitcast.54), channel_id=1, source_target_pairs={{0,1},{1,0},{2,3},{3,2},{4,5},{5,4},{6,7},{7,6},{8,9},{9,8},{10,11... | collective-permute-start | bytes 98312 | tf_op jit(solution)/shard_map/ppermute | solution.py:861
  2.5 17.5 %collective-permute-start.3 = (f32[4,10,8,128]{3,2,1,0:T(8,128)S(1)}, f32[4,10,8,128]{3,2,1,0:T(8,128)S(1)}, u32[]{:S(2)}, u32[]{:S(2)}) collective-permute-start(f32[4,10,8,128]{3,2,1,0:T(8,128)S(1)} %constant_dynamic-update-slice_fusion.slots), channel_id=1, source_target_pairs={{0,2},{1,3},{2,0},{3,1},{4,6},{5,7},{6,4},{7,5},{8,10},{9,11},{10,... | collective-permute-start | bytes 491528 | tf_op jit(solution)/shard_map/ppermute | solution.py:861
  5.5 14.6 %collective-permute-start.2 = (f32[2,10,8,128]{3,2,1,0:T(8,128)S(1)}, f32[2,10,8,128]{3,2,1,0:T(8,128)S(1)}, u32[]{:S(2)}, u32[]{:S(2)}) collective-permute-start(f32[2,10,8,128]{3,2,1,0:T(8,128)S(1)} %get-tuple-element.89), channel_id=1, source_target_pairs={{0,4},{1,5},{2,6},{3,7},{4,0},{5,1},{6,2},{7,3},{8,12},{9,13},{10,... | collective-permute-start | bytes 245768 | tf_op jit(solution)/shard_map/ppermute | solution.py:888
  7.1 12.9 %collective-permute-start.1 = (f32[2,10,8,128]{3,2,1,0:T(8,128)S(1)}, f32[2,10,8,128]{3,2,1,0:T(8,128)S(1)}, u32[]{:S(2)}, u32[]{:S(2)}) collective-permute-start(f32[2,10,8,128]{3,2,1,0:T(8,128)S(1)} %get-tuple-element.90), channel_id=1, source_target_pairs={{0,12},{1,13},{2,14},{3,15},{4,8},{5,9},{6,10},{7,11},{8,4},{9,5},... | collective-permute-start | bytes 245768 | tf_op jit(solution)/shard_map/ppermute | solution.py:887
  20.1 10.4 %collective-permute-start.4 = (f32[4,10,8,128]{3,2,1,0:T(8,128)S(1)}, f32[4,10,8,128]{3,2,1,0:T(8,128)S(1)}, u32[]{:S(2)}, u32[]{:S(2)}) collective-permute-start(f32[4,10,8,128]{3,2,1,0:T(8,128)S(1)} %pad_maximum_fusion), channel_id=1, source_target_pairs={{0,2},{1,3},{2,0},{3,1},{4,6},{5,7},{6,4},{7,5},{8,10},{9,11},{10,... | collective-permute-start | bytes 491528 | tf_op jit(solution)/shard_map/ppermute | solution.py:861
  31.7 3.3 %collective-permute-start.5 = (f32[4,2,2,128]{3,2,1,0:T(2,128)S(1)}, f32[4,2,2,128]{3,2,1,0:T(2,128)S(1)}, u32[]{:S(2)}, u32[]{:S(2)}) collective-permute-start(f32[4,2,2,128]{3,2,1,0:T(2,128)S(1)} %bitcast.60), channel_id=1, source_target_pairs={{0,1},{1,0},{2,3},{3,2},{4,5},{5,4},{6,7},{7,6},{8,9},{9,8},{10,11... | collective-permute-start | bytes 24584 | tf_op jit(solution)/shard_map/ppermute | solution.py:861
  35.1 5.0 %collective-permute-start.7 = (f32[2,10,2,128]{3,2,1,0:T(2,128)S(1)}, f32[2,10,2,128]{3,2,1,0:T(2,128)S(1)}, u32[]{:S(2)}, u32[]{:S(2)}) collective-permute-start(f32[2,10,2,128]{3,2,1,0:T(2,128)S(1)} %get-tuple-element.93), channel_id=1, source_target_pairs={{0,4},{1,5},{2,6},{3,7},{4,0},{5,1},{6,2},{7,3},{8,12},{9,13},{10,... | collective-permute-start | bytes 61448 | tf_op jit(solution)/shard_map/ppermute | solution.py:888
  35.9 5.6 %collective-permute-start.6 = (f32[2,10,2,128]{3,2,1,0:T(2,128)S(1)}, f32[2,10,2,128]{3,2,1,0:T(2,128)S(1)}, u32[]{:S(2)}, u32[]{:S(2)}) collective-permute-start(f32[2,10,2,128]{3,2,1,0:T(2,128)S(1)} %get-tuple-element.94), channel_id=1, source_target_pairs={{0,12},{1,13},{2,14},{3,15},{4,8},{5,9},{6,10},{7,11},{8,4},{9,5},... | collective-permute-start | bytes 61448 | tf_op jit(solution)/shard_map/ppermute | solution.py:887
  36.8 6.3 %collective-permute-start.9 = (f32[4,10,2,128]{3,2,1,0:T(2,128)S(1)}, f32[4,10,2,128]{3,2,1,0:T(2,128)S(1)}, u32[]{:S(2)}, u32[]{:S(2)}) collective-permute-start(f32[4,10,2,128]{3,2,1,0:T(2,128)S(1)} %constant_dynamic-update-slice_fusion.5.first), channel_id=1, source_target_pairs={{0,2},{1,3},{2,0},{3,1},{4,6},{5,7},{6,4},{7,5},{8,10},{9,11},{10,... | collective-permute-start | bytes 122888 | tf_op jit(solution)/shard_map/ppermute | solution.py:861
  41.5 4.1 %collective-permute-start.8 = (f32[4,10,2,128]{3,2,1,0:T(2,128)S(1)}, f32[4,10,2,128]{3,2,1,0:T(2,128)S(1)}, u32[]{:S(2)}, u32[]{:S(2)}) collective-permute-start(f32[4,10,2,128]{3,2,1,0:T(2,128)S(1)} %pad_maximum_fusion.1), channel_id=1, source_target_pairs={{0,2},{1,3},{2,0},{3,1},{4,6},{5,7},{6,4},{7,5},{8,10},{9,11},{10,... | collective-permute-start | bytes 122888 | tf_op jit(solution)/shard_map/ppermute | solution.py:861
  46.3 1.7 %collective-permute-start.10 = (f32[4,2,2,128]{3,2,1,0:T(2,128)S(1)}, f32[4,2,2,128]{3,2,1,0:T(2,128)S(1)}, u32[]{:S(2)}, u32[]{:S(2)}) collective-permute-start(f32[4,2,2,128]{3,2,1,0:T(2,128)S(1)} %bitcast.63), channel_id=1, source_target_pairs={{0,1},{1,0},{2,3},{3,2},{4,5},{5,4},{6,7},{7,6},{8,9},{9,8},{10,11... | collective-permute-start | bytes 24584 | tf_op jit(solution)/shard_map/ppermute | solution.py:861
  48.1 6.0 %collective-permute-start.13 = (f32[4,10,2,128]{3,2,1,0:T(2,128)S(1)}, f32[4,10,2,128]{3,2,1,0:T(2,128)S(1)}, u32[]{:S(2)}, u32[]{:S(2)}) collective-permute-start(f32[4,10,2,128]{3,2,1,0:T(2,128)S(1)} %constant_dynamic-update-slice_fusion.10.second), channel_id=1, source_target_pairs={{0,2},{1,3},{2,0},{3,1},{4,6},{5,7},{6,4},{7,5},{8,10},{9,11},{10,... | collective-permute-start | bytes 122888 | tf_op jit(solution)/shard_map/ppermute | solution.py:861
  49.6 4.4 %collective-permute-start.12 = (f32[2,10,2,128]{3,2,1,0:T(2,128)S(1)}, f32[2,10,2,128]{3,2,1,0:T(2,128)S(1)}, u32[]{:S(2)}, u32[]{:S(2)}) collective-permute-start(f32[2,10,2,128]{3,2,1,0:T(2,128)S(1)} %slice.89), channel_id=1, source_target_pairs={{0,12},{1,13},{2,14},{3,15},{4,0},{5,1},{6,2},{7,3},{8,4},{9,5},{1... | collective-permute-start | bytes 61448 | tf_op jit(solution)/shard_map/ppermute | solution.py:867
  50.5 4.7 %collective-permute-start.11 = (f32[2,10,2,128]{3,2,1,0:T(2,128)S(1)}, f32[2,10,2,128]{3,2,1,0:T(2,128)S(1)}, u32[]{:S(2)}, u32[]{:S(2)}) collective-permute-start(f32[2,10,2,128]{3,2,1,0:T(2,128)S(1)} %slice.89), channel_id=1, source_target_pairs={{0,14},{1,15},{2,12},{3,13},{4,2},{5,3},{6,0},{7,1},{8,6},{9,7},{1... | collective-permute-start | bytes 61448 | tf_op jit(solution)/shard_map/ppermute | solution.py:867
  55.2 10.1 %copy-start = (s32[32,128]{1,0:T(8,128)S(1)}, s32[32,128]{1,0:T(8,128)}, u32[]{:S(2)}) copy-start(s32[32,128]{1,0:T(8,128)} %atoms) | copy-start | bytes 49156
  55.2 10.1 %copy-start.1 = (s32[32]{0:T(128)S(1)}, s32[32]{0:T(128)}, u32[]{:S(2)}) copy-start(s32[32]{0:T(128)} %counts) | copy-start | bytes 388
  56.3 1.1 %collective-permute-start.14 = (f32[1,128]{1,0:T(1,128)S(1)}, f32[1,128]{1,0:T(1,128)S(1)}, u32[]{:S(2)}, u32[]{:S(2)}) collective-permute-start(f32[1,128]{1,0:T(1,128)S(1)} %shard_map.76), channel_id=1, source_target_pairs={{0,1},{1,0},{2,3},{3,2},{4,5},{5,4},{6,7},{7,6},{8,9},{9,8},{10,11... | collective-permute-start | bytes 1544 | tf_op jit(solution)/shard_map/ppermute | solution.py:861
  57.4 4.4 %collective-permute-start.17 = (f32[1,128]{1,0:T(1,128)S(1)}, f32[1,128]{1,0:T(1,128)S(1)}, u32[]{:S(2)}, u32[]{:S(2)}) collective-permute-start(f32[1,128]{1,0:T(1,128)S(1)} %add.24), channel_id=1, source_target_pairs={{0,6},{1,7},{2,4},{3,5},{4,2},{5,3},{6,0},{7,1},{8,14},{9,15},{10,... | collective-permute-start | bytes 1544 | tf_op jit(solution)/shard_map/ppermute | solution.py:861
  59.2 3.5 %collective-permute-start.16 = (f32[1,128]{1,0:T(1,128)S(1)}, f32[1,128]{1,0:T(1,128)S(1)}, u32[]{:S(2)}, u32[]{:S(2)}) collective-permute-start(f32[1,128]{1,0:T(1,128)S(1)} %add.24), channel_id=1, source_target_pairs={{0,4},{1,5},{2,6},{3,7},{4,0},{5,1},{6,2},{7,3},{8,12},{9,13},{10,... | collective-permute-start | bytes 1544 | tf_op jit(solution)/shard_map/ppermute | solution.py:861
  60.0 3.5 %collective-permute-start.15 = (f32[1,128]{1,0:T(1,128)S(1)}, f32[1,128]{1,0:T(1,128)S(1)}, u32[]{:S(2)}, u32[]{:S(2)}) collective-permute-start(f32[1,128]{1,0:T(1,128)S(1)} %add.24), channel_id=1, source_target_pairs={{0,2},{1,3},{2,0},{3,1},{4,6},{5,7},{6,4},{7,5},{8,10},{9,11},{10,... | collective-permute-start | bytes 1544 | tf_op jit(solution)/shard_map/ppermute | solution.py:861
  63.6 4.4 %collective-permute-start.18 = (f32[1,128]{1,0:T(1,128)S(1)}, f32[1,128]{1,0:T(1,128)S(1)}, u32[]{:S(2)}, u32[]{:S(2)}) collective-permute-start(f32[1,128]{1,0:T(1,128)S(1)} %add_add_fusion), channel_id=1, source_target_pairs={{0,8},{1,9},{2,10},{3,11},{4,12},{5,13},{6,14},{7,15},{8,0},{9,1},... | collective-permute-start | bytes 1544 | tf_op jit(solution)/shard_map/ppermute | solution.py:861

commit v3 on v2

--- a/solution.py
+++ b/solution.py
@@ -421,7 +421,7 @@
         build_cell(cell, cell, lines, turned, kernels, None, sums, below)
         return 0
 
-    lax.fori_loop(0, CELLS, one_cell, 0, unroll=2)
+    lax.fori_loop(0, CELLS, one_cell, 0, unroll=4)
 
 
 def face_kernel(
@@ -436,7 +436,7 @@
         build_cell(cell, cell, lines, turned, kernels, before, sums, None)
         return 0
 
-    lax.fori_loop(0, CELLS, one_cell, 0, unroll=2)
+    lax.fori_loop(0, CELLS, one_cell, 0, unroll=4)
 
 
 def corner_kernel(
@@ -552,7 +552,7 @@
         apply_cell(cell, cell, lines, stored, None, sums)
         return 0
 
-    lax.fori_loop(0, CELLS, one_cell, 0, unroll=4)
+    lax.fori_loop(0, CELLS, one_cell, 0, unroll=8)
 
 
 def apply_face_kernel(*refs):
@@ -568,7 +568,7 @@
         apply_cell(cell, cell, lines, stored, before, sums)
         return 0
 
-    lax.fori_loop(0, CELLS, one_cell, 0, unroll=4)
+    lax.fori_loop(0, CELLS, one_cell, 0, unroll=8)
 
 
 def apply_corner_cells(stored, before, spill_before, core, out, packed, spills, rest, sums):
@@ -638,7 +638,7 @@
             apply_cell(cell, cell, lines_of(packed, columns, z), stored, before, sums, first)
             return 0
 
-        lax.fori_loop(0, CZ, one_cell, 0, unroll=4)
+        lax.fori_loop(0, CZ, one_cell, 0, unroll=8)
 
 
 def apply_corner_kernel(

time: 69.3 us -> 69 us (level)
  no operation moved by 1% of the time
where the time goes in v3:
time: 69 us; the launch traced here: 68.8 us
  Pallas kernels  39.9 us (58%)
  starting transfers between devices  21.9 us (32%)
  waiting for transfers between devices  6.51 us (9%)
    pallas_call x12, Pallas kernels, call(): pl.pallas_call(kernel, out_shape=outs, in_specs=[IN_SMEM if array.ndim ==...  37 us
    ppermute x13, starting transfers between devices, partner(): lax.ppermute(block, axis, [(low, low ^ mask) for low in range(count)])  14.2 us
    ppermute x13, waiting for transfers between devices, partner(): lax.ppermute(block, axis, [(low, low ^ mask) for low in range(count)])  5.1 us
    ppermute x2, starting transfers between devices, x_faces(): second = lax.ppermute(jnp.where(odd, core[2:], core[:2]), 'gx', route)  3.38 us
    ppermute x2, starting transfers between devices, x_faces(): lax.ppermute(jnp.where(odd, core[:2], core[2:]), 'gx', [(i, i ^ 4) for i...  2.38 us
    ppermute x2, starting transfers between devices, shifted(): return lax.ppermute(block, 'gx', route)  1.96 us
  transfers between devices with their start and end apart: 19, of which 8 were waited for; matrix products, arithmetic and copies ran while one was open for 0% of the time, Pallas kernels for 51%

profile of v3, /device:TPU:0, one launch (start us, length us, event | category | flops | bytes accessed | tf_op | source)
XLA Modules:
  0.0 68.8 jit_solution(14281118286997703006)
XLA Ops:
  0.0 1.1 %shard_map.64 = (f32[8,8,128]{2,1,0:T(8,128)S(1)}, s32[32,128]{1,0:T(8,128)S(1)}, s32[32,128]{1,0:T(8,128)S(1)}, f32[20,8,128]{2,1,0:T(8,128)S(1)}, f32[20,8,128]{2,1,0:T(8,128)S(1)}) custom-call(s32[32]{0:T(128)} %counts, f32[3,2560]{1,0:T(4,128)} %offsets.1, f32[20,128]{1,0:T(8,128)} %bitcast.66, f32[20,128]{1,0:T(8,128)} %bitcast.67, f32[20,128]{1,0:T(8,128)} %bitcast.68, ...), custom_call_target="tpu_custom_call" | custom-call | tf_op jit(solution)/shard_map/pallas_call | solution.py:153
  1.1 0.5 collective-permute-start
  1.6 0.7 %shard_map.65 = f32[24,8,128]{2,1,0:T(8,128)S(1)} custom-call(s32[32,128]{1,0:T(8,128)S(1)} %get-tuple-element.47.counted, s32[32,128]{1,0:T(8,128)S(1)} %get-tuple-element.48.atoms, f32[20,8,128]{2,1,0:T(8,128)S(1)} %get-tuple-element.49.table, f32[20,8,128]{2,1,0:T(8,128)S(1)} %get-tuple-element.50.others), custom_call_target="tpu_custom_call" | custom-call | flops 1048576 | bytes 4194304 | tf_op jit(solution)/shard_map/pallas_call | solution.py:186
  2.4 0.1 collective-permute-done
  2.5 2.9 %collective-permute-start.3 = (f32[4,10,8,128]{3,2,1,0:T(8,128)S(1)}, f32[4,10,8,128]{3,2,1,0:T(8,128)S(1)}, u32[]{:S(2)}, u32[]{:S(2)}) collective-permute-start(f32[4,10,8,128]{3,2,1,0:T(8,128)S(1)} %constant_dynamic-update-slice_fusion.slots), channel_id=1, source_target_pairs={{0,2},{1,3},{2,0},{3,1},{4,6},{5,7},{6,4},{7,5},{8,10},{9,11},{10,... | collective-permute-start | bytes 491528 | tf_op jit(solution)/shard_map/ppermute | solution.py:861
  5.5 1.6 %collective-permute-start.2 = (f32[2,10,8,128]{3,2,1,0:T(8,128)S(1)}, f32[2,10,8,128]{3,2,1,0:T(8,128)S(1)}, u32[]{:S(2)}, u32[]{:S(2)}) collective-permute-start(f32[2,10,8,128]{3,2,1,0:T(8,128)S(1)} %get-tuple-element.89), channel_id=1, source_target_pairs={{0,4},{1,5},{2,6},{3,7},{4,0},{5,1},{6,2},{7,3},{8,12},{9,13},{10,... | collective-permute-start | bytes 245768 | tf_op jit(solution)/shard_map/ppermute | solution.py:888
  7.1 2.5 %collective-permute-start.1 = (f32[2,10,8,128]{3,2,1,0:T(8,128)S(1)}, f32[2,10,8,128]{3,2,1,0:T(8,128)S(1)}, u32[]{:S(2)}, u32[]{:S(2)}) collective-permute-start(f32[2,10,8,128]{3,2,1,0:T(8,128)S(1)} %get-tuple-element.90), channel_id=1, source_target_pairs={{0,12},{1,13},{2,14},{3,15},{4,8},{5,9},{6,10},{7,11},{8,4},{9,5},... | collective-permute-start | bytes 245768 | tf_op jit(solution)/shard_map/ppermute | solution.py:887
  9.6 10.3 %shard_map.66 = (f32[32,11,8,8,128]{4,3,2,1,0:T(8,128)S(1)}, f32[32,11,2,8,128]{4,3,2,1,0:T(8,128)S(1)}, f32[8,8,128]{2,1,0:T(8,128)S(1)}, f32[32,11,4,8,128]{4,3,2,1,0:T(8,128)S(1)}) custom-call(f32[40,8,128]{2,1,0:T(8,128)S(1)} %bitcast.24), custom_call_target="tpu_custom_call" | custom-call | flops 86507520 | bytes 23068672 | tf_op jit(solution)/shard_map/pallas_call | solution.py:481
  19.9 0.0 collective-permute-done.2
  19.9 0.0 collective-permute-done.1
  19.9 0.0 collective-permute-done.3
  20.0 0.6 collective-permute-start.4
  20.6 9.7 %shard_map.67 = (f32[32,11,8,8,128]{4,3,2,1,0:T(8,128)S(1)}, f32[32,11,2,8,128]{4,3,2,1,0:T(8,128)S(1)}, f32[32,8,128]{2,1,0:T(8,128)S(1)}) custom-call(f32[20,8,128]{2,1,0:T(8,128)S(1)} %bitcast.39, f32[20,8,128]{2,1,0:T(8,128)S(1)} %bitcast.36, f32[40,8,128]{2,1,0:T(8,128)S(1)} %bitcast.42, f32[32,11,4,8,128]{4,3,2,1,0:T(8,128)S(1)} %get-tuple-element.54.turned, ...), custom_call_target="tpu_custom_call" | custom-call | flops 86507520 | bytes 23068672 | tf_op jit(solution)/shard_map/pallas_call | solution.py:481
  30.2 0.0 collective-permute-done.4
  30.2 1.2 %shard_map.68 = (f32[8,11,3,8,128]{4,3,2,1,0:T(8,128)S(1)}, f32[8,2,128]{2,1,0:T(2,128)S(1)}) custom-call(f32[40,8,128]{2,1,0:T(8,128)S(1)} %bitcast.31, f32[32,11,4,8,128]{4,3,2,1,0:T(8,128)S(1)} %get-tuple-element.54.turned, f32[32,11,2,8,128]{4,3,2,1,0:T(8,128)S(1)} %get-tuple-element.58.before, f32[32,8,128]{2,1,0:T(8,128)S(1)} %get-tuple-element.59.spill_before, ...), custom_call_target="tpu_custom_call" | custom-call | flops 32440320 | bytes 8650752 | tf_op jit(solution)/shard_map/pallas_call | solution.py:481
  31.5 0.1 collective-permute-start.5
  31.5 3.2 %shard_map.69 = (f32[24,11,3,8,128]{4,3,2,1,0:T(8,128)S(1)}, f32[24,2,128]{2,1,0:T(2,128)S(1)}) custom-call(f32[40,8,128]{2,1,0:T(8,128)S(1)} %bitcast.32, f32[32,11,4,8,128]{4,3,2,1,0:T(8,128)S(1)} %get-tuple-element.54.turned, f32[32,11,2,8,128]{4,3,2,1,0:T(8,128)S(1)} %get-tuple-element.58.before, f32[32,8,128]{2,1,0:T(8,128)S(1)} %get-tuple-element.59.spill_before, ...), custom_call_target="tpu_custom_call" | custom-call | flops 32440320 | bytes 8650752 | tf_op jit(solution)/shard_map/pallas_call | solution.py:481
  34.8 0.0 collective-permute-done.5
  34.9 0.7 %collective-permute-start.7 = (f32[2,10,2,128]{3,2,1,0:T(2,128)S(1)}, f32[2,10,2,128]{3,2,1,0:T(2,128)S(1)}, u32[]{:S(2)}, u32[]{:S(2)}) collective-permute-start(f32[2,10,2,128]{3,2,1,0:T(2,128)S(1)} %get-tuple-element.93), channel_id=1, source_target_pairs={{0,4},{1,5},{2,6},{3,7},{4,0},{5,1},{6,2},{7,3},{8,12},{9,13},{10,... | collective-permute-start | bytes 61448 | tf_op jit(solution)/shard_map/ppermute | solution.py:888
  35.6 0.9 %collective-permute-start.6 = (f32[2,10,2,128]{3,2,1,0:T(2,128)S(1)}, f32[2,10,2,128]{3,2,1,0:T(2,128)S(1)}, u32[]{:S(2)}, u32[]{:S(2)}) collective-permute-start(f32[2,10,2,128]{3,2,1,0:T(2,128)S(1)} %get-tuple-element.94), channel_id=1, source_target_pairs={{0,12},{1,13},{2,14},{3,15},{4,8},{5,9},{6,10},{7,11},{8,4},{9,5},... | collective-permute-start | bytes 61448 | tf_op jit(solution)/shard_map/ppermute | solution.py:887
  36.5 1.5 %collective-permute-start.9 = (f32[4,10,2,128]{3,2,1,0:T(2,128)S(1)}, f32[4,10,2,128]{3,2,1,0:T(2,128)S(1)}, u32[]{:S(2)}, u32[]{:S(2)}) collective-permute-start(f32[4,10,2,128]{3,2,1,0:T(2,128)S(1)} %constant_dynamic-update-slice_fusion.5.first), channel_id=1, source_target_pairs={{0,2},{1,3},{2,0},{3,1},{4,6},{5,7},{6,4},{7,5},{8,10},{9,11},{10,... | collective-permute-start | bytes 122888 | tf_op jit(solution)/shard_map/ppermute | solution.py:861
  38.0 1.8 %shard_map.70 = (f32[32,11,2,8,128]{4,3,2,1,0:T(8,128)S(1)}, f32[8,8,128]{2,1,0:T(8,128)S(1)}) custom-call(f32[40,8,128]{2,1,0:T(8,128)S(1)} %bitcast.27, f32[40,2,128]{2,1,0:T(2,128)S(1)} %bitcast.41, f32[32,11,8,8,128]{4,3,2,1,0:T(8,128)S(1)} %get-tuple-element.62.stored), custom_call_target="tpu_custom_call" | custom-call | flops 21626880 | bytes 5767168 | tf_op jit(solution)/shard_map/pallas_call | solution.py:481
  39.8 0.0 collective-permute-done.7
  39.8 1.4 %collective-permute-done.6 = f32[2,10,2,128]{3,2,1,0:T(2,128)S(1)} collective-permute-done((f32[2,10,2,128]{3,2,1,0:T(2,128)S(1)}, f32[2,10,2,128]{3,2,1,0:T(2,128)S(1)}, u32[]{:S(2)}, u32[]{:S(2)}) %collective-permute-start.6) | collective-permute-done | bytes 20512 | tf_op jit(solution)/shard_map/ppermute | solution.py:887
  41.2 1.6 %collective-permute-start.8 = (f32[4,10,2,128]{3,2,1,0:T(2,128)S(1)}, f32[4,10,2,128]{3,2,1,0:T(2,128)S(1)}, u32[]{:S(2)}, u32[]{:S(2)}) collective-permute-start(f32[4,10,2,128]{3,2,1,0:T(2,128)S(1)} %pad_maximum_fusion.1), channel_id=1, source_target_pairs={{0,2},{1,3},{2,0},{3,1},{4,6},{5,7},{6,4},{7,5},{8,10},{9,11},{10,... | collective-permute-start | bytes 122888 | tf_op jit(solution)/shard_map/ppermute | solution.py:861
  42.8 0.0 collective-permute-done.9
  42.8 2.2 %shard_map.71 = (f32[32,11,2,8,128]{4,3,2,1,0:T(8,128)S(1)}, f32[32,8,128]{2,1,0:T(8,128)S(1)}) custom-call(f32[20,8,128]{2,1,0:T(8,128)S(1)} %bitcast.40, f32[20,8,128]{2,1,0:T(8,128)S(1)} %bitcast.37, f32[40,8,128]{2,1,0:T(8,128)S(1)} %bitcast.43, f32[20,2,128]{2,1,0:T(2,128)S(1)} %bitcast.47, f32[20,2,128]{2,1,0:T(2,128)S(1)} %bitcast.48, ...), custom_call_target="tpu_custom_call" | custom-call | flops 21626880 | bytes 5767168 | tf_op jit(solution)/shard_map/pallas_call | solution.py:481
  45.1 0.3 collective-permute-done.8
  45.3 0.7 shard_map.72
  46.0 0.1 collective-permute-start.10
  46.1 1.6 %shard_map.73 = f32[24,2,128]{2,1,0:T(2,128)S(1)} custom-call(f32[40,8,128]{2,1,0:T(8,128)S(1)} %bitcast.34, f32[40,2,128]{2,1,0:T(2,128)S(1)} %bitcast.52, f32[24,11,3,8,128]{4,3,2,1,0:T(8,128)S(1)} %get-tuple-element.72.stored.inner, f32[32,11,2,8,128]{4,3,2,1,0:T(8,128)S(1)} %get-tuple-element.70.before, ...), custom_call_target="tpu_custom_call" | custom-call | flops 21626880 | bytes 5767168 | tf_op jit(solution)/shard_map/pallas_call | solution.py:481
  47.7 0.0 collective-permute-done.10
  47.8 1.6 %collective-permute-start.13 = (f32[4,10,2,128]{3,2,1,0:T(2,128)S(1)}, f32[4,10,2,128]{3,2,1,0:T(2,128)S(1)}, u32[]{:S(2)}, u32[]{:S(2)}) collective-permute-start(f32[4,10,2,128]{3,2,1,0:T(2,128)S(1)} %constant_dynamic-update-slice_fusion.10.second), channel_id=1, source_target_pairs={{0,2},{1,3},{2,0},{3,1},{4,6},{5,7},{6,4},{7,5},{8,10},{9,11},{10,... | collective-permute-start | bytes 122888 | tf_op jit(solution)/shard_map/ppermute | solution.py:861
  49.4 0.9 %collective-permute-start.12 = (f32[2,10,2,128]{3,2,1,0:T(2,128)S(1)}, f32[2,10,2,128]{3,2,1,0:T(2,128)S(1)}, u32[]{:S(2)}, u32[]{:S(2)}) collective-permute-start(f32[2,10,2,128]{3,2,1,0:T(2,128)S(1)} %slice.89), channel_id=1, source_target_pairs={{0,12},{1,13},{2,14},{3,15},{4,0},{5,1},{6,2},{7,3},{8,4},{9,5},{1... | collective-permute-start | bytes 61448 | tf_op jit(solution)/shard_map/ppermute | solution.py:867
  50.3 1.1 %collective-permute-start.11 = (f32[2,10,2,128]{3,2,1,0:T(2,128)S(1)}, f32[2,10,2,128]{3,2,1,0:T(2,128)S(1)}, u32[]{:S(2)}, u32[]{:S(2)}) collective-permute-start(f32[2,10,2,128]{3,2,1,0:T(2,128)S(1)} %slice.89), channel_id=1, source_target_pairs={{0,14},{1,15},{2,12},{3,13},{4,2},{5,3},{6,0},{7,1},{8,6},{9,7},{1... | collective-permute-start | bytes 61448 | tf_op jit(solution)/shard_map/ppermute | solution.py:867
  51.3 2.4 %shard_map.74 = (f32[32,11,2,8,128]{4,3,2,1,0:T(8,128)S(1)}, f32[8,8,128]{2,1,0:T(8,128)S(1)}, f32[32,11,2,8,128]{4,3,2,1,0:T(8,128)S(1)}, f32[2,128]{1,0:T(2,128)S(1)}) custom-call(f32[40,8,128]{2,1,0:T(8,128)S(1)} %bitcast.30, f32[40,2,128]{2,1,0:T(2,128)S(1)} %bitcast.45, f32[32,11,8,8,128]{4,3,2,1,0:T(8,128)S(1)} %get-tuple-element.62.stored, ...), custom_call_target="tpu_custom_call" | custom-call | flops 21626880 | bytes 5767168 | tf_op jit(solution)/shard_map/pallas_call | solution.py:481
  53.7 0.0 collective-permute-done.12
  53.7 0.0 collective-permute-done.13
  53.7 1.2 %shard_map.75 = (f32[32,11,2,8,128]{4,3,2,1,0:T(8,128)S(1)}, f32[32,8,128]{2,1,0:T(8,128)S(1)}) custom-call(f32[20,8,128]{2,1,0:T(8,128)S(1)} %bitcast.38, f32[40,8,128]{2,1,0:T(8,128)S(1)} %bitcast.44, f32[20,2,128]{2,1,0:T(2,128)S(1)} %bitcast.59, f32[40,2,128]{2,1,0:T(2,128)S(1)} %bitcast.53, f32[32,11,8,8,128]{4,3,2,1,0:T(8,128)S(1)} %get-tuple-element.67.refs_6_.stored, ...), custom_call_target="tpu_custom_call" | custom-call | flops 21626880 | bytes 5767168 | tf_op jit(solution)/shard_map/pallas_call | solution.py:481
  54.9 0.0 collective-permute-done.11
  55.0 0.0 copy-start
  55.0 0.0 copy-start.1
  55.0 1.0 %shard_map.76 = f32[1,128]{1,0:T(1,128)S(1)} custom-call(f32[40,8,128]{2,1,0:T(8,128)S(1)} %bitcast.35, f32[20,2,128]{2,1,0:T(2,128)S(1)} %bitcast.58, f32[8,11,3,8,128]{4,3,2,1,0:T(8,128)S(1)} %get-tuple-element.66.stored.edge, f32[24,11,3,8,128]{4,3,2,1,0:T(8,128)S(1)} %get-tuple-element.72.stored.inner, ...), custom_call_target="tpu_custom_call" | custom-call | flops 21626880 | bytes 5767168 | tf_op jit(solution)/shard_map/pallas_call | solution.py:481
  56.0 0.0 collective-permute-start.14
  56.0 1.1 %collective-permute-done.14 = f32[1,128]{1,0:T(1,128)S(1)} collective-permute-done((f32[1,128]{1,0:T(1,128)S(1)}, f32[1,128]{1,0:T(1,128)S(1)}, u32[]{:S(2)}, u32[]{:S(2)}) %collective-permute-start.14) | collective-permute-done | bytes 544 | tf_op jit(solution)/shard_map/ppermute | solution.py:861
  57.1 1.9 %collective-permute-start.17 = (f32[1,128]{1,0:T(1,128)S(1)}, f32[1,128]{1,0:T(1,128)S(1)}, u32[]{:S(2)}, u32[]{:S(2)}) collective-permute-start(f32[1,128]{1,0:T(1,128)S(1)} %add.24), channel_id=1, source_target_pairs={{0,6},{1,7},{2,4},{3,5},{4,2},{5,3},{6,0},{7,1},{8,14},{9,15},{10,... | collective-permute-start | bytes 1544 | tf_op jit(solution)/shard_map/ppermute | solution.py:861
  59.0 0.8 %collective-permute-start.16 = (f32[1,128]{1,0:T(1,128)S(1)}, f32[1,128]{1,0:T(1,128)S(1)}, u32[]{:S(2)}, u32[]{:S(2)}) collective-permute-start(f32[1,128]{1,0:T(1,128)S(1)} %add.24), channel_id=1, source_target_pairs={{0,4},{1,5},{2,6},{3,7},{4,0},{5,1},{6,2},{7,3},{8,12},{9,13},{10,... | collective-permute-start | bytes 1544 | tf_op jit(solution)/shard_map/ppermute | solution.py:861
  59.7 0.9 %collective-permute-start.15 = (f32[1,128]{1,0:T(1,128)S(1)}, f32[1,128]{1,0:T(1,128)S(1)}, u32[]{:S(2)}, u32[]{:S(2)}) collective-permute-start(f32[1,128]{1,0:T(1,128)S(1)} %add.24), channel_id=1, source_target_pairs={{0,2},{1,3},{2,0},{3,1},{4,6},{5,7},{6,4},{7,5},{8,10},{9,11},{10,... | collective-permute-start | bytes 1544 | tf_op jit(solution)/shard_map/ppermute | solution.py:861
  60.6 0.9 %collective-permute-done.17 = f32[1,128]{1,0:T(1,128)S(1)} collective-permute-done((f32[1,128]{1,0:T(1,128)S(1)}, f32[1,128]{1,0:T(1,128)S(1)}, u32[]{:S(2)}, u32[]{:S(2)}) %collective-permute-start.17) | collective-permute-done | bytes 544 | tf_op jit(solution)/shard_map/ppermute | solution.py:861
  61.5 1.0 %collective-permute-done.16 = f32[1,128]{1,0:T(1,128)S(1)} collective-permute-done((f32[1,128]{1,0:T(1,128)S(1)}, f32[1,128]{1,0:T(1,128)S(1)}, u32[]{:S(2)}, u32[]{:S(2)}) %collective-permute-start.16) | collective-permute-done | bytes 544 | tf_op jit(solution)/shard_map/ppermute | solution.py:861
  62.5 0.8 %collective-permute-done.15 = f32[1,128]{1,0:T(1,128)S(1)} collective-permute-done((f32[1,128]{1,0:T(1,128)S(1)}, f32[1,128]{1,0:T(1,128)S(1)}, u32[]{:S(2)}, u32[]{:S(2)}) %collective-permute-start.15) | collective-permute-done | bytes 544 | tf_op jit(solution)/shard_map/ppermute | solution.py:861
  63.3 1.8 %collective-permute-start.18 = (f32[1,128]{1,0:T(1,128)S(1)}, f32[1,128]{1,0:T(1,128)S(1)}, u32[]{:S(2)}, u32[]{:S(2)}) collective-permute-start(f32[1,128]{1,0:T(1,128)S(1)} %add_add_fusion), channel_id=1, source_target_pairs={{0,8},{1,9},{2,10},{3,11},{4,12},{5,13},{6,14},{7,15},{8,0},{9,1},... | collective-permute-start | bytes 1544 | tf_op jit(solution)/shard_map/ppermute | solution.py:861
  65.1 0.0 copy-done
  65.1 0.0 copy-done.1
  65.1 1.7 %shard_map.77.places = s32[2,32,128]{2,1,0:T(8,128)S(1)} custom-call(s32[32]{0:T(128)S(1)} %copy-done.1, s32[32,128]{1,0:T(8,128)S(1)} %copy-done), custom_call_target="tpu_custom_call" | custom-call | flops 21626880 | bytes 5767168 | tf_op jit(solution)/shard_map/pallas_call | solution.py:481
  66.8 0.9 %collective-permute-done.18 = f32[1,128]{1,0:T(1,128)S(1)} collective-permute-done((f32[1,128]{1,0:T(1,128)S(1)}, f32[1,128]{1,0:T(1,128)S(1)}, u32[]{:S(2)}, u32[]{:S(2)}) %collective-permute-start.18) | collective-permute-done | bytes 544 | tf_op jit(solution)/shard_map/ppermute | solution.py:861
  67.7 1.1 %shard_map.78 = f32[20,128]{1,0:T(8,128)} custom-call(f32[1,128]{1,0:T(1,128)S(1)} %add.28.moments, f32[4,10,8,128]{3,2,1,0:T(8,128)S(1)} %constant_dynamic-update-slice_fusion.slots, f32[4,10,2,128]{3,2,1,0:T(2,128)S(1)} %constant_dynamic-update-slice_fusion.5.first, f32[4,10,2,128]{3,2,1,0:T(2,128)S(1)} %constant_dynamic-update-slice_fusion.10.second, ...), custom_call_target="tpu_custom_call" | custom-call | tf_op jit(solution)/shard_map/pallas_call | solution.py:849
  (25 shorter events, 0.2 us)
Async XLA Ops:
  1.1 1.4 %collective-permute-start = (f32[4,2,8,128]{3,2,1,0:T(8,128)S(1)}, f32[4,2,8,128]{3,2,1,0:T(8,128)S(1)}, u32[]{:S(2)}, u32[]{:S(2)}) collective-permute-start(f32[4,2,8,128]{3,2,1,0:T(8,128)S(1)} %bitcast.54), channel_id=1, source_target_pairs={{0,1},{1,0},{2,3},{3,2},{4,5},{5,4},{6,7},{7,6},{8,9},{9,8},{10,11... | collective-permute-start | bytes 98312 | tf_op jit(solution)/shard_map/ppermute | solution.py:861
  2.5 17.4 %collective-permute-start.3 = (f32[4,10,8,128]{3,2,1,0:T(8,128)S(1)}, f32[4,10,8,128]{3,2,1,0:T(8,128)S(1)}, u32[]{:S(2)}, u32[]{:S(2)}) collective-permute-start(f32[4,10,8,128]{3,2,1,0:T(8,128)S(1)} %constant_dynamic-update-slice_fusion.slots), channel_id=1, source_target_pairs={{0,2},{1,3},{2,0},{3,1},{4,6},{5,7},{6,4},{7,5},{8,10},{9,11},{10,... | collective-permute-start | bytes 491528 | tf_op jit(solution)/shard_map/ppermute | solution.py:861
  5.5 14.4 %collective-permute-start.2 = (f32[2,10,8,128]{3,2,1,0:T(8,128)S(1)}, f32[2,10,8,128]{3,2,1,0:T(8,128)S(1)}, u32[]{:S(2)}, u32[]{:S(2)}) collective-permute-start(f32[2,10,8,128]{3,2,1,0:T(8,128)S(1)} %get-tuple-element.89), channel_id=1, source_target_pairs={{0,4},{1,5},{2,6},{3,7},{4,0},{5,1},{6,2},{7,3},{8,12},{9,13},{10,... | collective-permute-start | bytes 245768 | tf_op jit(solution)/shard_map/ppermute | solution.py:888
  7.1 12.8 %collective-permute-start.1 = (f32[2,10,8,128]{3,2,1,0:T(8,128)S(1)}, f32[2,10,8,128]{3,2,1,0:T(8,128)S(1)}, u32[]{:S(2)}, u32[]{:S(2)}) collective-permute-start(f32[2,10,8,128]{3,2,1,0:T(8,128)S(1)} %get-tuple-element.90), channel_id=1, source_target_pairs={{0,12},{1,13},{2,14},{3,15},{4,8},{5,9},{6,10},{7,11},{8,4},{9,5},... | collective-permute-start | bytes 245768 | tf_op jit(solution)/shard_map/ppermute | solution.py:887
  20.0 10.2 %collective-permute-start.4 = (f32[4,10,8,128]{3,2,1,0:T(8,128)S(1)}, f32[4,10,8,128]{3,2,1,0:T(8,128)S(1)}, u32[]{:S(2)}, u32[]{:S(2)}) collective-permute-start(f32[4,10,8,128]{3,2,1,0:T(8,128)S(1)} %pad_maximum_fusion), channel_id=1, source_target_pairs={{0,2},{1,3},{2,0},{3,1},{4,6},{5,7},{6,4},{7,5},{8,10},{9,11},{10,... | collective-permute-start | bytes 491528 | tf_op jit(solution)/shard_map/ppermute | solution.py:861
  31.5 3.3 %collective-permute-start.5 = (f32[4,2,2,128]{3,2,1,0:T(2,128)S(1)}, f32[4,2,2,128]{3,2,1,0:T(2,128)S(1)}, u32[]{:S(2)}, u32[]{:S(2)}) collective-permute-start(f32[4,2,2,128]{3,2,1,0:T(2,128)S(1)} %bitcast.60), channel_id=1, source_target_pairs={{0,1},{1,0},{2,3},{3,2},{4,5},{5,4},{6,7},{7,6},{8,9},{9,8},{10,11... | collective-permute-start | bytes 24584 | tf_op jit(solution)/shard_map/ppermute | solution.py:861
  34.9 4.9 %collective-permute-start.7 = (f32[2,10,2,128]{3,2,1,0:T(2,128)S(1)}, f32[2,10,2,128]{3,2,1,0:T(2,128)S(1)}, u32[]{:S(2)}, u32[]{:S(2)}) collective-permute-start(f32[2,10,2,128]{3,2,1,0:T(2,128)S(1)} %get-tuple-element.93), channel_id=1, source_target_pairs={{0,4},{1,5},{2,6},{3,7},{4,0},{5,1},{6,2},{7,3},{8,12},{9,13},{10,... | collective-permute-start | bytes 61448 | tf_op jit(solution)/shard_map/ppermute | solution.py:888
  35.6 5.6 %collective-permute-start.6 = (f32[2,10,2,128]{3,2,1,0:T(2,128)S(1)}, f32[2,10,2,128]{3,2,1,0:T(2,128)S(1)}, u32[]{:S(2)}, u32[]{:S(2)}) collective-permute-start(f32[2,10,2,128]{3,2,1,0:T(2,128)S(1)} %get-tuple-element.94), channel_id=1, source_target_pairs={{0,12},{1,13},{2,14},{3,15},{4,8},{5,9},{6,10},{7,11},{8,4},{9,5},... | collective-permute-start | bytes 61448 | tf_op jit(solution)/shard_map/ppermute | solution.py:887
  36.5 6.3 %collective-permute-start.9 = (f32[4,10,2,128]{3,2,1,0:T(2,128)S(1)}, f32[4,10,2,128]{3,2,1,0:T(2,128)S(1)}, u32[]{:S(2)}, u32[]{:S(2)}) collective-permute-start(f32[4,10,2,128]{3,2,1,0:T(2,128)S(1)} %constant_dynamic-update-slice_fusion.5.first), channel_id=1, source_target_pairs={{0,2},{1,3},{2,0},{3,1},{4,6},{5,7},{6,4},{7,5},{8,10},{9,11},{10,... | collective-permute-start | bytes 122888 | tf_op jit(solution)/shard_map/ppermute | solution.py:861
  41.2 4.1 %collective-permute-start.8 = (f32[4,10,2,128]{3,2,1,0:T(2,128)S(1)}, f32[4,10,2,128]{3,2,1,0:T(2,128)S(1)}, u32[]{:S(2)}, u32[]{:S(2)}) collective-permute-start(f32[4,10,2,128]{3,2,1,0:T(2,128)S(1)} %pad_maximum_fusion.1), channel_id=1, source_target_pairs={{0,2},{1,3},{2,0},{3,1},{4,6},{5,7},{6,4},{7,5},{8,10},{9,11},{10,... | collective-permute-start | bytes 122888 | tf_op jit(solution)/shard_map/ppermute | solution.py:861
  46.0 1.7 %collective-permute-start.10 = (f32[4,2,2,128]{3,2,1,0:T(2,128)S(1)}, f32[4,2,2,128]{3,2,1,0:T(2,128)S(1)}, u32[]{:S(2)}, u32[]{:S(2)}) collective-permute-start(f32[4,2,2,128]{3,2,1,0:T(2,128)S(1)} %bitcast.63), channel_id=1, source_target_pairs={{0,1},{1,0},{2,3},{3,2},{4,5},{5,4},{6,7},{7,6},{8,9},{9,8},{10,11... | collective-permute-start | bytes 24584 | tf_op jit(solution)/shard_map/ppermute | solution.py:861
  47.8 5.9 %collective-permute-start.13 = (f32[4,10,2,128]{3,2,1,0:T(2,128)S(1)}, f32[4,10,2,128]{3,2,1,0:T(2,128)S(1)}, u32[]{:S(2)}, u32[]{:S(2)}) collective-permute-start(f32[4,10,2,128]{3,2,1,0:T(2,128)S(1)} %constant_dynamic-update-slice_fusion.10.second), channel_id=1, source_target_pairs={{0,2},{1,3},{2,0},{3,1},{4,6},{5,7},{6,4},{7,5},{8,10},{9,11},{10,... | collective-permute-start | bytes 122888 | tf_op jit(solution)/shard_map/ppermute | solution.py:861
  49.4 4.3 %collective-permute-start.12 = (f32[2,10,2,128]{3,2,1,0:T(2,128)S(1)}, f32[2,10,2,128]{3,2,1,0:T(2,128)S(1)}, u32[]{:S(2)}, u32[]{:S(2)}) collective-permute-start(f32[2,10,2,128]{3,2,1,0:T(2,128)S(1)} %slice.89), channel_id=1, source_target_pairs={{0,12},{1,13},{2,14},{3,15},{4,0},{5,1},{6,2},{7,3},{8,4},{9,5},{1... | collective-permute-start | bytes 61448 | tf_op jit(solution)/shard_map/ppermute | solution.py:867
  50.3 4.7 %collective-permute-start.11 = (f32[2,10,2,128]{3,2,1,0:T(2,128)S(1)}, f32[2,10,2,128]{3,2,1,0:T(2,128)S(1)}, u32[]{:S(2)}, u32[]{:S(2)}) collective-permute-start(f32[2,10,2,128]{3,2,1,0:T(2,128)S(1)} %slice.89), channel_id=1, source_target_pairs={{0,14},{1,15},{2,12},{3,13},{4,2},{5,3},{6,0},{7,1},{8,6},{9,7},{1... | collective-permute-start | bytes 61448 | tf_op jit(solution)/shard_map/ppermute | solution.py:867
  55.0 10.1 %copy-start = (s32[32,128]{1,0:T(8,128)S(1)}, s32[32,128]{1,0:T(8,128)}, u32[]{:S(2)}) copy-start(s32[32,128]{1,0:T(8,128)} %atoms) | copy-start | bytes 49156
  55.0 10.1 %copy-start.1 = (s32[32]{0:T(128)S(1)}, s32[32]{0:T(128)}, u32[]{:S(2)}) copy-start(s32[32]{0:T(128)} %counts) | copy-start | bytes 388
  56.0 1.1 %collective-permute-start.14 = (f32[1,128]{1,0:T(1,128)S(1)}, f32[1,128]{1,0:T(1,128)S(1)}, u32[]{:S(2)}, u32[]{:S(2)}) collective-permute-start(f32[1,128]{1,0:T(1,128)S(1)} %shard_map.76), channel_id=1, source_target_pairs={{0,1},{1,0},{2,3},{3,2},{4,5},{5,4},{6,7},{7,6},{8,9},{9,8},{10,11... | collective-permute-start | bytes 1544 | tf_op jit(solution)/shard_map/ppermute | solution.py:861
  57.1 4.4 %collective-permute-start.17 = (f32[1,128]{1,0:T(1,128)S(1)}, f32[1,128]{1,0:T(1,128)S(1)}, u32[]{:S(2)}, u32[]{:S(2)}) collective-permute-start(f32[1,128]{1,0:T(1,128)S(1)} %add.24), channel_id=1, source_target_pairs={{0,6},{1,7},{2,4},{3,5},{4,2},{5,3},{6,0},{7,1},{8,14},{9,15},{10,... | collective-permute-start | bytes 1544 | tf_op jit(solution)/shard_map/ppermute | solution.py:861
  59.0 3.5 %collective-permute-start.16 = (f32[1,128]{1,0:T(1,128)S(1)}, f32[1,128]{1,0:T(1,128)S(1)}, u32[]{:S(2)}, u32[]{:S(2)}) collective-permute-start(f32[1,128]{1,0:T(1,128)S(1)} %add.24), channel_id=1, source_target_pairs={{0,4},{1,5},{2,6},{3,7},{4,0},{5,1},{6,2},{7,3},{8,12},{9,13},{10,... | collective-permute-start | bytes 1544 | tf_op jit(solution)/shard_map/ppermute | solution.py:861
  59.7 3.5 %collective-permute-start.15 = (f32[1,128]{1,0:T(1,128)S(1)}, f32[1,128]{1,0:T(1,128)S(1)}, u32[]{:S(2)}, u32[]{:S(2)}) collective-permute-start(f32[1,128]{1,0:T(1,128)S(1)} %add.24), channel_id=1, source_target_pairs={{0,2},{1,3},{2,0},{3,1},{4,6},{5,7},{6,4},{7,5},{8,10},{9,11},{10,... | collective-permute-start | bytes 1544 | tf_op jit(solution)/shard_map/ppermute | solution.py:861
  63.3 4.4 %collective-permute-start.18 = (f32[1,128]{1,0:T(1,128)S(1)}, f32[1,128]{1,0:T(1,128)S(1)}, u32[]{:S(2)}, u32[]{:S(2)}) collective-permute-start(f32[1,128]{1,0:T(1,128)S(1)} %add_add_fusion), channel_id=1, source_target_pairs={{0,8},{1,9},{2,10},{3,11},{4,12},{5,13},{6,14},{7,15},{8,0},{9,1},... | collective-permute-start | bytes 1544 | tf_op jit(solution)/shard_map/ppermute | solution.py:861

commit v4 on v3

--- a/solution.py
+++ b/solution.py
@@ -904,7 +904,7 @@
     if faces_last:
         second, first, beyond, sums = lax.optimization_barrier((second, first, beyond, sums))
     else:
-        second, first, sums = lax.optimization_barrier((second, first, sums))
+        first, second, sums = lax.optimization_barrier((first, second, sums))
     low, high = sorted_faces(first, second)
     corners = partner(jnp.concatenate([low, high], axis=0), "gx", 2)
     pieces = [flat(part) for part in (low, high, beyond)]

time: 69 us -> 69.3 us (level)
  starting transfers between devices: 21.9 us -> 22.9 us
  waiting for transfers between devices: 6.51 us -> 5.69 us
    ppermute x2, starting transfers between devices: 1.96 us -> 3.53 us  [shifted(): return lax.ppermute(block, 'gx', route)]
    ppermute x2, starting transfers between devices: 2.38 us -> 1.64 us  [x_faces(): lax.ppermute(jnp.where(odd, core[:2], core[2:]), 'gx', [(i, i ^ 4) for i...]
  transfers between devices with their start and end apart: 19 -> 19, of which waited for: 8 -> 8; matrix products, arithmetic and copies ran while one was open for 0% -> 0% of each run, Pallas kernels for 51% -> 50%
where the time goes in v4:
time: 69.3 us; the launch traced here: 69.1 us
  Pallas kernels  39.9 us (58%)
  starting transfers between devices  22.9 us (33%)
  waiting for transfers between devices  5.69 us (8%)
    pallas_call x12, Pallas kernels, call(): pl.pallas_call(kernel, out_shape=outs, in_specs=[IN_SMEM if array.ndim ==...  37 us
    ppermute x13, starting transfers between devices, partner(): lax.ppermute(block, axis, [(low, low ^ mask) for low in range(count)])  13.9 us
    ppermute x13, waiting for transfers between devices, partner(): lax.ppermute(block, axis, [(low, low ^ mask) for low in range(count)])  4.74 us
    ppermute x2, starting transfers between devices, x_faces(): second = lax.ppermute(jnp.where(odd, core[2:], core[:2]), 'gx', route)  3.87 us
    ppermute x2, starting transfers between devices, shifted(): return lax.ppermute(block, 'gx', route)  3.53 us
    ppermute x2, starting transfers between devices, x_faces(): lax.ppermute(jnp.where(odd, core[:2], core[2:]), 'gx', [(i, i ^ 4) for i...  1.64 us
  transfers between devices with their start and end apart: 19, of which 8 were waited for; matrix products, arithmetic and copies ran while one was open for 0% of the time, Pallas kernels for 50%

profile of v4, /device:TPU:0, one launch (start us, length us, event | category | flops | bytes accessed | tf_op | source)
XLA Modules:
  0.0 69.1 jit_solution(9885748902070706334)
XLA Ops:
  0.0 1.1 %shard_map.64 = (f32[8,8,128]{2,1,0:T(8,128)S(1)}, s32[32,128]{1,0:T(8,128)S(1)}, s32[32,128]{1,0:T(8,128)S(1)}, f32[20,8,128]{2,1,0:T(8,128)S(1)}, f32[20,8,128]{2,1,0:T(8,128)S(1)}) custom-call(s32[32]{0:T(128)} %counts, f32[3,2560]{1,0:T(4,128)} %offsets.1, f32[20,128]{1,0:T(8,128)} %bitcast.66, f32[20,128]{1,0:T(8,128)} %bitcast.67, f32[20,128]{1,0:T(8,128)} %bitcast.68, ...), custom_call_target="tpu_custom_call" | custom-call | tf_op jit(solution)/shard_map/pallas_call | solution.py:153
  1.1 0.5 collective-permute-start
  1.6 0.7 %shard_map.65 = f32[24,8,128]{2,1,0:T(8,128)S(1)} custom-call(s32[32,128]{1,0:T(8,128)S(1)} %get-tuple-element.47.counted, s32[32,128]{1,0:T(8,128)S(1)} %get-tuple-element.48.atoms, f32[20,8,128]{2,1,0:T(8,128)S(1)} %get-tuple-element.49.table, f32[20,8,128]{2,1,0:T(8,128)S(1)} %get-tuple-element.50.others), custom_call_target="tpu_custom_call" | custom-call | flops 1048576 | bytes 4194304 | tf_op jit(solution)/shard_map/pallas_call | solution.py:186
  2.4 0.1 collective-permute-done
  2.5 2.9 %collective-permute-start.3 = (f32[4,10,8,128]{3,2,1,0:T(8,128)S(1)}, f32[4,10,8,128]{3,2,1,0:T(8,128)S(1)}, u32[]{:S(2)}, u32[]{:S(2)}) collective-permute-start(f32[4,10,8,128]{3,2,1,0:T(8,128)S(1)} %constant_dynamic-update-slice_fusion.slots), channel_id=1, source_target_pairs={{0,2},{1,3},{2,0},{3,1},{4,6},{5,7},{6,4},{7,5},{8,10},{9,11},{10,... | collective-permute-start | bytes 491528 | tf_op jit(solution)/shard_map/ppermute | solution.py:861
  5.5 1.6 %collective-permute-start.2 = (f32[2,10,8,128]{3,2,1,0:T(8,128)S(1)}, f32[2,10,8,128]{3,2,1,0:T(8,128)S(1)}, u32[]{:S(2)}, u32[]{:S(2)}) collective-permute-start(f32[2,10,8,128]{3,2,1,0:T(8,128)S(1)} %get-tuple-element.89), channel_id=1, source_target_pairs={{0,4},{1,5},{2,6},{3,7},{4,0},{5,1},{6,2},{7,3},{8,12},{9,13},{10,... | collective-permute-start | bytes 245768 | tf_op jit(solution)/shard_map/ppermute | solution.py:888
  7.1 2.5 %collective-permute-start.1 = (f32[2,10,8,128]{3,2,1,0:T(8,128)S(1)}, f32[2,10,8,128]{3,2,1,0:T(8,128)S(1)}, u32[]{:S(2)}, u32[]{:S(2)}) collective-permute-start(f32[2,10,8,128]{3,2,1,0:T(8,128)S(1)} %get-tuple-element.90), channel_id=1, source_target_pairs={{0,12},{1,13},{2,14},{3,15},{4,8},{5,9},{6,10},{7,11},{8,4},{9,5},... | collective-permute-start | bytes 245768 | tf_op jit(solution)/shard_map/ppermute | solution.py:887
  9.6 10.3 %shard_map.66 = (f32[32,11,8,8,128]{4,3,2,1,0:T(8,128)S(1)}, f32[32,11,2,8,128]{4,3,2,1,0:T(8,128)S(1)}, f32[8,8,128]{2,1,0:T(8,128)S(1)}, f32[32,11,4,8,128]{4,3,2,1,0:T(8,128)S(1)}) custom-call(f32[40,8,128]{2,1,0:T(8,128)S(1)} %bitcast.24), custom_call_target="tpu_custom_call" | custom-call | flops 86507520 | bytes 23068672 | tf_op jit(solution)/shard_map/pallas_call | solution.py:481
  19.9 0.0 collective-permute-done.2
  19.9 0.0 collective-permute-done.1
  19.9 0.0 collective-permute-done.3
  20.0 0.6 collective-permute-start.4
  20.6 9.7 %shard_map.67 = (f32[32,11,8,8,128]{4,3,2,1,0:T(8,128)S(1)}, f32[32,11,2,8,128]{4,3,2,1,0:T(8,128)S(1)}, f32[32,8,128]{2,1,0:T(8,128)S(1)}) custom-call(f32[20,8,128]{2,1,0:T(8,128)S(1)} %bitcast.39, f32[20,8,128]{2,1,0:T(8,128)S(1)} %bitcast.36, f32[40,8,128]{2,1,0:T(8,128)S(1)} %bitcast.42, f32[32,11,4,8,128]{4,3,2,1,0:T(8,128)S(1)} %get-tuple-element.54.turned, ...), custom_call_target="tpu_custom_call" | custom-call | flops 86507520 | bytes 23068672 | tf_op jit(solution)/shard_map/pallas_call | solution.py:481
  30.2 0.0 collective-permute-done.4
  30.2 1.2 %shard_map.68 = (f32[8,11,3,8,128]{4,3,2,1,0:T(8,128)S(1)}, f32[8,2,128]{2,1,0:T(2,128)S(1)}) custom-call(f32[40,8,128]{2,1,0:T(8,128)S(1)} %bitcast.31, f32[32,11,4,8,128]{4,3,2,1,0:T(8,128)S(1)} %get-tuple-element.54.turned, f32[32,11,2,8,128]{4,3,2,1,0:T(8,128)S(1)} %get-tuple-element.58.before, f32[32,8,128]{2,1,0:T(8,128)S(1)} %get-tuple-element.59.spill_before, ...), custom_call_target="tpu_custom_call" | custom-call | flops 32440320 | bytes 8650752 | tf_op jit(solution)/shard_map/pallas_call | solution.py:481
  31.5 0.1 collective-permute-start.5
  31.5 3.2 %shard_map.69 = (f32[24,11,3,8,128]{4,3,2,1,0:T(8,128)S(1)}, f32[24,2,128]{2,1,0:T(2,128)S(1)}) custom-call(f32[40,8,128]{2,1,0:T(8,128)S(1)} %bitcast.32, f32[32,11,4,8,128]{4,3,2,1,0:T(8,128)S(1)} %get-tuple-element.54.turned, f32[32,11,2,8,128]{4,3,2,1,0:T(8,128)S(1)} %get-tuple-element.58.before, f32[32,8,128]{2,1,0:T(8,128)S(1)} %get-tuple-element.59.spill_before, ...), custom_call_target="tpu_custom_call" | custom-call | flops 32440320 | bytes 8650752 | tf_op jit(solution)/shard_map/pallas_call | solution.py:481
  34.8 0.0 collective-permute-done.5
  34.9 1.4 %collective-permute-start.7 = (f32[2,10,2,128]{3,2,1,0:T(2,128)S(1)}, f32[2,10,2,128]{3,2,1,0:T(2,128)S(1)}, u32[]{:S(2)}, u32[]{:S(2)}) collective-permute-start(f32[2,10,2,128]{3,2,1,0:T(2,128)S(1)} %get-tuple-element.93), channel_id=1, source_target_pairs={{0,12},{1,13},{2,14},{3,15},{4,8},{5,9},{6,10},{7,11},{8,4},{9,5},... | collective-permute-start | bytes 61448 | tf_op jit(solution)/shard_map/ppermute | solution.py:887
  36.3 0.0 collective-permute-start.6
  36.3 1.5 %collective-permute-start.9 = (f32[4,10,2,128]{3,2,1,0:T(2,128)S(1)}, f32[4,10,2,128]{3,2,1,0:T(2,128)S(1)}, u32[]{:S(2)}, u32[]{:S(2)}) collective-permute-start(f32[4,10,2,128]{3,2,1,0:T(2,128)S(1)} %constant_dynamic-update-slice_fusion.5.first), channel_id=1, source_target_pairs={{0,2},{1,3},{2,0},{3,1},{4,6},{5,7},{6,4},{7,5},{8,10},{9,11},{10,... | collective-permute-start | bytes 122888 | tf_op jit(solution)/shard_map/ppermute | solution.py:861
  37.8 1.8 %shard_map.70 = (f32[32,11,2,8,128]{4,3,2,1,0:T(8,128)S(1)}, f32[8,8,128]{2,1,0:T(8,128)S(1)}) custom-call(f32[40,8,128]{2,1,0:T(8,128)S(1)} %bitcast.27, f32[40,2,128]{2,1,0:T(2,128)S(1)} %bitcast.41, f32[32,11,8,8,128]{4,3,2,1,0:T(8,128)S(1)} %get-tuple-element.62.stored), custom_call_target="tpu_custom_call" | custom-call | flops 21626880 | bytes 5767168 | tf_op jit(solution)/shard_map/pallas_call | solution.py:481
  39.6 0.9 %collective-permute-done.7 = f32[2,10,2,128]{3,2,1,0:T(2,128)S(1)} collective-permute-done((f32[2,10,2,128]{3,2,1,0:T(2,128)S(1)}, f32[2,10,2,128]{3,2,1,0:T(2,128)S(1)}, u32[]{:S(2)}, u32[]{:S(2)}) %collective-permute-start.7) | collective-permute-done | bytes 20512 | tf_op jit(solution)/shard_map/ppermute | solution.py:887
  40.5 0.0 collective-permute-done.6
  40.6 1.6 %collective-permute-start.8 = (f32[4,10,2,128]{3,2,1,0:T(2,128)S(1)}, f32[4,10,2,128]{3,2,1,0:T(2,128)S(1)}, u32[]{:S(2)}, u32[]{:S(2)}) collective-permute-start(f32[4,10,2,128]{3,2,1,0:T(2,128)S(1)} %pad_maximum_fusion.1), channel_id=1, source_target_pairs={{0,2},{1,3},{2,0},{3,1},{4,6},{5,7},{6,4},{7,5},{8,10},{9,11},{10,... | collective-permute-start | bytes 122888 | tf_op jit(solution)/shard_map/ppermute | solution.py:861
  42.2 0.0 collective-permute-done.9
  42.2 2.2 %shard_map.71 = (f32[32,11,2,8,128]{4,3,2,1,0:T(8,128)S(1)}, f32[32,8,128]{2,1,0:T(8,128)S(1)}) custom-call(f32[20,8,128]{2,1,0:T(8,128)S(1)} %bitcast.40, f32[20,8,128]{2,1,0:T(8,128)S(1)} %bitcast.37, f32[40,8,128]{2,1,0:T(8,128)S(1)} %bitcast.43, f32[20,2,128]{2,1,0:T(2,128)S(1)} %bitcast.47, f32[20,2,128]{2,1,0:T(2,128)S(1)} %bitcast.48, ...), custom_call_target="tpu_custom_call" | custom-call | flops 21626880 | bytes 5767168 | tf_op jit(solution)/shard_map/pallas_call | solution.py:481
  44.4 0.3 collective-permute-done.8
  44.6 0.7 shard_map.72
  45.3 0.1 collective-permute-start.10
  45.4 1.6 %shard_map.73 = f32[24,2,128]{2,1,0:T(2,128)S(1)} custom-call(f32[40,8,128]{2,1,0:T(8,128)S(1)} %bitcast.34, f32[40,2,128]{2,1,0:T(2,128)S(1)} %bitcast.52, f32[24,11,3,8,128]{4,3,2,1,0:T(8,128)S(1)} %get-tuple-element.72.stored.inner, f32[32,11,2,8,128]{4,3,2,1,0:T(8,128)S(1)} %get-tuple-element.70.before, ...), custom_call_target="tpu_custom_call" | custom-call | flops 21626880 | bytes 5767168 | tf_op jit(solution)/shard_map/pallas_call | solution.py:481
  47.0 0.0 collective-permute-done.10
  47.1 1.6 %collective-permute-start.13 = (f32[4,10,2,128]{3,2,1,0:T(2,128)S(1)}, f32[4,10,2,128]{3,2,1,0:T(2,128)S(1)}, u32[]{:S(2)}, u32[]{:S(2)}) collective-permute-start(f32[4,10,2,128]{3,2,1,0:T(2,128)S(1)} %constant_dynamic-update-slice_fusion.10.second), channel_id=1, source_target_pairs={{0,2},{1,3},{2,0},{3,1},{4,6},{5,7},{6,4},{7,5},{8,10},{9,11},{10,... | collective-permute-start | bytes 122888 | tf_op jit(solution)/shard_map/ppermute | solution.py:861
  48.7 2.0 %collective-permute-start.12 = (f32[2,10,2,128]{3,2,1,0:T(2,128)S(1)}, f32[2,10,2,128]{3,2,1,0:T(2,128)S(1)}, u32[]{:S(2)}, u32[]{:S(2)}) collective-permute-start(f32[2,10,2,128]{3,2,1,0:T(2,128)S(1)} %slice.89), channel_id=1, source_target_pairs={{0,12},{1,13},{2,14},{3,15},{4,0},{5,1},{6,2},{7,3},{8,4},{9,5},{1... | collective-permute-start | bytes 61448 | tf_op jit(solution)/shard_map/ppermute | solution.py:867
  50.7 1.5 %collective-permute-start.11 = (f32[2,10,2,128]{3,2,1,0:T(2,128)S(1)}, f32[2,10,2,128]{3,2,1,0:T(2,128)S(1)}, u32[]{:S(2)}, u32[]{:S(2)}) collective-permute-start(f32[2,10,2,128]{3,2,1,0:T(2,128)S(1)} %slice.89), channel_id=1, source_target_pairs={{0,14},{1,15},{2,12},{3,13},{4,2},{5,3},{6,0},{7,1},{8,6},{9,7},{1... | collective-permute-start | bytes 61448 | tf_op jit(solution)/shard_map/ppermute | solution.py:867
  52.2 2.4 %shard_map.74 = (f32[32,11,2,8,128]{4,3,2,1,0:T(8,128)S(1)}, f32[8,8,128]{2,1,0:T(8,128)S(1)}, f32[32,11,2,8,128]{4,3,2,1,0:T(8,128)S(1)}, f32[2,128]{1,0:T(2,128)S(1)}) custom-call(f32[40,8,128]{2,1,0:T(8,128)S(1)} %bitcast.30, f32[40,2,128]{2,1,0:T(2,128)S(1)} %bitcast.45, f32[32,11,8,8,128]{4,3,2,1,0:T(8,128)S(1)} %get-tuple-element.62.stored, ...), custom_call_target="tpu_custom_call" | custom-call | flops 21626880 | bytes 5767168 | tf_op jit(solution)/shard_map/pallas_call | solution.py:481
  54.6 0.0 collective-permute-done.12
  54.6 0.0 collective-permute-done.13
  54.6 1.2 %shard_map.75 = (f32[32,11,2,8,128]{4,3,2,1,0:T(8,128)S(1)}, f32[32,8,128]{2,1,0:T(8,128)S(1)}) custom-call(f32[20,8,128]{2,1,0:T(8,128)S(1)} %bitcast.38, f32[40,8,128]{2,1,0:T(8,128)S(1)} %bitcast.44, f32[20,2,128]{2,1,0:T(2,128)S(1)} %bitcast.59, f32[40,2,128]{2,1,0:T(2,128)S(1)} %bitcast.53, f32[32,11,8,8,128]{4,3,2,1,0:T(8,128)S(1)} %get-tuple-element.67.refs_6_.stored, ...), custom_call_target="tpu_custom_call" | custom-call | flops 21626880 | bytes 5767168 | tf_op jit(solution)/shard_map/pallas_call | solution.py:481
  55.8 0.0 collective-permute-done.11
  55.8 0.0 copy-start
  55.9 0.0 copy-start.1
  55.9 1.0 %shard_map.76 = f32[1,128]{1,0:T(1,128)S(1)} custom-call(f32[40,8,128]{2,1,0:T(8,128)S(1)} %bitcast.35, f32[20,2,128]{2,1,0:T(2,128)S(1)} %bitcast.58, f32[8,11,3,8,128]{4,3,2,1,0:T(8,128)S(1)} %get-tuple-element.66.stored.edge, f32[24,11,3,8,128]{4,3,2,1,0:T(8,128)S(1)} %get-tuple-element.72.stored.inner, ...), custom_call_target="tpu_custom_call" | custom-call | flops 21626880 | bytes 5767168 | tf_op jit(solution)/shard_map/pallas_call | solution.py:481
  56.9 0.0 collective-permute-start.14
  56.9 1.1 %collective-permute-done.14 = f32[1,128]{1,0:T(1,128)S(1)} collective-permute-done((f32[1,128]{1,0:T(1,128)S(1)}, f32[1,128]{1,0:T(1,128)S(1)}, u32[]{:S(2)}, u32[]{:S(2)}) %collective-permute-start.14) | collective-permute-done | bytes 544 | tf_op jit(solution)/shard_map/ppermute | solution.py:861
  58.0 1.4 %collective-permute-start.17 = (f32[1,128]{1,0:T(1,128)S(1)}, f32[1,128]{1,0:T(1,128)S(1)}, u32[]{:S(2)}, u32[]{:S(2)}) collective-permute-start(f32[1,128]{1,0:T(1,128)S(1)} %add.24), channel_id=1, source_target_pairs={{0,6},{1,7},{2,4},{3,5},{4,2},{5,3},{6,0},{7,1},{8,14},{9,15},{10,... | collective-permute-start | bytes 1544 | tf_op jit(solution)/shard_map/ppermute | solution.py:861
  59.4 0.5 collective-permute-start.16
  60.0 1.5 %collective-permute-start.15 = (f32[1,128]{1,0:T(1,128)S(1)}, f32[1,128]{1,0:T(1,128)S(1)}, u32[]{:S(2)}, u32[]{:S(2)}) collective-permute-start(f32[1,128]{1,0:T(1,128)S(1)} %add.24), channel_id=1, source_target_pairs={{0,2},{1,3},{2,0},{3,1},{4,6},{5,7},{6,4},{7,5},{8,10},{9,11},{10,... | collective-permute-start | bytes 1544 | tf_op jit(solution)/shard_map/ppermute | solution.py:861
  61.5 0.9 %collective-permute-done.17 = f32[1,128]{1,0:T(1,128)S(1)} collective-permute-done((f32[1,128]{1,0:T(1,128)S(1)}, f32[1,128]{1,0:T(1,128)S(1)}, u32[]{:S(2)}, u32[]{:S(2)}) %collective-permute-start.17) | collective-permute-done | bytes 544 | tf_op jit(solution)/shard_map/ppermute | solution.py:861
  62.4 0.5 collective-permute-done.16
  63.0 0.5 collective-permute-done.15
  63.5 1.5 %collective-permute-start.18 = (f32[1,128]{1,0:T(1,128)S(1)}, f32[1,128]{1,0:T(1,128)S(1)}, u32[]{:S(2)}, u32[]{:S(2)}) collective-permute-start(f32[1,128]{1,0:T(1,128)S(1)} %add_add_fusion), channel_id=1, source_target_pairs={{0,8},{1,9},{2,10},{3,11},{4,12},{5,13},{6,14},{7,15},{8,0},{9,1},... | collective-permute-start | bytes 1544 | tf_op jit(solution)/shard_map/ppermute | solution.py:861
  65.0 0.0 copy-done
  65.0 0.0 copy-done.1
  65.0 1.7 %shard_map.77.places = s32[2,32,128]{2,1,0:T(8,128)S(1)} custom-call(s32[32]{0:T(128)S(1)} %copy-done.1, s32[32,128]{1,0:T(8,128)S(1)} %copy-done), custom_call_target="tpu_custom_call" | custom-call | flops 21626880 | bytes 5767168 | tf_op jit(solution)/shard_map/pallas_call | solution.py:481
  66.8 1.2 %collective-permute-done.18 = f32[1,128]{1,0:T(1,128)S(1)} collective-permute-done((f32[1,128]{1,0:T(1,128)S(1)}, f32[1,128]{1,0:T(1,128)S(1)}, u32[]{:S(2)}, u32[]{:S(2)}) %collective-permute-start.18) | collective-permute-done | bytes 544 | tf_op jit(solution)/shard_map/ppermute | solution.py:861
  68.0 1.1 %shard_map.78 = f32[20,128]{1,0:T(8,128)} custom-call(f32[1,128]{1,0:T(1,128)S(1)} %add.28.moments, f32[4,10,8,128]{3,2,1,0:T(8,128)S(1)} %constant_dynamic-update-slice_fusion.slots, f32[4,10,2,128]{3,2,1,0:T(2,128)S(1)} %constant_dynamic-update-slice_fusion.5.first, f32[4,10,2,128]{3,2,1,0:T(2,128)S(1)} %constant_dynamic-update-slice_fusion.10.second, ...), custom_call_target="tpu_custom_call" | custom-call | tf_op jit(solution)/shard_map/pallas_call | solution.py:849
  (25 shorter events, 0.2 us)
Async XLA Ops:
  1.1 1.4 %collective-permute-start = (f32[4,2,8,128]{3,2,1,0:T(8,128)S(1)}, f32[4,2,8,128]{3,2,1,0:T(8,128)S(1)}, u32[]{:S(2)}, u32[]{:S(2)}) collective-permute-start(f32[4,2,8,128]{3,2,1,0:T(8,128)S(1)} %bitcast.54), channel_id=1, source_target_pairs={{0,1},{1,0},{2,3},{3,2},{4,5},{5,4},{6,7},{7,6},{8,9},{9,8},{10,11... | collective-permute-start | bytes 98312 | tf_op jit(solution)/shard_map/ppermute | solution.py:861
  2.5 17.4 %collective-permute-start.3 = (f32[4,10,8,128]{3,2,1,0:T(8,128)S(1)}, f32[4,10,8,128]{3,2,1,0:T(8,128)S(1)}, u32[]{:S(2)}, u32[]{:S(2)}) collective-permute-start(f32[4,10,8,128]{3,2,1,0:T(8,128)S(1)} %constant_dynamic-update-slice_fusion.slots), channel_id=1, source_target_pairs={{0,2},{1,3},{2,0},{3,1},{4,6},{5,7},{6,4},{7,5},{8,10},{9,11},{10,... | collective-permute-start | bytes 491528 | tf_op jit(solution)/shard_map/ppermute | solution.py:861
  5.5 14.4 %collective-permute-start.2 = (f32[2,10,8,128]{3,2,1,0:T(8,128)S(1)}, f32[2,10,8,128]{3,2,1,0:T(8,128)S(1)}, u32[]{:S(2)}, u32[]{:S(2)}) collective-permute-start(f32[2,10,8,128]{3,2,1,0:T(8,128)S(1)} %get-tuple-element.89), channel_id=1, source_target_pairs={{0,4},{1,5},{2,6},{3,7},{4,0},{5,1},{6,2},{7,3},{8,12},{9,13},{10,... | collective-permute-start | bytes 245768 | tf_op jit(solution)/shard_map/ppermute | solution.py:888
  7.1 12.8 %collective-permute-start.1 = (f32[2,10,8,128]{3,2,1,0:T(8,128)S(1)}, f32[2,10,8,128]{3,2,1,0:T(8,128)S(1)}, u32[]{:S(2)}, u32[]{:S(2)}) collective-permute-start(f32[2,10,8,128]{3,2,1,0:T(8,128)S(1)} %get-tuple-element.90), channel_id=1, source_target_pairs={{0,12},{1,13},{2,14},{3,15},{4,8},{5,9},{6,10},{7,11},{8,4},{9,5},... | collective-permute-start | bytes 245768 | tf_op jit(solution)/shard_map/ppermute | solution.py:887
  20.0 10.2 %collective-permute-start.4 = (f32[4,10,8,128]{3,2,1,0:T(8,128)S(1)}, f32[4,10,8,128]{3,2,1,0:T(8,128)S(1)}, u32[]{:S(2)}, u32[]{:S(2)}) collective-permute-start(f32[4,10,8,128]{3,2,1,0:T(8,128)S(1)} %pad_maximum_fusion), channel_id=1, source_target_pairs={{0,2},{1,3},{2,0},{3,1},{4,6},{5,7},{6,4},{7,5},{8,10},{9,11},{10,... | collective-permute-start | bytes 491528 | tf_op jit(solution)/shard_map/ppermute | solution.py:861
  31.5 3.3 %collective-permute-start.5 = (f32[4,2,2,128]{3,2,1,0:T(2,128)S(1)}, f32[4,2,2,128]{3,2,1,0:T(2,128)S(1)}, u32[]{:S(2)}, u32[]{:S(2)}) collective-permute-start(f32[4,2,2,128]{3,2,1,0:T(2,128)S(1)} %bitcast.60), channel_id=1, source_target_pairs={{0,1},{1,0},{2,3},{3,2},{4,5},{5,4},{6,7},{7,6},{8,9},{9,8},{10,11... | collective-permute-start | bytes 24584 | tf_op jit(solution)/shard_map/ppermute | solution.py:861
  34.9 5.6 %collective-permute-start.7 = (f32[2,10,2,128]{3,2,1,0:T(2,128)S(1)}, f32[2,10,2,128]{3,2,1,0:T(2,128)S(1)}, u32[]{:S(2)}, u32[]{:S(2)}) collective-permute-start(f32[2,10,2,128]{3,2,1,0:T(2,128)S(1)} %get-tuple-element.93), channel_id=1, source_target_pairs={{0,12},{1,13},{2,14},{3,15},{4,8},{5,9},{6,10},{7,11},{8,4},{9,5},... | collective-permute-start | bytes 61448 | tf_op jit(solution)/shard_map/ppermute | solution.py:887
  36.3 4.3 %collective-permute-start.6 = (f32[2,10,2,128]{3,2,1,0:T(2,128)S(1)}, f32[2,10,2,128]{3,2,1,0:T(2,128)S(1)}, u32[]{:S(2)}, u32[]{:S(2)}) collective-permute-start(f32[2,10,2,128]{3,2,1,0:T(2,128)S(1)} %get-tuple-element.94), channel_id=1, source_target_pairs={{0,4},{1,5},{2,6},{3,7},{4,0},{5,1},{6,2},{7,3},{8,12},{9,13},{10,... | collective-permute-start | bytes 61448 | tf_op jit(solution)/shard_map/ppermute | solution.py:888
  36.3 5.9 %collective-permute-start.9 = (f32[4,10,2,128]{3,2,1,0:T(2,128)S(1)}, f32[4,10,2,128]{3,2,1,0:T(2,128)S(1)}, u32[]{:S(2)}, u32[]{:S(2)}) collective-permute-start(f32[4,10,2,128]{3,2,1,0:T(2,128)S(1)} %constant_dynamic-update-slice_fusion.5.first), channel_id=1, source_target_pairs={{0,2},{1,3},{2,0},{3,1},{4,6},{5,7},{6,4},{7,5},{8,10},{9,11},{10,... | collective-permute-start | bytes 122888 | tf_op jit(solution)/shard_map/ppermute | solution.py:861
  40.6 4.1 %collective-permute-start.8 = (f32[4,10,2,128]{3,2,1,0:T(2,128)S(1)}, f32[4,10,2,128]{3,2,1,0:T(2,128)S(1)}, u32[]{:S(2)}, u32[]{:S(2)}) collective-permute-start(f32[4,10,2,128]{3,2,1,0:T(2,128)S(1)} %pad_maximum_fusion.1), channel_id=1, source_target_pairs={{0,2},{1,3},{2,0},{3,1},{4,6},{5,7},{6,4},{7,5},{8,10},{9,11},{10,... | collective-permute-start | bytes 122888 | tf_op jit(solution)/shard_map/ppermute | solution.py:861
  45.3 1.7 %collective-permute-start.10 = (f32[4,2,2,128]{3,2,1,0:T(2,128)S(1)}, f32[4,2,2,128]{3,2,1,0:T(2,128)S(1)}, u32[]{:S(2)}, u32[]{:S(2)}) collective-permute-start(f32[4,2,2,128]{3,2,1,0:T(2,128)S(1)} %bitcast.63), channel_id=1, source_target_pairs={{0,1},{1,0},{2,3},{3,2},{4,5},{5,4},{6,7},{7,6},{8,9},{9,8},{10,11... | collective-permute-start | bytes 24584 | tf_op jit(solution)/shard_map/ppermute | solution.py:861
  47.1 7.5 %collective-permute-start.13 = (f32[4,10,2,128]{3,2,1,0:T(2,128)S(1)}, f32[4,10,2,128]{3,2,1,0:T(2,128)S(1)}, u32[]{:S(2)}, u32[]{:S(2)}) collective-permute-start(f32[4,10,2,128]{3,2,1,0:T(2,128)S(1)} %constant_dynamic-update-slice_fusion.10.second), channel_id=1, source_target_pairs={{0,2},{1,3},{2,0},{3,1},{4,6},{5,7},{6,4},{7,5},{8,10},{9,11},{10,... | collective-permute-start | bytes 122888 | tf_op jit(solution)/shard_map/ppermute | solution.py:861
  48.7 5.9 %collective-permute-start.12 = (f32[2,10,2,128]{3,2,1,0:T(2,128)S(1)}, f32[2,10,2,128]{3,2,1,0:T(2,128)S(1)}, u32[]{:S(2)}, u32[]{:S(2)}) collective-permute-start(f32[2,10,2,128]{3,2,1,0:T(2,128)S(1)} %slice.89), channel_id=1, source_target_pairs={{0,12},{1,13},{2,14},{3,15},{4,0},{5,1},{6,2},{7,3},{8,4},{9,5},{1... | collective-permute-start | bytes 61448 | tf_op jit(solution)/shard_map/ppermute | solution.py:867
  50.7 5.1 %collective-permute-start.11 = (f32[2,10,2,128]{3,2,1,0:T(2,128)S(1)}, f32[2,10,2,128]{3,2,1,0:T(2,128)S(1)}, u32[]{:S(2)}, u32[]{:S(2)}) collective-permute-start(f32[2,10,2,128]{3,2,1,0:T(2,128)S(1)} %slice.89), channel_id=1, source_target_pairs={{0,14},{1,15},{2,12},{3,13},{4,2},{5,3},{6,0},{7,1},{8,6},{9,7},{1... | collective-permute-start | bytes 61448 | tf_op jit(solution)/shard_map/ppermute | solution.py:867
  55.8 9.2 %copy-start = (s32[32,128]{1,0:T(8,128)S(1)}, s32[32,128]{1,0:T(8,128)}, u32[]{:S(2)}) copy-start(s32[32,128]{1,0:T(8,128)} %atoms) | copy-start | bytes 49156
  55.9 9.2 %copy-start.1 = (s32[32]{0:T(128)S(1)}, s32[32]{0:T(128)}, u32[]{:S(2)}) copy-start(s32[32]{0:T(128)} %counts) | copy-start | bytes 388
  56.9 1.1 %collective-permute-start.14 = (f32[1,128]{1,0:T(1,128)S(1)}, f32[1,128]{1,0:T(1,128)S(1)}, u32[]{:S(2)}, u32[]{:S(2)}) collective-permute-start(f32[1,128]{1,0:T(1,128)S(1)} %shard_map.76), channel_id=1, source_target_pairs={{0,1},{1,0},{2,3},{3,2},{4,5},{5,4},{6,7},{7,6},{8,9},{9,8},{10,11... | collective-permute-start | bytes 1544 | tf_op jit(solution)/shard_map/ppermute | solution.py:861
  58.0 4.4 %collective-permute-start.17 = (f32[1,128]{1,0:T(1,128)S(1)}, f32[1,128]{1,0:T(1,128)S(1)}, u32[]{:S(2)}, u32[]{:S(2)}) collective-permute-start(f32[1,128]{1,0:T(1,128)S(1)} %add.24), channel_id=1, source_target_pairs={{0,6},{1,7},{2,4},{3,5},{4,2},{5,3},{6,0},{7,1},{8,14},{9,15},{10,... | collective-permute-start | bytes 1544 | tf_op jit(solution)/shard_map/ppermute | solution.py:861
  59.4 3.5 %collective-permute-start.16 = (f32[1,128]{1,0:T(1,128)S(1)}, f32[1,128]{1,0:T(1,128)S(1)}, u32[]{:S(2)}, u32[]{:S(2)}) collective-permute-start(f32[1,128]{1,0:T(1,128)S(1)} %add.24), channel_id=1, source_target_pairs={{0,4},{1,5},{2,6},{3,7},{4,0},{5,1},{6,2},{7,3},{8,12},{9,13},{10,... | collective-permute-start | bytes 1544 | tf_op jit(solution)/shard_map/ppermute | solution.py:861
  60.0 3.5 %collective-permute-start.15 = (f32[1,128]{1,0:T(1,128)S(1)}, f32[1,128]{1,0:T(1,128)S(1)}, u32[]{:S(2)}, u32[]{:S(2)}) collective-permute-start(f32[1,128]{1,0:T(1,128)S(1)} %add.24), channel_id=1, source_target_pairs={{0,2},{1,3},{2,0},{3,1},{4,6},{5,7},{6,4},{7,5},{8,10},{9,11},{10,... | collective-permute-start | bytes 1544 | tf_op jit(solution)/shard_map/ppermute | solution.py:861
  63.5 4.4 %collective-permute-start.18 = (f32[1,128]{1,0:T(1,128)S(1)}, f32[1,128]{1,0:T(1,128)S(1)}, u32[]{:S(2)}, u32[]{:S(2)}) collective-permute-start(f32[1,128]{1,0:T(1,128)S(1)} %add_add_fusion), channel_id=1, source_target_pairs={{0,8},{1,9},{2,10},{3,11},{4,12},{5,13},{6,14},{7,15},{8,0},{9,1},... | collective-permute-start | bytes 1544 | tf_op jit(solution)/shard_map/ppermute | solution.py:861
